TPU v7x, 32 devices: a whole 2x2x4 slice. The times are simulated.
32 devices in a mesh: parts: 2 (over y), fsdp: 4 (over z), member: 2 (over x), dp: 2 (over core).
Axes of the slice: x: 2, y: 2, z: 4, core: 2. Of those that a mesh axis runs over, the one named last changes fastest.
Arguments:
- skip_stream: bfloat16 [40, 512, 5120], P(('parts', 'member'), ('fsdp', 'dp')), parts along dimension 0
- projected_output_adjoint: bfloat16 [40, 512, 1024], P(('parts', 'member'), ('fsdp', 'dp')), parts along dimension 0, may hold values from -12 to 12
- frozen_projection_kernel: bfloat16 [5120, 1024], P('fsdp'), may hold values from -0.078125 to 0.078125
- lowering_projections: bfloat16 [5120, 512], P('fsdp', ('parts', 'member')), parts along dimension 1, may hold values from -0.078125 to 0.078125
- lifting_projections: bfloat16 [512, 1024], P(('parts', 'member')), parts along dimension 0, may hold values from -0.75 to 0.75
- normalizer_scales: float32 [5120], replicated, may hold values from 0.1 to 1.9
- tile_assignee: int32 [40], P(('parts', 'member')), parts along dimension 0, may hold values from 0 to 4, as said below
Outputs:
- residual_grad: bfloat16 [40, 512, 5120], P(('parts', 'member'), ('fsdp', 'dp')), parts along dimension 0
- grad_down: float32 [5120, 512], P(('fsdp', 'dp'), ('parts', 'member')), parts along dimension 1
- raising_factor_sensitivity: float32 [512, 1024], P(('parts', 'member'), ('fsdp', 'dp')), parts along dimension 0
There are 2 independent parts, one for each index of `parts`. A program takes and returns all parts, laid end to end along the dimension named above; an argument that names none is the same for every part. Nothing has to cross between parts.
Inputs may be any that keep to these rules, and one draw needn't show every extreme that they name: `tile_assignee`: slots m*10 to (m+1)*10 - 1 hold members m*2 to (m+1)*2 - 1 or padding (4); in each such group the live slots come first, in runs of increasing member, and every member has at least one slot.
All inputs are finite; a program needn't handle non-finite values.
Results may differ from a plain program's by a relative error of at most 0.0051.
Values may be sent and summed in bfloat16 or wider, within the bound.
No kernel may reach another device: no remote copies, remote signals or barrier semaphores. Data moves between devices by JAX's collectives and lax.ppermute only.
A program may use at most 128 MiB of HBM per device.

v0:
```python
import jax
import jax.numpy as jnp
from jax import lax
from jax.sharding import PartitionSpec as P

LOW_DIM = 64
BLOCK = 512


epsilon = 1e-06


def base_grad(grads, weight_rows):
    product = jnp.einsum("srk,nk->srn", grads, weight_rows, preferred_element_type=jnp.float32)
    return product.astype(jnp.bfloat16)


def per_device(
    skip_stream,
    projected_output_adjoint,
    frozen_projection_kernel,
    lowering_projections,
    lifting_projections,
    normalizer_scales,
    tile_assignee,
):
    within_group_indices = lifting_projections.shape[0] // LOW_DIM
    first_member = lax.axis_index("member") * within_group_indices
    member_ids = first_member + jnp.arange(within_group_indices, dtype=jnp.int32)
    onehot = tile_assignee[:, None] == member_ids[None, :]
    live_mask = jnp.any(onehot, axis=1)
    block_count = jnp.sum(onehot.astype(jnp.float32), axis=0)
    filtered_sensitivity_lines = jnp.where(
        live_mask[:, None, None], projected_output_adjoint, jnp.zeros_like(projected_output_adjoint)
    )
    column_mask = jnp.repeat(onehot, LOW_DIM, axis=1)[:, None, :]
    widened = skip_stream.astype(jnp.float32)
    root_mean = jnp.sqrt(jnp.mean(widened * widened, axis=-1, keepdims=True) + epsilon)
    normed = widened / root_mean
    hidden = (normed * normalizer_scales).astype(jnp.bfloat16)
    middle_product = jnp.einsum(
        "qgr,vr->qgv",
        filtered_sensitivity_lines,
        lifting_projections,
        preferred_element_type=jnp.float32,
    )
    middle_product = jnp.where(column_mask, middle_product, 0.0).astype(jnp.bfloat16)
    weight_full, down_full = (
        lax.all_gather(frozen_projection_kernel, "fsdp", axis=0, tiled=True),
        lax.all_gather(lowering_projections, "fsdp", axis=0, tiled=True),
    )
    base_part = base_grad(filtered_sensitivity_lines, weight_full)
    projected = jnp.einsum("srd,dm->srm", hidden, down_full, preferred_element_type=jnp.float32)
    projected = jnp.where(column_mask, projected, 0.0).astype(jnp.bfloat16)
    hidden_grad = base_part.astype(jnp.float32) + jnp.einsum(
        "srm,dm->srd", middle_product, down_full, preferred_element_type=jnp.float32
    )
    scaled = hidden_grad * normalizer_scales
    residual_grad = (
        (scaled - normed * jnp.mean(scaled * normed, axis=-1, keepdims=True)) / root_mean
    ).astype(jnp.bfloat16)
    term_down = jnp.einsum(
        "srd,srm->dm", hidden, middle_product, preferred_element_type=jnp.float32
    )
    term_up = jnp.einsum(
        "srm,srk->mk", projected, filtered_sensitivity_lines, preferred_element_type=jnp.float32
    )
    sum_down, sum_up = (
        lax.psum_scatter(term_down, ("fsdp", "dp"), scatter_dimension=0, tiled=True),
        lax.psum_scatter(term_up, ("fsdp", "dp"), scatter_dimension=1, tiled=True),
    )
    inverse = jnp.repeat(1.0 / (BLOCK * block_count), LOW_DIM)
    return (residual_grad, sum_down * inverse[None, :], sum_up * inverse[:, None])


def solution(mesh):
    placed = (
        P(("parts", "member"), ("fsdp", "dp"), None),
        P(("parts", "member"), ("fsdp", "dp"), None),
        P("fsdp", None),
        P("fsdp", ("parts", "member")),
        P(("parts", "member"), None),
        P(),
        P(("parts", "member")),
    )
    return jax.shard_map(
        per_device,
        mesh=mesh,
        in_specs=placed,
        out_specs=(
            P(("parts", "member"), ("fsdp", "dp"), None),
            P(("fsdp", "dp"), ("parts", "member")),
            P(("parts", "member"), ("fsdp", "dp")),
        ),
        check_vma=False,
    )
```

profile of v0, /device:TPU:0, one launch (start us, length us, event | category | flops | bytes accessed | tf_op | source)
XLA Modules:
  0.0 328.1 jit_solution(16773907247585796190)
XLA Ops:
  7.2 0.0 copy-start
  7.2 0.0 copy-start.3
  7.2 0.0 all-gather.3.cloned.1.call-start
  7.2 0.7 all-gather.3.cloned.1.call-update
  7.9 0.0 all-gather.5.cloned.1.call-start
  8.0 0.7 all-gather.5.cloned.1.call-update
  8.7 0.0 reduce-scatter.5.cloned.1.call-start
  8.7 0.8 broadcast_compare_fusion
  9.6 0.1 broadcast_in_dim.44
  9.7 0.1 broadcast_in_dim.45
  9.7 4.2 %fusion = f32[10,64]{1,0:T(8,128)S(1)} fusion(bf16[10,64,5120]{2,1,0:T(8,128)(2,1)} %param.7), kind=kLoop, calls=%fused_computation.2 | loop fusion | flops 9829760 | bytes 6556160 | tf_op jit(solution)/shard_map/reduce_sum | solution.py:38
  14.0 0.0 copy-done
  14.0 0.0 copy-done.3
  14.0 0.5 fusion.15
  14.5 0.0 copy-start.1
  14.6 181.7 %all-gather.3.cloned.1.call-done = bf16[5120,1024]{1,0:T(8,128)(2,1)} async-done(((bf16[1280,1024]{1,0:T(8,128)(2,1)}), bf16[5120,1024]{1,0:T(8,128)(2,1)}) %all-gather.3.cloned.1.call-update) | async-done | bytes 10485776 | tf_op jit(solution)/shard_map/all_gather | solution.py:49
  196.2 12.9 %fusion.3 = bf16[10,64,5120]{2,1,0:T(8,128)(2,1)} fusion(bf16[5120,1024]{1,0:T(8,128)(2,1)} %all-gather.3.cloned.1.call-done, bf16[10,64,1024]{2,1,0:T(8,128)(2,1)S(1)} %copy-done.3, pred[10]{0:T(512)(128)(4,1)S(1)} %get-tuple-element.6), kind=kOutput, calls=%fused_computation.9 | convolution fusion | flops 6714818560 | bytes 18350090 | tf_op jit(solution)/shard_map/srk,nk->srn/dot_general | solution.py:14
  209.2 19.6 %all-gather.5.cloned.1.call-done = bf16[5120,128]{1,0:T(8,128)(2,1)} async-done(((bf16[1280,128]{1,0:T(8,128)(2,1)}), bf16[5120,128]{1,0:T(8,128)(2,1)}) %all-gather.5.cloned.1.call-update) | async-done | bytes 1310736 | tf_op jit(solution)/shard_map/all_gather | solution.py:50
  228.7 0.0 copy-done.1
  228.7 7.1 %multiply_reduce_fusion = (f32[10,64]{1,0:T(8,128)S(1)}, f32[10,64,5120]{2,1,0:T(8,128)S(1)}) fusion(f32[10,64]{1,0:T(8,128)S(1)} %add_sqrt_fusion, bf16[10,64,5120]{2,1,0:T(8,128)(2,1)} %param.7, f32[5120]{0:T(1024)S(1)} %copy-done.1, bf16[10,64,128]{2,1,0:T(8,128)(2,1)S(1)} %fusion.15, bf16[5120,128]{1,0:T(8,128)(2,1)} %all-gather.5.cloned.1.call-done, ...), kind=kOutput, calls=%fused_computation.5 | convolution fusion | flops 861797760 | bytes 27714560 | tf_op jit(solution)/shard_map/srm,dm->srd/dot_general | solution.py:55
  235.8 0.0 copy-start.4
  235.9 9.6 %multiply_convert_fusion = (bf16[10,64,5120]{2,1,0:T(8,128)(2,1)}, bf16[10,64,5120]{2,1,0:T(8,128)(2,1)}) fusion(f32[5120]{0:T(1024)S(1)} %copy-done.1, f32[10,64]{1,0:T(8,128)S(1)} %add_sqrt_fusion, bf16[10,64,5120]{2,1,0:T(8,128)(2,1)} %param.7, f32[10,64,5120]{2,1,0:T(8,128)S(1)} %get-tuple-element.8, f32[10,64]{1,0:T(8,128)S(1)} %broadcast_multiply_fusion.2), kind=kLoop, calls=%fused_computation.3 | loop fusion | flops 26214400 | bytes 32793600 | tf_op jit(solution)/shard_map/convert_element_type | solution.py:40
  245.5 0.0 copy-done.4
  245.5 6.2 %convolution_bitcast_fusion.1 = f32[128,1024]{1,0:T(8,128)} fusion(bf16[10,64,5120]{2,1,0:T(8,128)(2,1)} %get-tuple-element.3, bf16[5120,128]{1,0:T(8,128)(2,1)S(1)} %copy-done.4, pred[10,128]{1,0:T(8,128)(4,1)S(1)} %broadcast_in_dim.45, bf16[10,64,1024]{2,1,0:T(8,128)(2,1)S(1)} %copy-done.3, pred[10]{0:T(512)(128)(4,1)S(1)} %get-tuple-element.6), kind=kOutput, calls=%fused_computation.15 | convolution fusion | flops 1007452160 | bytes 9700618 | tf_op jit(solution)/shard_map/srm,srk->mk/dot_general | solution.py:65
  251.7 0.0 reduce-scatter.5.cloned.1.call-update
  251.7 0.0 copy-start.2
  251.8 0.0 reduce-scatter.3.cloned.1.call-start
  251.8 6.3 %convolution_bitcast_fusion = f32[5120,128]{1,0:T(8,128)} fusion(bf16[10,64,5120]{2,1,0:T(8,128)(2,1)} %get-tuple-element.3, bf16[10,64,128]{2,1,0:T(8,128)(2,1)S(1)} %fusion.15), kind=kOutput, calls=%fused_computation.10 | convolution fusion | flops 838860800 | bytes 9338880 | tf_op jit(solution)/shard_map/srd,srm->dm/dot_general | solution.py:62
  258.1 0.0 reduce-scatter.3.cloned.1.call-update
  258.2 0.0 copy-done.2
  258.2 0.1 convert_reduce_fusion
  258.3 0.1 broadcast_in_dim.48
  258.3 0.1 mul.61
  258.4 23.4 %reduce-scatter.5.cloned.1.call-done = f32[128,128]{1,0:T(8,128)} async-done(((f32[128,1024]{1,0:T(8,128)}), f32[128,128]{1,0:T(8,128)}) %reduce-scatter.5.cloned.1.call-update) | async-done | bytes 65552 | tf_op jit(solution)/shard_map/reduce_scatter | solution.py:70
  281.8 1.6 broadcast_multiply_fusion.1
  283.4 36.4 %reduce-scatter.3.cloned.1.call-done = f32[640,128]{1,0:T(8,128)} async-done(((f32[5120,128]{1,0:T(8,128)}), f32[640,128]{1,0:T(8,128)}) %reduce-scatter.3.cloned.1.call-update) | async-done | bytes 327696 | tf_op jit(solution)/shard_map/reduce_scatter | solution.py:69
  319.8 1.7 broadcast_multiply_fusion
  (4 shorter events, 0.0 us)
Async XLA Ops:
  7.2 6.8 %copy-start = (bf16[128,1024]{1,0:T(8,128)(2,1)S(1)}, bf16[128,1024]{1,0:T(8,128)(2,1)}, u32[]{:S(2)}) copy-start(bf16[128,1024]{1,0:T(8,128)(2,1)} %param.11) | copy-start | bytes 786436
  7.2 6.8 %copy-start.3 = (bf16[10,64,1024]{2,1,0:T(8,128)(2,1)S(1)}, bf16[10,64,1024]{2,1,0:T(8,128)(2,1)}, u32[]{:S(2)}) copy-start(bf16[10,64,1024]{2,1,0:T(8,128)(2,1)} %param.8) | copy-start | bytes 3932164
  7.2 189.1 %all-gather.3.cloned.1.call-start = ((), (), s32[]{:S(2)}) async-start(), calls=%async_computation.2 | async-start | bytes 13107200 | tf_op jit(solution)/shard_map/all_gather | solution.py:49
  7.9 220.8 %all-gather.5.cloned.1.call-start = ((), (), s32[]{:S(2)}) async-start(), calls=%async_computation.3 | async-start | bytes 1638400 | tf_op jit(solution)/shard_map/all_gather | solution.py:50
  8.7 273.2 %reduce-scatter.5.cloned.1.call-start = ((), (), s32[]{:S(2)}) async-start(), calls=%async_computation.5 | async-start | bytes 589824 | tf_op jit(solution)/shard_map/reduce_scatter | solution.py:70
  14.5 214.2 %copy-start.1 = (f32[5120]{0:T(1024)S(1)}, f32[5120]{0:T(1024)}, u32[]{:S(2)}) copy-start(f32[5120]{0:T(1024)} %param.12) | copy-start | bytes 61444
  235.8 9.6 %copy-start.4 = (bf16[5120,128]{1,0:T(8,128)(2,1)S(1)}, bf16[5120,128]{1,0:T(8,128)(2,1)}, u32[]{:S(2)}) copy-start(bf16[5120,128]{1,0:T(8,128)(2,1)} %all-gather.5.cloned.1.call-done) | copy-start | bytes 3932164
  251.7 6.4 %copy-start.2 = (s32[10]{0:T(128)S(1)}, s32[10]{0:T(128)}, u32[]{:S(2)}) copy-start(s32[10]{0:T(128)} %param.13) | copy-start | bytes 124
  251.8 68.1 %reduce-scatter.3.cloned.1.call-start = ((), (), s32[]{:S(2)}) async-start(), calls=%async_computation.4 | async-start | bytes 2949120 | tf_op jit(solution)/shard_map/reduce_scatter | solution.py:69
Sparse Core Ops, SparseCore 0:
  9.6 186.6 all-gather.2
  197.8 30.8 all-gather.4
  251.9 29.9 reduce-scatter.4
  284.1 35.6 reduce-scatter.2
where the time goes:
time: 328 us
  waiting for transfers between devices  263 us (80%)
  matrix products  33.1 us (10%)
  other arithmetic  18.1 us (6%)
  between operations  13.9 us (4%)
    all_gather x1, waiting for transfers between devices, per_device(): lax.all_gather(frozen_projection_kernel, 'fsdp', axis=0, tiled=True)  182 us
    reduce_scatter x1, waiting for transfers between devices, per_device(): lax.psum_scatter(term_down, ('fsdp', 'dp'), scatter_dimension=0, tiled=True)  36.4 us
    reduce_scatter x1, waiting for transfers between devices, per_device(): lax.psum_scatter(term_up, ('fsdp', 'dp'), scatter_dimension=1, tiled=True)  23.4 us
    all_gather x1, waiting for transfers between devices, per_device(): lax.all_gather(lowering_projections, 'fsdp', axis=0, tiled=True)  19.6 us
    dot_general x1, matrix products, base_grad(): jnp.einsum('srk,nk->srn', grads, weight_rows, preferred_element_type=jnp....  12.9 us
    convert_element_type x1, other arithmetic, per_device(): hidden = (normed * normalizer_scales).astype(jnp.bfloat16)  9.63 us
    dot_general x1, matrix products, per_device(): jnp.einsum('srm,dm->srd', middle_product, down_full, preferred_element_ty...  7.09 us
  transfers between devices with their start and end apart: 4, of which 4 were waited for; matrix products, arithmetic and copies ran while one was open for 8% of the time, Pallas kernels for 0%

commit v1 on v0

--- a/solution.py
+++ b/solution.py
@@ -1,6 +1,10 @@
+import functools
+
 import jax
 import jax.numpy as jnp
 from jax import lax
+from jax.experimental import pallas as pl
+from jax.experimental.pallas import tpu as pltpu
 from jax.sharding import PartitionSpec as P
 
 LOW_DIM = 64
@@ -8,6 +12,10 @@
 
 
 epsilon = 1e-06
+
+F32 = jnp.float32
+BF16 = jnp.bfloat16
+MIB = 1024 * 1024
 
 
 def base_grad(grads, weight_rows):
@@ -15,7 +23,7 @@
     return product.astype(jnp.bfloat16)
 
 
-def per_device(
+def per_device_any(
     skip_stream,
     projected_output_adjoint,
     frozen_projection_kernel,
@@ -73,6 +81,336 @@
     return (residual_grad, sum_down * inverse[None, :], sum_up * inverse[:, None])
 
 
+def nt_dot(a, b):
+    return lax.dot_general(a, b, (((1,), (1,)), ((), ())), preferred_element_type=F32)
+
+
+def tn_dot(a, b):
+    return lax.dot_general(a, b, (((0,), (0,)), ((), ())), preferred_element_type=F32)
+
+
+def params(mib=48):
+    return pltpu.CompilerParams(vmem_limit_bytes=mib * MIB)
+
+
+def norm_kernel(slot_ref, cols_ref, skip_ref, grad_ref, up_ref, scale_ref, hidden_ref, mid_ref, live_ref, rel_ref, inv_ref):
+    step = pl.program_id(0)
+    slots, rows, width = skip_ref.shape
+    tokens = slots * rows
+    kdim = grad_ref.shape[2]
+    low = up_ref.shape[0]
+    wide = skip_ref[...].reshape(tokens, width).astype(F32)
+    inverse = lax.rsqrt(jnp.mean(wide * wide, axis=-1, keepdims=True) + epsilon)
+    inv_ref[...] = jnp.broadcast_to(inverse, inv_ref.shape)
+    hidden_ref[...] = (wide * inverse * scale_ref[...]).astype(BF16)
+    lane_member = lax.broadcasted_iota(jnp.int32, (rows, low), 1) // LOW_DIM
+    masks = []
+    for s in range(slots):
+        local = slot_ref[step * slots + s]
+        alive = jnp.logical_and(local >= 0, local < low // LOW_DIM)
+        live_ref[s * rows : (s + 1) * rows, :] = jnp.where(alive, grad_ref[s], jnp.zeros_like(grad_ref[s]))
+        masks.append(lane_member == local)
+    live = live_ref[...]
+    mid = nt_dot(live, up_ref[...])
+    mid_ref[...] = jnp.where(jnp.concatenate(masks, axis=0), mid, 0.0).astype(BF16)
+    for j in range(kdim // 128):
+        at = pl.multiple_of(cols_ref[j] * 128, 128)
+        rel_ref[:, j * 128 : (j + 1) * 128] = live_ref[:, pl.ds(at, 128)]
+
+
+def norm_call(slots_local, cols, skip, grad, up, scales, per_step):
+    count, rows, width = skip.shape
+    kdim = grad.shape[2]
+    low = up.shape[0]
+    block = per_step * rows
+    tokens = count * rows
+    row_block = lambda n: pl.BlockSpec((block, n), lambda i, *_: (i, 0))
+    return pl.pallas_call(
+        norm_kernel,
+        out_shape=(
+            jax.ShapeDtypeStruct((tokens, width), BF16),
+            jax.ShapeDtypeStruct((tokens, low), BF16),
+            jax.ShapeDtypeStruct((tokens, kdim), BF16),
+            jax.ShapeDtypeStruct((tokens, kdim), BF16),
+            jax.ShapeDtypeStruct((tokens, 128), F32),
+        ),
+        grid_spec=pltpu.PrefetchScalarGridSpec(
+            num_scalar_prefetch=2,
+            grid=(count // per_step,),
+            in_specs=[
+                pl.BlockSpec((per_step, rows, width), lambda i, *_: (i, 0, 0)),
+                pl.BlockSpec((per_step, rows, kdim), lambda i, *_: (i, 0, 0)),
+                pl.BlockSpec((low, kdim), lambda i, *_: (0, 0)),
+                pl.BlockSpec((1, width), lambda i, *_: (0, 0)),
+            ],
+            out_specs=[row_block(width), row_block(low), row_block(kdim), row_block(kdim), row_block(128)],
+        ),
+        compiler_params=params(),
+        cost_estimate=pl.CostEstimate(flops=2 * tokens * kdim * low, bytes_accessed=2 * tokens * (2 * width + 3 * kdim), transcendentals=0),
+        name="norm",
+    )(slots_local, cols, skip, grad, up, scales)
+
+
+def terms_kernel(slot_ref, blocks_ref, hidden_ref, mid_ref, keep_ref, other_ref, live_ref, out_ref, up_ref, proj_ref):
+    k = pl.program_id(0)
+    steps = pl.num_programs(0)
+    half = keep_ref.shape[1]
+    out_ref[0, 0] = tn_dot(mid_ref[...], hidden_ref[...])
+
+    @pl.when(k == 0)
+    def _():
+        proj_ref[...] = jnp.zeros_like(proj_ref)
+
+    down = jnp.where(k % 2 == 0, keep_ref[k // 2], other_ref[k // 2])
+    proj_ref[...] += jnp.dot(hidden_ref[...], down, preferred_element_type=F32)
+
+    @pl.when(k == steps - 1)
+    def _():
+        tokens, low = proj_ref.shape
+        count = slot_ref.shape[0]
+        rows = tokens // count
+        lane_member = lax.broadcasted_iota(jnp.int32, (rows, low), 1) // LOW_DIM
+        mask = jnp.concatenate([lane_member == slot_ref[s] for s in range(count)], axis=0)
+        projected = jnp.where(mask, proj_ref[...], 0.0).astype(BF16)
+        for j in range(steps):
+            at = pl.multiple_of(blocks_ref[j] * 128, 128)
+            up_ref[j % 2, j // 2] = tn_dot(projected, live_ref[:, pl.ds(at, 128)])
+
+
+def terms_call(slots_local, blocks, hidden, mid, keep, other, live):
+    tokens, width = hidden.shape
+    low = mid.shape[1]
+    fsdp, half, _ = keep.shape
+    steps = 2 * fsdp
+    whole = lambda a: pl.BlockSpec(a.shape, lambda k, *_: (0,) * a.ndim)
+    return pl.pallas_call(
+        terms_kernel,
+        out_shape=(
+            jax.ShapeDtypeStruct((2, fsdp, low, half), F32),
+            jax.ShapeDtypeStruct((2, fsdp, low, 128), F32),
+        ),
+        grid_spec=pltpu.PrefetchScalarGridSpec(
+            num_scalar_prefetch=2,
+            grid=(steps,),
+            in_specs=[
+                pl.BlockSpec((tokens, half), lambda k, slot, blocks: (0, blocks[k])),
+                whole(mid),
+                whole(keep),
+                whole(other),
+                whole(live),
+            ],
+            out_specs=[
+                pl.BlockSpec((1, 1, low, half), lambda k, *_: (k % 2, k // 2, 0, 0)),
+                pl.BlockSpec((2, fsdp, low, 128), lambda k, *_: (0, 0, 0, 0)),
+            ],
+            scratch_shapes=[pltpu.VMEM((tokens, low), F32)],
+        ),
+        compiler_params=params(),
+        cost_estimate=pl.CostEstimate(flops=4 * tokens * width * low, bytes_accessed=2 * tokens * width, transcendentals=0),
+        name="terms",
+    )(slots_local, blocks, hidden, mid, keep, other, live)
+
+
+def base_own_kernel(live_ref, weight_ref, out_ref):
+    out_ref[...] = nt_dot(live_ref[...], weight_ref[...]).astype(BF16)
+
+
+def base_own_call(live, weight):
+    tokens, kdim = live.shape
+    n = weight.shape[0]
+    return pl.pallas_call(
+        base_own_kernel,
+        out_shape=jax.ShapeDtypeStruct((tokens, n), BF16),
+        grid=(n // 256,),
+        in_specs=[
+            pl.BlockSpec((tokens, kdim), lambda i: (0, 0)),
+            pl.BlockSpec((256, kdim), lambda i: (i, 0)),
+        ],
+        out_specs=pl.BlockSpec((tokens, 256), lambda i: (0, i)),
+        compiler_params=params(),
+        cost_estimate=pl.CostEstimate(flops=2 * tokens * kdim * n, bytes_accessed=2 * (n * kdim + tokens * (n + kdim)), transcendentals=0),
+        name="base_own",
+    )(live, weight)
+
+
+def base_kernel(rel_ref, mine_ref, theirs_ref, out_ref):
+    total = None
+    for part, ref in enumerate((mine_ref, theirs_ref)):
+        for i in range(2):
+            weight = jnp.concatenate([ref[2 * i], ref[2 * i + 1]], axis=-1)
+            at = (part * 2 + i) * 256
+            term = nt_dot(rel_ref[:, at : at + 256], weight)
+            total = term if total is None else total + term
+    out_ref[...] = total.astype(BF16)
+
+
+def base_call(rel, mine, theirs):
+    tokens, kdim = rel.shape
+    n = mine.shape[1]
+    piece = pl.BlockSpec((4, 256, 128), lambda i: (0, i, 0))
+    return pl.pallas_call(
+        base_kernel,
+        out_shape=jax.ShapeDtypeStruct((tokens, n), BF16),
+        grid=(n // 256,),
+        in_specs=[pl.BlockSpec((tokens, kdim), lambda i: (0, 0)), piece, piece],
+        out_specs=pl.BlockSpec((tokens, 256), lambda i: (0, i)),
+        compiler_params=params(),
+        cost_estimate=pl.CostEstimate(flops=2 * tokens * kdim * n, bytes_accessed=2 * (n * kdim + tokens * (n + kdim)), transcendentals=0),
+        name="base",
+    )(rel, mine, theirs)
+
+
+def residual_kernel(blocks_ref, skip_ref, inv_ref, mid_ref, keep_ref, other_ref, scale_ref, *rest):
+    *bases, out_ref, scaled_ref = rest
+    slots, rows, width = skip_ref.shape
+    tokens = slots * rows
+    half = keep_ref.shape[1]
+    inverse = inv_ref[:, :1]
+    mid = mid_ref[...]
+    total = jnp.zeros((tokens, 1), F32)
+    for r, base_ref in enumerate(bases):
+        for h in range(2):
+            block = blocks_ref[2 * r + h]
+            at = pl.multiple_of(block * half, 128)
+            inside = pl.multiple_of((block % 2) * half, 128)
+            down = (keep_ref if h == 0 else other_ref)[r]
+            grad = base_ref[:, pl.ds(inside, half)].astype(F32) + nt_dot(mid, down)
+            scaled = grad * scale_ref[:, pl.ds(at, half)]
+            scaled_ref[:, pl.ds(at, half)] = scaled
+            normed = skip_ref[:, :, pl.ds(at, half)].reshape(tokens, half).astype(F32) * inverse
+            total += jnp.sum(scaled * normed, axis=-1, keepdims=True)
+    mean = total * (inverse / width)
+    for k in range(2 * len(bases)):
+        cols = slice(k * half, (k + 1) * half)
+        wide = skip_ref[:, :, cols].reshape(tokens, half).astype(F32)
+        out = (scaled_ref[:, cols] - wide * mean) * inverse
+        out_ref[:, :, cols] = out.astype(BF16).reshape(slots, rows, half)
+
+
+def residual_call(blocks, skip, inv, mid, keep, other, scales, bases, per_step):
+    count, rows, width = skip.shape
+    low = mid.shape[1]
+    block = per_step * rows
+    n = bases[0].shape[1]
+    tokens = count * rows
+    row_block = lambda m: pl.BlockSpec((block, m), lambda i, *_: (i, 0))
+    whole = lambda a: pl.BlockSpec(a.shape, lambda k, *_: (0,) * a.ndim)
+    return pl.pallas_call(
+        residual_kernel,
+        out_shape=jax.ShapeDtypeStruct(skip.shape, BF16),
+        grid_spec=pltpu.PrefetchScalarGridSpec(
+            num_scalar_prefetch=1,
+            grid=(count // per_step,),
+            in_specs=[
+                pl.BlockSpec((per_step, rows, width), lambda i, *_: (i, 0, 0)),
+                row_block(128),
+                row_block(low),
+                whole(keep),
+                whole(other),
+                whole(scales),
+            ]
+            + [row_block(n)] * len(bases),
+            out_specs=pl.BlockSpec((per_step, rows, width), lambda i, *_: (i, 0, 0)),
+            scratch_shapes=[pltpu.VMEM((block, width), F32)],
+        ),
+        compiler_params=params(),
+        cost_estimate=pl.CostEstimate(flops=2 * tokens * width * low, bytes_accessed=6 * tokens * width, transcendentals=0),
+        name="residual",
+    )(blocks, skip, inv, mid, keep, other, scales, *bases)
+
+
+def finish_kernel(inv_ref, own_ref, *rest):
+    *others, down_ref, up_ref = rest
+    total = own_ref[0]
+    for ref in others:
+        total = total + ref[...].astype(F32)
+    total = total * inv_ref[:, :1]
+    half = down_ref.shape[0]
+    down_ref[...] = total[:, :half].T
+    up_ref[...] = total[:, half:]
+
+
+def finish_call(inverse, own, others):
+    low, both = own.shape[1:]
+    half = both - 128
+    return pl.pallas_call(
+        finish_kernel,
+        out_shape=(jax.ShapeDtypeStruct((half, low), F32), jax.ShapeDtypeStruct((low, 128), F32)),
+        grid=(1,),
+        in_specs=[
+            pl.BlockSpec(inverse.shape, lambda i: (0, 0)),
+            pl.BlockSpec((1, low, both), lambda i: (0, 0, 0)),
+        ]
+        + [pl.BlockSpec((low, both), lambda i: (0, 0))] * len(others),
+        out_specs=[pl.BlockSpec((half, low), lambda i: (0, 0)), pl.BlockSpec((low, 128), lambda i: (0, 0))],
+        compiler_params=params(),
+        name="finish",
+    )(inverse, own, *others)
+
+
+SWAP = [(0, 1), (1, 0)]
+
+
+def per_device_square(
+    fsdp,
+    skip,
+    grad,
+    weight,
+    down,
+    up,
+    scales,
+    assignee,
+):
+    z = lax.axis_index("fsdp")
+    c = lax.axis_index("dp")
+    m = lax.axis_index("member")
+    piece = c * 4 + lax.axis_index("parts") * 2 + m
+    half = down.shape[0] // 2
+    low = up.shape[0]
+    members = low // LOW_DIM
+
+    shift = lambda v, r: lax.ppermute(v, "fsdp", [(i, (i + r) % fsdp) for i in range(fsdp)])
+    over = lambda v, axis: lax.ppermute(v, axis, SWAP)
+
+    down_half = lax.dynamic_slice_in_dim(down, c * half, half, 0)
+    unit = lax.dynamic_slice_in_dim(weight, piece * 128, 128, 1)
+    keep = jnp.stack([down_half] + [shift(down_half, -r) for r in range(1, fsdp)])
+    other = over(keep, "dp")
+    mine, theirs = [], []
+    for r in range(1, fsdp):
+        u = shift(unit, -r)
+        ux = over(u, "member")
+        uy = over(u, "parts")
+        mid_row = u.shape[0] // 2
+        d0 = over(ux[:mid_row], "parts")
+        d1 = over(uy[mid_row:], "member")
+        own = jnp.concatenate([u, ux, uy, d0, d1], axis=0).reshape(4, u.shape[0], 128)
+        mine.append(own)
+        theirs.append(over(own, "dp"))
+
+    local = assignee - m * members
+    cols = piece ^ jnp.arange(8, dtype=jnp.int32)
+    steps = jnp.arange(2 * fsdp, dtype=jnp.int32)
+    blocks = ((z + steps // 2) % fsdp) * 2 + (c ^ (steps % 2))
+    scale_row = scales[None, :]
+
+    hidden, mid, live, rel, inv = norm_call(local, cols, skip, grad, up, scale_row, 2)
+    bases = [base_own_call(live, weight)]
+    term_down, term_up = terms_call(local, blocks, hidden, mid, keep, other, live)
+    terms = jnp.concatenate([term_down, term_up], axis=-1)
+    summed = terms[0] + over(terms[1], "dp")
+    sent = summed.astype(BF16)
+    others = [shift(sent[r], r) for r in range(1, fsdp)]
+    counts = jnp.sum((local[:, None] == jnp.arange(members)[None, :]).astype(F32), axis=0)
+    inverse = jnp.repeat(1.0 / (BLOCK * counts), LOW_DIM)
+    grad_down, grad_up = finish_call(jnp.broadcast_to(inverse[:, None], (low, 128)), summed, others)
+
+    for own, far in zip(mine, theirs):
+        bases.append(base_call(rel, own, far))
+    residual = residual_call(blocks, skip, inv, mid, keep, other, scale_row, bases, 2)
+    return residual, grad_down, grad_up
+
+
 def solution(mesh):
     placed = (
         P(("parts", "member"), ("fsdp", "dp"), None),
@@ -83,8 +421,10 @@
         P(),
         P(("parts", "member")),
     )
+    sizes = dict(mesh.shape)
+    square = sizes["parts"] == 2 and sizes["member"] == 2 and sizes["dp"] == 2 and sizes["fsdp"] == 4
     return jax.shard_map(
-        per_device,
+        functools.partial(per_device_square, sizes["fsdp"]) if square else per_device_any,
         mesh=mesh,
         in_specs=placed,
         out_specs=(

time: 328 us -> 137 us (0.42)
  waiting for transfers between devices: 263 us -> 20.5 us
  Pallas kernels: 0 us -> 48.4 us
  starting transfers between devices: 0.16 us -> 38.2 us
  matrix products: 33.1 us -> 0 us
  local copies, waits for them, and re-layouts: 0.35 us -> 23.8 us
  other arithmetic: 18.1 us -> 4.32 us
  between operations: 13.9 us -> 0.9 us
    all_gather x2 -> x0, waiting for transfers between devices: 201 us -> none  [the longest x1 182 us: per_device(): lax.all_gather(frozen_projection_kernel, 'fsdp', axis=0, tiled=True)]
    reduce_scatter x2 -> x0, waiting for transfers between devices: 59.9 us -> none  [the longest x1 36.4 us: per_device(): lax.psum_scatter(term_down, ('fsdp', 'dp'), scatter_dimension=0, tiled=True)]
    pallas_call x0 -> x8, Pallas kernels: none -> 48.4 us  [the longest x3 14.6 us: base_call(): pl.pallas_call(base_kernel, out_shape=jax.ShapeDtypeStruct((tokens, n), B...]
    ppermute x0 -> x26, starting transfers between devices: none -> 38.2 us  [the longest x9 22.4 us: per_device_square(): lax.ppermute(v, 'fsdp', [(i, (i + r) % fsdp) for i in range(fsdp)])]
    dot_general x5 -> x0, matrix products: 33.1 us -> none  [the longest x1 12.9 us: base_grad(): jnp.einsum('srk,nk->srn', grads, weight_rows, preferred_element_type=jnp....]
    ppermute x0 -> x26, waiting for transfers between devices: none -> 20.5 us  [the longest x9 10.4 us: per_device_square(): lax.ppermute(v, 'fsdp', [(i, (i + r) % fsdp) for i in range(fsdp)])]
    unnamed x10 -> x41, local copies, waits for them, and re-layouts: 0.03 us -> 18.2 us
    convert_element_type x1, other arithmetic: 9.63 us -> 2.37 us  [per_device_square(): sent = summed.astype(BF16)]
  transfers between devices with their start and end apart: 4 -> 26, of which waited for: 4 -> 7; matrix products, arithmetic and copies ran while one was open for 8% -> 14% of each run, Pallas kernels for 0% -> 35%
where the time goes in v1:
time: 137 us; the launch traced here: 136 us
  Pallas kernels  48.4 us (35%)
  starting transfers between devices  38.2 us (28%)
  local copies, waits for them, and re-layouts  23.8 us (17%)
  waiting for transfers between devices  20.5 us (15%)
  other arithmetic  4.32 us (3%)
    ppermute x9, starting transfers between devices, per_device_square(): lax.ppermute(v, 'fsdp', [(i, (i + r) % fsdp) for i in range(fsdp)])  22.4 us
    unnamed x41, local copies, waits for them, and re-layouts  18.2 us
    ppermute x17, starting transfers between devices, per_device_square(): over = lambda v, axis: lax.ppermute(v, axis, SWAP)  15.9 us
    pallas_call x3, Pallas kernels, base_call(): pl.pallas_call(base_kernel, out_shape=jax.ShapeDtypeStruct((tokens, n), B...  14.6 us
    pallas_call x1, Pallas kernels, residual_call(): pl.pallas_call(residual_kernel, out_shape=jax.ShapeDtypeStruct(skip.shape...  11.1 us
    ppermute x9, waiting for transfers between devices, per_device_square(): lax.ppermute(v, 'fsdp', [(i, (i + r) % fsdp) for i in range(fsdp)])  10.4 us
    ppermute x17, waiting for transfers between devices, per_device_square(): over = lambda v, axis: lax.ppermute(v, axis, SWAP)  10.1 us
    pallas_call x1, Pallas kernels, terms_call(): pl.pallas_call(terms_kernel, out_shape=(jax.ShapeDtypeStruct((2, fsdp, lo...  9.81 us
  transfers between devices with their start and end apart: 26, of which 7 were waited for; matrix products, arithmetic and copies ran while one was open for 14% of the time, Pallas kernels for 35%

profile of v1, /device:TPU:0, one launch (start us, length us, event | category | flops | bytes accessed | tf_op | source)
XLA Modules:
  0.0 136.2 jit_solution(9680548252421548788)
XLA Ops:
  0.7 1.0 copy-done
  1.6 0.7 constant_dynamic-slice_fusion.1
  2.3 5.0 %collective-permute-start = (bf16[640,128]{1,0:T(8,128)(2,1)}, bf16[640,128]{1,0:T(8,128)(2,1)S(1)}, u32[]{:S(2)}, u32[]{:S(2)}) collective-permute-start(bf16[640,128]{1,0:T(8,128)(2,1)} %constant_dynamic-slice_fusion.1), channel_id=1, source_target_pairs={{0,12},{4,0},{8,4},{12,8},{1,13},{5,1},{9,5},{13,9},{2,14},{6,2},{... | collective-permute-start | bytes 491528 | tf_op jit(solution)/shard_map/ppermute | solution.py:372
  7.3 1.0 collective-permute-start.2
  8.3 1.0 constant_dynamic-slice_fusion
  9.3 2.5 %collective-permute-start.16 = (bf16[1280,128]{1,0:T(8,128)(2,1)S(1)}, bf16[1280,128]{1,0:T(8,128)(2,1)S(1)}, u32[]{:S(2)}, u32[]{:S(2)}) collective-permute-start(bf16[1280,128]{1,0:T(8,128)(2,1)S(1)} %constant_dynamic-slice_fusion), channel_id=1, source_target_pairs={{0,4},{4,8},{8,12},{12,0},{1,5},{5,9},{9,13},{13,1},{2,6},{6,10},{... | collective-permute-start | bytes 983048 | tf_op jit(solution)/shard_map/ppermute | solution.py:372
  11.9 0.9 collective-permute-start.10
  12.8 0.7 broadcast_subtract_fusion.slot_ref
  13.5 1.3 copy-done.3
  14.8 0.9 copy-done.4
  15.7 0.7 copy-done.5
  16.4 9.1 %norm.1 = (bf16[640,5120]{1,0:T(8,128)(2,1)}, bf16[640,128]{1,0:T(8,128)(2,1)S(1)}, bf16[640,1024]{1,0:T(8,128)(2,1)S(1)}, bf16[640,1024]{1,0:T(8,128)(2,1)S(1)}, f32[640,128]{1,0:T(8,128)S(1)}) custom-call(s32[10]{0:T(128)S(1)} %broadcast_subtract_fusion.slot_ref, s32[8]{0:T(128)S(1)} %iota_xor_fusion.cols_ref, bf16[10,64,5120]{2,1,0:T(8,128)(2,1)} %skip_ref.3, ...), custom_call_target="tpu_custom_call" | custom-call | flops 167772160 | bytes 17039360 | tf_op jit(solution)/shard_map/norm/pallas_call | solution.py:128
  25.6 1.6 %collective-permute-start.4 = (bf16[1280,128]{1,0:T(8,128)(2,1)S(1)}, bf16[1280,128]{1,0:T(8,128)(2,1)S(1)}, u32[]{:S(2)}, u32[]{:S(2)}) collective-permute-start(bf16[1280,128]{1,0:T(8,128)(2,1)S(1)} %constant_dynamic-slice_fusion), channel_id=1, source_target_pairs={{0,12},{4,0},{8,4},{12,8},{1,13},{5,1},{9,5},{13,9},{2,14},{6,2},{... | collective-permute-start | bytes 983048 | tf_op jit(solution)/shard_map/ppermute | solution.py:372
  27.2 9.0 %collective-permute-done.1 = bf16[640,128]{1,0:T(8,128)(2,1)S(1)} collective-permute-done((bf16[640,128]{1,0:T(8,128)(2,1)}, bf16[640,128]{1,0:T(8,128)(2,1)S(1)}, u32[]{:S(2)}, u32[]{:S(2)}) %collective-permute-start.1) | collective-permute-done | bytes 163872 | tf_op jit(solution)/shard_map/ppermute | solution.py:372
  36.1 0.7 copy-done.13
  36.8 1.2 pad_maximum_fusion.keep_ref
  37.9 1.6 %collective-permute-start.17 = (bf16[1280,128]{1,0:T(8,128)(2,1)S(1)}, bf16[1280,128]{1,0:T(8,128)(2,1)S(1)}, u32[]{:S(2)}, u32[]{:S(2)}) collective-permute-start(bf16[1280,128]{1,0:T(8,128)(2,1)S(1)} %collective-permute-done.16), channel_id=1, source_target_pairs={{0,2},{2,0},{1,3},{3,1},{4,6},{6,4},{5,7},{7,5},{8,10},{10,8},{9,1... | collective-permute-start | bytes 983048 | tf_op jit(solution)/shard_map/ppermute | solution.py:373
  39.5 0.8 constant_dynamic-update-slice_fusion.14
  40.3 1.5 %collective-permute-start.18 = (bf16[1280,128]{1,0:T(8,128)(2,1)S(1)}, bf16[1280,128]{1,0:T(8,128)(2,1)S(1)}, u32[]{:S(2)}, u32[]{:S(2)}) collective-permute-start(bf16[1280,128]{1,0:T(8,128)(2,1)S(1)} %collective-permute-done.16), channel_id=1, source_target_pairs={{0,16},{16,0},{1,17},{17,1},{2,18},{18,2},{3,19},{19,3},{4,20},{20... | collective-permute-start | bytes 983048 | tf_op jit(solution)/shard_map/ppermute | solution.py:373
  41.8 1.4 %collective-permute-done.10 = bf16[1280,128]{1,0:T(8,128)(2,1)} collective-permute-done((bf16[1280,128]{1,0:T(8,128)(2,1)S(1)}, bf16[1280,128]{1,0:T(8,128)(2,1)}, u32[]{:S(2)}, u32[]{:S(2)}) %collective-permute-start.10) | collective-permute-done | bytes 327712 | tf_op jit(solution)/shard_map/ppermute | solution.py:372
  43.2 1.5 %collective-permute-start.11 = (bf16[1280,128]{1,0:T(8,128)(2,1)}, bf16[1280,128]{1,0:T(8,128)(2,1)S(1)}, u32[]{:S(2)}, u32[]{:S(2)}) collective-permute-start(bf16[1280,128]{1,0:T(8,128)(2,1)} %collective-permute-done.10), channel_id=1, source_target_pairs={{0,2},{2,0},{1,3},{3,1},{4,6},{6,4},{5,7},{7,5},{8,10},{10,8},{9,1... | collective-permute-start | bytes 983048 | tf_op jit(solution)/shard_map/ppermute | solution.py:373
  44.7 1.5 %collective-permute-start.12 = (bf16[1280,128]{1,0:T(8,128)(2,1)}, bf16[1280,128]{1,0:T(8,128)(2,1)S(1)}, u32[]{:S(2)}, u32[]{:S(2)}) collective-permute-start(bf16[1280,128]{1,0:T(8,128)(2,1)} %collective-permute-done.10), channel_id=1, source_target_pairs={{0,16},{16,0},{1,17},{17,1},{2,18},{18,2},{3,19},{19,3},{4,20},{20... | collective-permute-start | bytes 983048 | tf_op jit(solution)/shard_map/ppermute | solution.py:373
  46.2 0.5 collective-permute-start.5
  46.7 1.7 %constant_dynamic-update-slice_fusion.9 = bf16[5120,128]{1,0:T(8,128)(2,1)} fusion(bf16[1280,128]{1,0:T(8,128)(2,1)} %collective-permute-done.10), kind=kLoop, calls=%fused_computation.16 | loop fusion | bytes 655360
  48.5 1.1 collective-permute-start.6
  49.6 0.8 constant_dynamic-update-slice_fusion.4
  50.8 4.3 %collective-permute-done.11 = bf16[1280,128]{1,0:T(8,128)(2,1)S(1)} collective-permute-done((bf16[1280,128]{1,0:T(8,128)(2,1)}, bf16[1280,128]{1,0:T(8,128)(2,1)S(1)}, u32[]{:S(2)}, u32[]{:S(2)}) %collective-permute-start.11) | collective-permute-done | bytes 327712 | tf_op jit(solution)/shard_map/ppermute | solution.py:373
  55.1 1.5 %collective-permute-start.19 = (bf16[640,128]{1,0:T(8,128)(2,1)S(1)}, bf16[640,128]{1,0:T(8,128)(2,1)S(1)}, u32[]{:S(2)}, u32[]{:S(2)}) collective-permute-start(bf16[640,128]{1,0:T(8,128)(2,1)S(1)} %slice.48), channel_id=1, source_target_pairs={{0,16},{16,0},{1,17},{17,1},{2,18},{18,2},{3,19},{19,3},{4,20},{20... | collective-permute-start | bytes 491528 | tf_op jit(solution)/shard_map/ppermute | solution.py:373
  56.6 1.2 collective-permute-done.12
  57.8 0.5 collective-permute-start.20
  58.3 3.7 %collective-permute-done.5 = bf16[1280,128]{1,0:T(8,128)(2,1)S(1)} collective-permute-done((bf16[1280,128]{1,0:T(8,128)(2,1)S(1)}, bf16[1280,128]{1,0:T(8,128)(2,1)S(1)}, u32[]{:S(2)}, u32[]{:S(2)}) %collective-permute-start.5) | collective-permute-done | bytes 327712 | tf_op jit(solution)/shard_map/ppermute | solution.py:373
  62.1 1.5 %collective-permute-start.13 = (bf16[640,128]{1,0:T(8,128)(2,1)S(1)}, bf16[640,128]{1,0:T(8,128)(2,1)S(1)}, u32[]{:S(2)}, u32[]{:S(2)}) collective-permute-start(bf16[640,128]{1,0:T(8,128)(2,1)S(1)} %slice.46), channel_id=1, source_target_pairs={{0,16},{16,0},{1,17},{17,1},{2,18},{18,2},{3,19},{19,3},{4,20},{20... | collective-permute-start | bytes 491528 | tf_op jit(solution)/shard_map/ppermute | solution.py:373
  63.6 0.7 constant_dynamic-update-slice_fusion.13
  64.8 1.1 collective-permute-start.14
  65.9 0.8 constant_dynamic-update-slice_fusion.12
  66.6 0.7 constant_dynamic-update-slice_fusion.8
  67.4 0.7 constant_dynamic-update-slice_fusion.7
  68.1 1.0 collective-permute-start.7
  69.1 9.8 %terms.1 = (f32[2,4,128,640]{3,2,1,0:T(8,128)S(1)}, f32[2,4,128,128]{3,2,1,0:T(8,128)S(1)}) custom-call(s32[10]{0:T(128)S(1)} %broadcast_subtract_fusion.slot_ref, s32[8]{0:T(128)S(1)} %fusion.3.blocks_ref, bf16[640,5120]{1,0:T(8,128)(2,1)} %get-tuple-element.16.hidden_ref, bf16[640,128]{1,0:T(8,128)(2,1)S(1)} %get-tuple-element.13.mid_ref, ...), custom_call_target="tpu_custom_call" | custom-call | flops 1677721600 | bytes 6553600 | tf_op jit(solution)/shard_map/terms/pallas_call | solution.py:186
  79.2 1.5 %slice_bitcast_fusion = f32[4,128,768]{2,1,0:T(8,128)} fusion(f32[2,4,128,768]{3,2,1,0:T(8,128)S(1)} %constant_dynamic-update-slice_fusion.15), kind=kLoop, calls=%fused_computation | loop fusion | bytes 3145728 | tf_op jit(solution)/shard_map/squeeze | solution.py:401
  80.8 0.7 copy-done.10
  81.4 1.5 %collective-permute-start.8 = (bf16[640,128]{1,0:T(8,128)(2,1)S(1)}, bf16[640,128]{1,0:T(8,128)(2,1)S(1)}, u32[]{:S(2)}, u32[]{:S(2)}) collective-permute-start(bf16[640,128]{1,0:T(8,128)(2,1)S(1)} %slice.45), channel_id=1, source_target_pairs={{0,2},{2,0},{1,3},{3,1},{4,6},{6,4},{5,7},{7,5},{8,10},{10,8},{9,1... | collective-permute-start | bytes 491528 | tf_op jit(solution)/shard_map/ppermute | solution.py:373
  82.9 0.7 constant_dynamic-update-slice_fusion.11
  83.6 0.7 constant_dynamic-update-slice_fusion.10
  84.3 0.5 collective-permute-start.21
  84.8 0.7 constant_dynamic-update-slice_fusion.6
  85.5 0.7 constant_dynamic-update-slice_fusion.5
  86.1 0.7 constant_dynamic-update-slice_fusion.3
  86.9 0.7 constant_dynamic-update-slice_fusion.2
  87.6 0.7 constant_dynamic-update-slice_fusion.1
  88.3 0.7 constant_dynamic-update-slice_fusion
  89.0 0.5 collective-permute-start.9
  89.8 1.7 %copy-done.7 = bf16[1280,1024]{1,0:T(8,128)(2,1)S(1)} copy-done((bf16[1280,1024]{1,0:T(8,128)(2,1)S(1)}, bf16[1280,1024]{1,0:T(8,128)(2,1)}, u32[]{:S(2)}) %copy-start.7) | copy-done | bytes 2621464
  91.6 2.8 %base_own.1.rest_0_ = bf16[640,1280]{1,0:T(8,128)(2,1)S(1)} custom-call(bf16[640,1024]{1,0:T(8,128)(2,1)S(1)} %get-tuple-element.14.live_ref, bf16[1280,1024]{1,0:T(8,128)(2,1)S(1)} %copy-done.7), custom_call_target="tpu_custom_call" | custom-call | flops 1677721600 | bytes 5570560 | tf_op jit(solution)/shard_map/base_own/pallas_call | solution.py:221
  94.4 4.8 %base.5.rest_3_ = bf16[640,1280]{1,0:T(8,128)(2,1)S(1)} custom-call(bf16[640,1024]{1,0:T(8,128)(2,1)S(1)} %copy-done.9, bf16[4,1280,128]{2,1,0:T(8,128)(2,1)} %bitcast.7.mine_ref, bf16[4,1280,128]{2,1,0:T(8,128)(2,1)} %collective-permute-done.21.theirs_ref), custom_call_target="tpu_custom_call" | custom-call | flops 1677721600 | bytes 5570560 | tf_op jit(solution)/shard_map/base/pallas_call | solution.py:251
  99.2 1.2 copy-done.1
  100.4 4.9 %base.4.rest_2_ = bf16[640,1280]{1,0:T(8,128)(2,1)S(1)} custom-call(bf16[640,1024]{1,0:T(8,128)(2,1)S(1)} %copy-done.9, bf16[4,1280,128]{2,1,0:T(8,128)(2,1)} %bitcast.6.mine_ref, bf16[4,1280,128]{2,1,0:T(8,128)(2,1)} %collective-permute-done.15.theirs_ref), custom_call_target="tpu_custom_call" | custom-call | flops 1677721600 | bytes 5570560 | tf_op jit(solution)/shard_map/base/pallas_call | solution.py:251
  105.4 2.4 %fusion.7 = (bf16[4,128,768]{2,1,0:T(8,128)(2,1)S(1)}, f32[4,128,768]{2,1,0:T(8,128)S(1)}) fusion(f32[4,128,768]{2,1,0:T(8,128)} %collective-permute-done.22, f32[2,4,128,768]{3,2,1,0:T(8,128)S(1)} %copy-done.11), kind=kLoop, calls=%fused_computation.44 | loop fusion | flops 786432 | bytes 5505024 | tf_op jit(solution)/shard_map/convert_element_type | solution.py:402
  107.8 5.0 %collective-permute-start.23 = (bf16[128,768]{1,0:T(8,128)(2,1)S(1)}, bf16[128,768]{1,0:T(8,128)(2,1)S(1)}, u32[]{:S(2)}, u32[]{:S(2)}) collective-permute-start(bf16[128,768]{1,0:T(8,128)(2,1)S(1)} %get-tuple-element.25), channel_id=1, source_target_pairs={{0,4},{4,8},{8,12},{12,0},{1,5},{5,9},{9,13},{13,1},{2,6},{6,10},{... | collective-permute-start | bytes 589832 | tf_op jit(solution)/shard_map/ppermute | solution.py:372
  112.8 3.5 %collective-permute-start.24 = (bf16[128,768]{1,0:T(8,128)(2,1)S(1)}, bf16[128,768]{1,0:T(8,128)(2,1)S(1)}, u32[]{:S(2)}, u32[]{:S(2)}) collective-permute-start(bf16[128,768]{1,0:T(8,128)(2,1)S(1)} %get-tuple-element.24), channel_id=1, source_target_pairs={{0,8},{4,12},{8,0},{12,4},{1,9},{5,13},{9,1},{13,5},{2,10},{6,14},... | collective-permute-start | bytes 589832 | tf_op jit(solution)/shard_map/ppermute | solution.py:372
  116.3 2.8 %collective-permute-start.25 = (bf16[128,768]{1,0:T(8,128)(2,1)S(1)}, bf16[128,768]{1,0:T(8,128)(2,1)S(1)}, u32[]{:S(2)}, u32[]{:S(2)}) collective-permute-start(bf16[128,768]{1,0:T(8,128)(2,1)S(1)} %get-tuple-element.23), channel_id=1, source_target_pairs={{0,12},{4,0},{8,4},{12,8},{1,13},{5,1},{9,5},{13,9},{2,14},{6,2},{... | collective-permute-start | bytes 589832 | tf_op jit(solution)/shard_map/ppermute | solution.py:372
  119.1 4.8 %base.3.rest_1_ = bf16[640,1280]{1,0:T(8,128)(2,1)S(1)} custom-call(bf16[640,1024]{1,0:T(8,128)(2,1)S(1)} %copy-done.9, bf16[4,1280,128]{2,1,0:T(8,128)(2,1)} %bitcast.5.mine_ref, bf16[4,1280,128]{2,1,0:T(8,128)(2,1)} %collective-permute-done.9.theirs_ref), custom_call_target="tpu_custom_call" | custom-call | flops 1677721600 | bytes 5570560 | tf_op jit(solution)/shard_map/base/pallas_call | solution.py:251
  124.0 11.1 %residual.1 = bf16[10,64,5120]{2,1,0:T(8,128)(2,1)} custom-call(s32[8]{0:T(128)S(1)} %fusion.3.blocks_ref, bf16[10,64,5120]{2,1,0:T(8,128)(2,1)} %skip_ref.3, f32[640,128]{1,0:T(8,128)S(1)} %get-tuple-element.12.inv_ref, bf16[640,128]{1,0:T(8,128)(2,1)S(1)} %get-tuple-element.13.mid_ref, bf16[4,640,128]{2,1,0:T(8,128)(2,1)S(1)} %pad_maximum_fusion.keep_ref, ...), custom_call_target="tpu_custom_call" | custom-call | flops 838860800 | bytes 19660800 | tf_op jit(solution)/shard_map/residual/pallas_call | solution.py:298
  135.2 1.0 finish.1
  (62 shorter events, 1.7 us)
Async XLA Ops:
  0.6 1.0 copy-start
  2.3 23.3 %collective-permute-start = (bf16[640,128]{1,0:T(8,128)(2,1)}, bf16[640,128]{1,0:T(8,128)(2,1)S(1)}, u32[]{:S(2)}, u32[]{:S(2)}) collective-permute-start(bf16[640,128]{1,0:T(8,128)(2,1)} %constant_dynamic-slice_fusion.1), channel_id=1, source_target_pairs={{0,12},{4,0},{8,4},{12,8},{1,13},{5,1},{9,5},{13,9},{2,14},{6,2},{... | collective-permute-start | bytes 491528 | tf_op jit(solution)/shard_map/ppermute | solution.py:372
  7.3 28.8 %collective-permute-start.1 = (bf16[640,128]{1,0:T(8,128)(2,1)}, bf16[640,128]{1,0:T(8,128)(2,1)S(1)}, u32[]{:S(2)}, u32[]{:S(2)}) collective-permute-start(bf16[640,128]{1,0:T(8,128)(2,1)} %constant_dynamic-slice_fusion.1), channel_id=1, source_target_pairs={{0,8},{4,12},{8,0},{12,4},{1,9},{5,13},{9,1},{13,5},{2,10},{6,14},... | collective-permute-start | bytes 491528 | tf_op jit(solution)/shard_map/ppermute | solution.py:372
  7.3 28.8 %collective-permute-start.2 = (bf16[640,128]{1,0:T(8,128)(2,1)}, bf16[640,128]{1,0:T(8,128)(2,1)}, u32[]{:S(2)}, u32[]{:S(2)}) collective-permute-start(bf16[640,128]{1,0:T(8,128)(2,1)} %constant_dynamic-slice_fusion.1), channel_id=1, source_target_pairs={{0,4},{4,8},{8,12},{12,0},{1,5},{5,9},{9,13},{13,1},{2,6},{6,10},{... | collective-permute-start | bytes 491528 | tf_op jit(solution)/shard_map/ppermute | solution.py:372
  9.3 28.6 %collective-permute-start.16 = (bf16[1280,128]{1,0:T(8,128)(2,1)S(1)}, bf16[1280,128]{1,0:T(8,128)(2,1)S(1)}, u32[]{:S(2)}, u32[]{:S(2)}) collective-permute-start(bf16[1280,128]{1,0:T(8,128)(2,1)S(1)} %constant_dynamic-slice_fusion), channel_id=1, source_target_pairs={{0,4},{4,8},{8,12},{12,0},{1,5},{5,9},{9,13},{13,1},{2,6},{6,10},{... | collective-permute-start | bytes 983048 | tf_op jit(solution)/shard_map/ppermute | solution.py:372
  11.9 31.3 %collective-permute-start.10 = (bf16[1280,128]{1,0:T(8,128)(2,1)S(1)}, bf16[1280,128]{1,0:T(8,128)(2,1)}, u32[]{:S(2)}, u32[]{:S(2)}) collective-permute-start(bf16[1280,128]{1,0:T(8,128)(2,1)S(1)} %constant_dynamic-slice_fusion), channel_id=1, source_target_pairs={{0,8},{4,12},{8,0},{12,4},{1,9},{5,13},{9,1},{13,5},{2,10},{6,14},... | collective-permute-start | bytes 983048 | tf_op jit(solution)/shard_map/ppermute | solution.py:372
  13.5 1.3 copy-start.3
  14.8 0.9 copy-start.4
  15.7 0.7 copy-start.5
  25.5 22.9 %copy-start.8 = (bf16[640,1024]{1,0:T(8,128)(2,1)}, bf16[640,1024]{1,0:T(8,128)(2,1)S(1)}, u32[]{:S(2)}) copy-start(bf16[640,1024]{1,0:T(8,128)(2,1)S(1)} %get-tuple-element.15.rel_ref) | copy-start | bytes 3932164
  25.6 10.6 %copy-start.12 = (bf16[640,128]{1,0:T(8,128)(2,1)}, bf16[640,128]{1,0:T(8,128)(2,1)S(1)}, u32[]{:S(2)}) copy-start(bf16[640,128]{1,0:T(8,128)(2,1)S(1)} %collective-permute-done) | copy-start | bytes 491524
  25.6 20.6 %collective-permute-start.4 = (bf16[1280,128]{1,0:T(8,128)(2,1)S(1)}, bf16[1280,128]{1,0:T(8,128)(2,1)S(1)}, u32[]{:S(2)}, u32[]{:S(2)}) collective-permute-start(bf16[1280,128]{1,0:T(8,128)(2,1)S(1)} %constant_dynamic-slice_fusion), channel_id=1, source_target_pairs={{0,12},{4,0},{8,4},{12,8},{1,13},{5,1},{9,5},{13,9},{2,14},{6,2},{... | collective-permute-start | bytes 983048 | tf_op jit(solution)/shard_map/ppermute | solution.py:372
  36.1 0.7 copy-start.13
  37.9 10.5 %collective-permute-start.17 = (bf16[1280,128]{1,0:T(8,128)(2,1)S(1)}, bf16[1280,128]{1,0:T(8,128)(2,1)S(1)}, u32[]{:S(2)}, u32[]{:S(2)}) collective-permute-start(bf16[1280,128]{1,0:T(8,128)(2,1)S(1)} %collective-permute-done.16), channel_id=1, source_target_pairs={{0,2},{2,0},{1,3},{3,1},{4,6},{6,4},{5,7},{7,5},{8,10},{10,8},{9,1... | collective-permute-start | bytes 983048 | tf_op jit(solution)/shard_map/ppermute | solution.py:373
  40.3 10.5 %collective-permute-start.18 = (bf16[1280,128]{1,0:T(8,128)(2,1)S(1)}, bf16[1280,128]{1,0:T(8,128)(2,1)S(1)}, u32[]{:S(2)}, u32[]{:S(2)}) collective-permute-start(bf16[1280,128]{1,0:T(8,128)(2,1)S(1)} %collective-permute-done.16), channel_id=1, source_target_pairs={{0,16},{16,0},{1,17},{17,1},{2,18},{18,2},{3,19},{19,3},{4,20},{20... | collective-permute-start | bytes 983048 | tf_op jit(solution)/shard_map/ppermute | solution.py:373
  43.2 11.9 %collective-permute-start.11 = (bf16[1280,128]{1,0:T(8,128)(2,1)}, bf16[1280,128]{1,0:T(8,128)(2,1)S(1)}, u32[]{:S(2)}, u32[]{:S(2)}) collective-permute-start(bf16[1280,128]{1,0:T(8,128)(2,1)} %collective-permute-done.10), channel_id=1, source_target_pairs={{0,2},{2,0},{1,3},{3,1},{4,6},{6,4},{5,7},{7,5},{8,10},{10,8},{9,1... | collective-permute-start | bytes 983048 | tf_op jit(solution)/shard_map/ppermute | solution.py:373
  44.7 13.1 %collective-permute-start.12 = (bf16[1280,128]{1,0:T(8,128)(2,1)}, bf16[1280,128]{1,0:T(8,128)(2,1)S(1)}, u32[]{:S(2)}, u32[]{:S(2)}) collective-permute-start(bf16[1280,128]{1,0:T(8,128)(2,1)} %collective-permute-done.10), channel_id=1, source_target_pairs={{0,16},{16,0},{1,17},{17,1},{2,18},{18,2},{3,19},{19,3},{4,20},{20... | collective-permute-start | bytes 983048 | tf_op jit(solution)/shard_map/ppermute | solution.py:373
  46.2 15.9 %collective-permute-start.5 = (bf16[1280,128]{1,0:T(8,128)(2,1)S(1)}, bf16[1280,128]{1,0:T(8,128)(2,1)S(1)}, u32[]{:S(2)}, u32[]{:S(2)}) collective-permute-start(bf16[1280,128]{1,0:T(8,128)(2,1)S(1)} %collective-permute-done.4), channel_id=1, source_target_pairs={{0,2},{2,0},{1,3},{3,1},{4,6},{6,4},{5,7},{7,5},{8,10},{10,8},{9,1... | collective-permute-start | bytes 983048 | tf_op jit(solution)/shard_map/ppermute | solution.py:373
  48.5 16.3 %collective-permute-start.6 = (bf16[1280,128]{1,0:T(8,128)(2,1)S(1)}, bf16[1280,128]{1,0:T(8,128)(2,1)S(1)}, u32[]{:S(2)}, u32[]{:S(2)}) collective-permute-start(bf16[1280,128]{1,0:T(8,128)(2,1)S(1)} %collective-permute-done.4), channel_id=1, source_target_pairs={{0,16},{16,0},{1,17},{17,1},{2,18},{18,2},{3,19},{19,3},{4,20},{20... | collective-permute-start | bytes 983048 | tf_op jit(solution)/shard_map/ppermute | solution.py:373
  50.8 17.4 %collective-permute-start.3 = (bf16[4,640,128]{2,1,0:T(8,128)(2,1)S(1)}, bf16[4,640,128]{2,1,0:T(8,128)(2,1)S(1)}, u32[]{:S(2)}, u32[]{:S(2)}) collective-permute-start(bf16[4,640,128]{2,1,0:T(8,128)(2,1)S(1)} %pad_maximum_fusion.keep_ref), channel_id=1, source_target_pairs={{0,1},{1,0},{2,3},{3,2},{4,5},{5,4},{6,7},{7,6},{8,9},{9,8},{10,11... | collective-permute-start | bytes 1966088 | tf_op jit(solution)/shard_map/ppermute | solution.py:373
  55.1 26.4 %collective-permute-start.19 = (bf16[640,128]{1,0:T(8,128)(2,1)S(1)}, bf16[640,128]{1,0:T(8,128)(2,1)S(1)}, u32[]{:S(2)}, u32[]{:S(2)}) collective-permute-start(bf16[640,128]{1,0:T(8,128)(2,1)S(1)} %slice.48), channel_id=1, source_target_pairs={{0,16},{16,0},{1,17},{17,1},{2,18},{18,2},{3,19},{19,3},{4,20},{20... | collective-permute-start | bytes 491528 | tf_op jit(solution)/shard_map/ppermute | solution.py:373
  57.8 25.8 %collective-permute-start.20 = (bf16[640,128]{1,0:T(8,128)(2,1)S(1)}, bf16[640,128]{1,0:T(8,128)(2,1)S(1)}, u32[]{:S(2)}, u32[]{:S(2)}) collective-permute-start(bf16[640,128]{1,0:T(8,128)(2,1)S(1)} %slice.49), channel_id=1, source_target_pairs={{0,2},{2,0},{1,3},{3,1},{4,6},{6,4},{5,7},{7,5},{8,10},{10,8},{9,1... | collective-permute-start | bytes 491528 | tf_op jit(solution)/shard_map/ppermute | solution.py:373
  62.1 22.2 %collective-permute-start.13 = (bf16[640,128]{1,0:T(8,128)(2,1)S(1)}, bf16[640,128]{1,0:T(8,128)(2,1)S(1)}, u32[]{:S(2)}, u32[]{:S(2)}) collective-permute-start(bf16[640,128]{1,0:T(8,128)(2,1)S(1)} %slice.46), channel_id=1, source_target_pairs={{0,16},{16,0},{1,17},{17,1},{2,18},{18,2},{3,19},{19,3},{4,20},{20... | collective-permute-start | bytes 491528 | tf_op jit(solution)/shard_map/ppermute | solution.py:373
  64.8 20.7 %collective-permute-start.14 = (bf16[640,128]{1,0:T(8,128)(2,1)S(1)}, bf16[640,128]{1,0:T(8,128)(2,1)S(1)}, u32[]{:S(2)}, u32[]{:S(2)}) collective-permute-start(bf16[640,128]{1,0:T(8,128)(2,1)S(1)} %slice.47), channel_id=1, source_target_pairs={{0,2},{2,0},{1,3},{3,1},{4,6},{6,4},{5,7},{7,5},{8,10},{10,8},{9,1... | collective-permute-start | bytes 491528 | tf_op jit(solution)/shard_map/ppermute | solution.py:373
  68.1 19.5 %collective-permute-start.7 = (bf16[640,128]{1,0:T(8,128)(2,1)S(1)}, bf16[640,128]{1,0:T(8,128)(2,1)S(1)}, u32[]{:S(2)}, u32[]{:S(2)}) collective-permute-start(bf16[640,128]{1,0:T(8,128)(2,1)S(1)} %slice.44), channel_id=1, source_target_pairs={{0,16},{16,0},{1,17},{17,1},{2,18},{18,2},{3,19},{19,3},{4,20},{20... | collective-permute-start | bytes 491528 | tf_op jit(solution)/shard_map/ppermute | solution.py:373
  79.2 2.2 %copy-start.10 = (f32[2,4,128,768]{3,2,1,0:T(8,128)}, f32[2,4,128,768]{3,2,1,0:T(8,128)S(1)}, u32[]{:S(2)}) copy-start(f32[2,4,128,768]{3,2,1,0:T(8,128)S(1)} %constant_dynamic-update-slice_fusion.15) | copy-start | bytes 9437188
  81.4 6.9 %collective-permute-start.8 = (bf16[640,128]{1,0:T(8,128)(2,1)S(1)}, bf16[640,128]{1,0:T(8,128)(2,1)S(1)}, u32[]{:S(2)}, u32[]{:S(2)}) collective-permute-start(bf16[640,128]{1,0:T(8,128)(2,1)S(1)} %slice.45), channel_id=1, source_target_pairs={{0,2},{2,0},{1,3},{3,1},{4,6},{6,4},{5,7},{7,5},{8,10},{10,8},{9,1... | collective-permute-start | bytes 491528 | tf_op jit(solution)/shard_map/ppermute | solution.py:373
  83.6 21.8 %collective-permute-start.22 = (f32[4,128,768]{2,1,0:T(8,128)}, f32[4,128,768]{2,1,0:T(8,128)}, u32[]{:S(2)}, u32[]{:S(2)}) collective-permute-start(f32[4,128,768]{2,1,0:T(8,128)} %slice_bitcast_fusion), channel_id=1, source_target_pairs={{0,1},{1,0},{2,3},{3,2},{4,5},{5,4},{6,7},{7,6},{8,9},{9,8},{10,11... | collective-permute-start | bytes 4718600 | tf_op jit(solution)/shard_map/ppermute | solution.py:373
  84.3 10.1 %collective-permute-start.21 = (bf16[4,1280,128]{2,1,0:T(8,128)(2,1)}, bf16[4,1280,128]{2,1,0:T(8,128)(2,1)}, u32[]{:S(2)}, u32[]{:S(2)}) collective-permute-start(bf16[4,1280,128]{2,1,0:T(8,128)(2,1)} %bitcast.7.mine_ref), channel_id=1, source_target_pairs={{0,1},{1,0},{2,3},{3,2},{4,5},{5,4},{6,7},{7,6},{8,9},{9,8},{10,11... | collective-permute-start | bytes 3932168 | tf_op jit(solution)/shard_map/ppermute | solution.py:373
  86.1 14.3 %collective-permute-start.15 = (bf16[4,1280,128]{2,1,0:T(8,128)(2,1)}, bf16[4,1280,128]{2,1,0:T(8,128)(2,1)}, u32[]{:S(2)}, u32[]{:S(2)}) collective-permute-start(bf16[4,1280,128]{2,1,0:T(8,128)(2,1)} %bitcast.6.mine_ref), channel_id=1, source_target_pairs={{0,1},{1,0},{2,3},{3,2},{4,5},{5,4},{6,7},{7,6},{8,9},{9,8},{10,11... | collective-permute-start | bytes 3932168 | tf_op jit(solution)/shard_map/ppermute | solution.py:373
  89.0 30.1 %collective-permute-start.9 = (bf16[4,1280,128]{2,1,0:T(8,128)(2,1)}, bf16[4,1280,128]{2,1,0:T(8,128)(2,1)}, u32[]{:S(2)}, u32[]{:S(2)}) collective-permute-start(bf16[4,1280,128]{2,1,0:T(8,128)(2,1)} %bitcast.5.mine_ref), channel_id=1, source_target_pairs={{0,1},{1,0},{2,3},{3,2},{4,5},{5,4},{6,7},{7,6},{8,9},{9,8},{10,11... | collective-permute-start | bytes 3932168 | tf_op jit(solution)/shard_map/ppermute | solution.py:373
  89.8 1.7 %copy-start.7 = (bf16[1280,1024]{1,0:T(8,128)(2,1)S(1)}, bf16[1280,1024]{1,0:T(8,128)(2,1)}, u32[]{:S(2)}) copy-start(bf16[1280,1024]{1,0:T(8,128)(2,1)} %weight_ref.1) | copy-start | bytes 7864324
  91.5 2.8 %copy-start.9 = (bf16[640,1024]{1,0:T(8,128)(2,1)S(1)}, bf16[640,1024]{1,0:T(8,128)(2,1)}, u32[]{:S(2)}) copy-start(bf16[640,1024]{1,0:T(8,128)(2,1)} %copy-done.8) | copy-start | bytes 3932164
  99.2 1.2 copy-start.1
  100.4 5.0 %copy-start.11 = (f32[2,4,128,768]{3,2,1,0:T(8,128)S(1)}, f32[2,4,128,768]{3,2,1,0:T(8,128)}, u32[]{:S(2)}) copy-start(f32[2,4,128,768]{3,2,1,0:T(8,128)} %copy-done.10) | copy-start | bytes 9437188
  105.4 2.4 %copy-start.2 = (bf16[640,1280]{1,0:T(8,128)(2,1)}, bf16[640,1280]{1,0:T(8,128)(2,1)S(1)}, u32[]{:S(2)}) copy-start(bf16[640,1280]{1,0:T(8,128)(2,1)S(1)} %base.4.rest_2_) | copy-start | bytes 4915204
  107.8 27.3 %collective-permute-start.23 = (bf16[128,768]{1,0:T(8,128)(2,1)S(1)}, bf16[128,768]{1,0:T(8,128)(2,1)S(1)}, u32[]{:S(2)}, u32[]{:S(2)}) collective-permute-start(bf16[128,768]{1,0:T(8,128)(2,1)S(1)} %get-tuple-element.25), channel_id=1, source_target_pairs={{0,4},{4,8},{8,12},{12,0},{1,5},{5,9},{9,13},{13,1},{2,6},{6,10},{... | collective-permute-start | bytes 589832 | tf_op jit(solution)/shard_map/ppermute | solution.py:372
  112.8 22.2 %collective-permute-start.24 = (bf16[128,768]{1,0:T(8,128)(2,1)S(1)}, bf16[128,768]{1,0:T(8,128)(2,1)S(1)}, u32[]{:S(2)}, u32[]{:S(2)}) collective-permute-start(bf16[128,768]{1,0:T(8,128)(2,1)S(1)} %get-tuple-element.24), channel_id=1, source_target_pairs={{0,8},{4,12},{8,0},{12,4},{1,9},{5,13},{9,1},{13,5},{2,10},{6,14},... | collective-permute-start | bytes 589832 | tf_op jit(solution)/shard_map/ppermute | solution.py:372
  116.3 7.6 %copy-start.6 = (f32[5120]{0:T(1024)S(1)}, f32[5120]{0:T(1024)}, u32[]{:S(2)}) copy-start(f32[5120]{0:T(1024)} %param.12) | copy-start | bytes 61444
  116.3 18.8 %collective-permute-start.25 = (bf16[128,768]{1,0:T(8,128)(2,1)S(1)}, bf16[128,768]{1,0:T(8,128)(2,1)S(1)}, u32[]{:S(2)}, u32[]{:S(2)}) collective-permute-start(bf16[128,768]{1,0:T(8,128)(2,1)S(1)} %get-tuple-element.23), channel_id=1, source_target_pairs={{0,12},{4,0},{8,4},{12,8},{1,13},{5,1},{9,5},{13,9},{2,14},{6,2},{... | collective-permute-start | bytes 589832 | tf_op jit(solution)/shard_map/ppermute | solution.py:372

commit v2 on v0

--- a/solution.py
+++ b/solution.py
@@ -1,6 +1,10 @@
+import functools
+
 import jax
 import jax.numpy as jnp
 from jax import lax
+from jax.experimental import pallas as pl
+from jax.experimental.pallas import tpu as pltpu
 from jax.sharding import PartitionSpec as P
 
 LOW_DIM = 64
@@ -8,6 +12,10 @@
 
 
 epsilon = 1e-06
+
+F32 = jnp.float32
+BF16 = jnp.bfloat16
+MIB = 1024 * 1024
 
 
 def base_grad(grads, weight_rows):
@@ -15,7 +23,7 @@
     return product.astype(jnp.bfloat16)
 
 
-def per_device(
+def per_device_any(
     skip_stream,
     projected_output_adjoint,
     frozen_projection_kernel,
@@ -73,6 +81,421 @@
     return (residual_grad, sum_down * inverse[None, :], sum_up * inverse[:, None])
 
 
+def nt_dot(a, b):
+    return lax.dot_general(a, b, (((1,), (1,)), ((), ())), preferred_element_type=F32)
+
+
+def tn_dot(a, b):
+    return lax.dot_general(a, b, (((0,), (0,)), ((), ())), preferred_element_type=F32)
+
+
+COST = pl.CostEstimate(flops=1000, bytes_accessed=1000, transcendentals=0)
+
+
+def params(mib=20):
+    return pltpu.CompilerParams(vmem_limit_bytes=mib * MIB)
+
+
+def member_mask(local, rows, shape, token_axis):
+    slot = lax.broadcasted_iota(jnp.int32, shape, token_axis) // rows
+    column_member = lax.broadcasted_iota(jnp.int32, shape, 1 - token_axis) // LOW_DIM
+    token_member = jnp.full(shape, -1, jnp.int32)
+    for s, e in enumerate(local):
+        token_member = jnp.where(slot == s, e, token_member)
+    return token_member == column_member
+
+
+HBM = pl.BlockSpec(memory_space=pltpu.HBM)
+VMEM = pl.BlockSpec(memory_space=pltpu.VMEM)
+SMEM = pl.BlockSpec(memory_space=pltpu.SMEM)
+ROWS = 128
+COLUMNS = 256
+
+
+class Copies:
+    def __init__(self, sems):
+        self.sems = sems
+        self.used = 0
+
+    def start(self, pairs):
+        group = []
+        for source, target in pairs:
+            copy = pltpu.make_async_copy(source, target, self.sems.at[self.used])
+            self.used += 1
+            copy.start()
+            group.append(copy)
+        return group
+
+
+def wait(group):
+    for copy in group:
+        copy.wait()
+
+
+def quarters(width):
+    step = width // 4
+    return [slice(q * step, (q + 1) * step) for q in range(4)]
+
+
+def norm_kernel(slot_ref, skip_ref, grad_ref, up_ref, inv_ref, mid_ref, turned_ref):
+    tokens, width = skip_ref.shape
+    low = up_ref.shape[0]
+    count = slot_ref.shape[0]
+    rows = tokens // count
+    for first in range(0, tokens, ROWS):
+        at = slice(first, first + ROWS)
+        local = [slot_ref[s] for s in range(at.start // rows, at.stop // rows)]
+        across = member_mask(local, rows, (ROWS, low), 0)
+        along = member_mask(local, rows, (low, ROWS), 1)
+        mid_ref[at, :] = jnp.where(across, nt_dot(grad_ref[at, :], up_ref[...]), 0.0).astype(BF16)
+        turned_ref[:, at] = jnp.where(along, nt_dot(up_ref[...], grad_ref[at, :]), 0.0).astype(BF16)
+        totals = [jnp.zeros((ROWS, 128), F32), jnp.zeros((ROWS, 128), F32)]
+        for j in range(width // 128):
+            wide = skip_ref[at, j * 128 : (j + 1) * 128].astype(F32)
+            totals[j % 2] += wide * wide
+        mean = jnp.sum(totals[0] + totals[1], axis=-1, keepdims=True) / width
+        inv_ref[at, :] = jnp.broadcast_to(lax.rsqrt(mean + epsilon), (ROWS, 128))
+
+
+def norm_call(slots_local, skip, grad, up):
+    tokens, width = skip.shape
+    low = up.shape[0]
+    return pl.pallas_call(
+        norm_kernel,
+        out_shape=(
+            pltpu.VMEM((tokens, 128), F32),
+            pltpu.VMEM((tokens, low), BF16),
+            pltpu.VMEM((low, tokens), BF16),
+        ),
+        in_specs=[SMEM, VMEM, VMEM, VMEM],
+        out_specs=[VMEM] * 3,
+        compiler_params=params(),
+        cost_estimate=COST,
+        name="norm",
+    )(slots_local, skip, grad, up)
+
+
+def terms_kernel(fsdp, slot_ref, place_ref, skip_ref, grad_ref, inv_ref, scale_ref, turned_ref, own_ref, *rest):
+    far_refs, rest = rest[: 2 * (fsdp - 1)], rest[2 * (fsdp - 1) :]
+    keep_out, send_out, term_ref, hidden_ref, down_ref, up_ref, sems = rest
+    outs = (keep_out, send_out)
+    core = place_ref[0]
+    tokens, width = skip_ref.shape
+    n = width // fsdp
+    half = n // 2
+    low = turned_ref.shape[0]
+    copies = Copies(sems)
+    inverse = inv_ref[...]
+    projected = jnp.zeros((tokens, low), F32)
+    stores = []
+    for r in range(fsdp):
+        start = lax.rem(place_ref[1] + r, fsdp) * n
+        if r == 0:
+            down = own_ref[...]
+        else:
+            for k in range(2):
+                down_ref[core ^ k] = far_refs[k * (fsdp - 1) + r - 1][...]
+            down = down_ref[...].reshape(n, low)
+        for j in range(n // 128):
+            cols = pl.ds(pl.multiple_of(start + j * 128, 128), 128)
+            hidden_ref[:, j * 128 : (j + 1) * 128] = (skip_ref[:, cols].astype(F32) * inverse * scale_ref[:, cols]).astype(BF16)
+        for h in range(2):
+            cols = slice(h * half, (h + 1) * half)
+            term_ref[core ^ h, r, :, :half] = jnp.dot(turned_ref[...], hidden_ref[:, cols], preferred_element_type=F32)
+        stores += copies.start([(term_ref.at[h, r, :, pl.ds(0, half)], outs[h].at[r, :, pl.ds(0, half)]) for h in range(2)])
+        projected += jnp.dot(hidden_ref[...], down, preferred_element_type=F32)
+    count = slot_ref.shape[0]
+    mask = member_mask([slot_ref[s] for s in range(count)], tokens // count, (tokens, low), 0)
+    projected = jnp.where(mask, projected, 0.0).astype(BF16)
+    up_ref[...] = tn_dot(projected, grad_ref[...])
+    for r in range(fsdp):
+        shard = lax.rem(place_ref[1] + r, fsdp)
+        for h in range(2):
+            at = pl.multiple_of((shard * 2 + (core ^ h)) * 128, 128)
+            term_ref[h, r, :, half:] = up_ref[:, pl.ds(at, 128)]
+    stores += copies.start([(term_ref.at[h, :, :, pl.ds(half, 128)], outs[h].at[:, :, pl.ds(half, 128)]) for h in range(2)])
+    wait(stores)
+
+
+def terms_call(slots_local, place, skip, inv, scales, turned, down, keep, other, grad):
+    tokens, width = skip.shape
+    low = turned.shape[0]
+    n = down.shape[0]
+    fsdp = width // n
+    both = n // 2 + 128
+    out = jax.ShapeDtypeStruct((fsdp, low, both), F32)
+    return pl.pallas_call(
+        functools.partial(terms_kernel, fsdp),
+        out_shape=(out, out),
+        in_specs=[SMEM, SMEM] + [VMEM] * (6 + 2 * (fsdp - 1)),
+        out_specs=[pl.BlockSpec(memory_space=pl.ANY)] * 2,
+        scratch_shapes=[
+            pltpu.VMEM((2, fsdp, low, both), F32),
+            pltpu.VMEM((tokens, n), BF16),
+            pltpu.VMEM((2, n // 2, low), BF16),
+            pltpu.VMEM((low, grad.shape[1]), F32),
+            pltpu.SemaphoreType.DMA((2 * fsdp + 2,)),
+        ],
+        compiler_params=params(),
+        cost_estimate=COST,
+        name="terms",
+    )(slots_local, place, skip, grad, inv, scales, turned, down, *keep, *other)
+
+
+def base_kernel(r, fsdp, spans, place_ref, grad_ref, mid_ref, skip_ref, scale_ref, *rest):
+    *ins, out_ref, sum_ref, both_ref, weight_ref, down_ref = rest
+    tokens, n = out_ref.shape
+    kdim = grad_ref.shape[1]
+    core = place_ref[0]
+    start = lax.rem(place_ref[1] + r, fsdp) * n
+    half = n // 2
+    if r:
+        for j in range(kdim // 128):
+            at = pl.multiple_of((place_ref[2] ^ j) * 128, 128)
+            both_ref[:, j * 128 : (j + 1) * 128] = grad_ref[:, pl.ds(at, 128)]
+        for k in range(2):
+            at = pl.multiple_of((core ^ k) * half, half)
+            down_ref[pl.ds(at, half), :] = ins[len(spans) + k][...]
+        for ref, (column, first, count, wide) in zip(ins, spans):
+            weight_ref[first : first + count, column : column + wide] = ref[...]
+    else:
+        both_ref[:, :kdim] = grad_ref[...]
+        down_ref[...] = ins[1][...]
+    both_ref[:, kdim:] = mid_ref[...]
+    total = jnp.zeros(sum_ref.shape, F32)
+    for i in range(n // COLUMNS):
+        rows = slice(i * COLUMNS, (i + 1) * COLUMNS)
+        weight = jnp.concatenate([(weight_ref if r else ins[0])[rows, :], down_ref[rows, :]], axis=-1)
+        scale = scale_ref[:, pl.ds(pl.multiple_of(start + i * COLUMNS, 128), COLUMNS)]
+        scaled = nt_dot(both_ref[...], weight) * scale
+        out_ref[:, rows] = scaled.astype(BF16)
+        for j in range(COLUMNS // 128):
+            cols = pl.ds(pl.multiple_of(start + i * COLUMNS + j * 128, 128), 128)
+            total += scaled[:, j * 128 : (j + 1) * 128] * skip_ref[:, cols].astype(F32)
+    sum_ref[...] = total
+
+
+def base_call(r, fsdp, place, grad, mid, skip, scales, spans, ins):
+    tokens, kdim = grad.shape
+    low = mid.shape[1]
+    n = skip.shape[1] // fsdp
+    return pl.pallas_call(
+        functools.partial(base_kernel, r, fsdp, spans),
+        out_shape=(pltpu.VMEM((tokens, n), BF16), pltpu.VMEM((tokens, 128), F32)),
+        in_specs=[SMEM] + [VMEM] * (4 + len(ins)),
+        out_specs=[VMEM] * 2,
+        scratch_shapes=[
+            pltpu.VMEM((tokens, kdim + low), BF16),
+            pltpu.VMEM((n, kdim) if r else (8, 128), BF16),
+            pltpu.VMEM((n, low), BF16),
+        ],
+        compiler_params=params(),
+        cost_estimate=COST,
+        name="base",
+    )(place, grad, mid, skip, scales, *ins)
+
+
+def residual_kernel(fsdp, slot_ref, place_ref, skip_ref, inv_ref, *rest):
+    base_refs, sum_refs, rest = rest[:fsdp], rest[fsdp : 2 * fsdp], rest[2 * fsdp :]
+    out_hbm, out_ref, keep_ref, pull_ref, sems = rest
+    tokens, width = skip_ref.shape
+    n = width // fsdp
+    rows = tokens // slot_ref.shape[0]
+    copies = Copies(sems)
+    inverse = inv_ref[...]
+    total = sum_refs[0][...]
+    for ref in sum_refs[1:]:
+        total = total + ref[...]
+    mean = jnp.sum(total, axis=-1, keepdims=True) * inverse / width
+    pull_ref[...] = mean * inverse
+    for s in range(slot_ref.shape[0]):
+        local = slot_ref[s]
+        alive = jnp.logical_and(local >= 0, local < place_ref[3])
+        at = slice(s * rows, (s + 1) * rows)
+        keep_ref[at, :] = inverse[at, :] * jnp.where(alive, 1.0, 0.0)
+    stores = []
+    for first in range(0, tokens, ROWS):
+
+        def some_rows(k, carry):
+            at = pl.ds(pl.multiple_of(first + k * 32, 32), 32)
+            for r in range(fsdp):
+                start = lax.rem(place_ref[1] + r, fsdp) * n
+                for j in range(n // 128):
+                    cols = pl.ds(pl.multiple_of(start + j * 128, 128), 128)
+                    wide = skip_ref[at, cols].astype(F32)
+                    scaled = base_refs[r][at, j * 128 : (j + 1) * 128].astype(F32)
+                    out_ref[at, cols] = ((scaled - wide * pull_ref[at, :]) * keep_ref[at, :]).astype(BF16)
+            return carry
+
+        lax.fori_loop(0, ROWS // 32, some_rows, 0)
+        at = pl.ds(first, ROWS)
+        stores += copies.start([(out_ref.at[at, q], out_hbm.at[at, q]) for q in quarters(width)])
+    wait(stores)
+
+
+def residual_call(slots_local, place, skip, inv, bases, sums):
+    tokens, width = skip.shape
+    fsdp = len(bases)
+    small = pltpu.VMEM((tokens, 128), F32)
+    return pl.pallas_call(
+        functools.partial(residual_kernel, fsdp),
+        out_shape=jax.ShapeDtypeStruct(skip.shape, BF16),
+        in_specs=[SMEM, SMEM] + [VMEM] * (2 + 2 * fsdp),
+        out_specs=HBM,
+        scratch_shapes=[
+            pltpu.VMEM((tokens, width), BF16),
+            small,
+            small,
+            pltpu.SemaphoreType.DMA((4 * (tokens // ROWS),)),
+        ],
+        compiler_params=params(),
+        cost_estimate=COST,
+        name="residual",
+    )(slots_local, place, skip, inv, *bases, *sums)
+
+
+def both_kernel(keep_ref, got_ref, own_ref, *sent_refs):
+    own_ref[...] = keep_ref[0] + got_ref[0]
+    for r, ref in enumerate(sent_refs, 1):
+        ref[...] = (keep_ref[r] + got_ref[r]).astype(BF16)
+
+
+def both_call(keep, got):
+    fsdp, low, both = keep.shape
+    sent = jax.ShapeDtypeStruct((low, both), BF16)
+    return pl.pallas_call(
+        both_kernel,
+        out_shape=(jax.ShapeDtypeStruct((low, both), F32),) + (sent,) * (fsdp - 1),
+        in_specs=[VMEM] * 2,
+        out_specs=[VMEM] * fsdp,
+        compiler_params=params(),
+        cost_estimate=COST,
+        name="both",
+    )(keep, got)
+
+
+def finish_kernel(slot_ref, own_ref, *rest):
+    *others, down_ref, up_ref = rest
+    total = own_ref[...]
+    for ref in others:
+        total = total + ref[...].astype(F32)
+    low = total.shape[0]
+    member = lax.broadcasted_iota(jnp.int32, (low, 128), 0) // LOW_DIM
+    counts = jnp.zeros((low, 128), F32)
+    for s in range(slot_ref.shape[0]):
+        counts += jnp.where(member == slot_ref[s], 1.0, 0.0)
+    inverse = 1.0 / (BLOCK * counts)
+    half = down_ref.shape[0]
+    for j in range(half // 128):
+        cols = slice(j * 128, (j + 1) * 128)
+        down_ref[cols, :] = (total[:, cols] * inverse).T
+    up_ref[...] = total[:, half:] * inverse
+
+
+def finish_call(slots_local, own, others):
+    low, both = own.shape
+    half = both - 128
+    return pl.pallas_call(
+        finish_kernel,
+        out_shape=(jax.ShapeDtypeStruct((half, low), F32), jax.ShapeDtypeStruct((low, 128), F32)),
+        in_specs=[SMEM] + [VMEM] * (1 + len(others)),
+        out_specs=[VMEM] * 2,
+        compiler_params=params(),
+        cost_estimate=COST,
+        name="finish",
+    )(slots_local, own, *others)
+
+
+SWAP = [(0, 1), (1, 0)]
+
+
+def after(value, *deps):
+    return lax.optimization_barrier((value, *deps))[0]
+
+
+def per_device_square(
+    fsdp,
+    skip_stream,
+    grad_stream,
+    weight,
+    down,
+    up,
+    scales,
+    assignee,
+):
+    z = lax.axis_index("fsdp")
+    c = lax.axis_index("dp")
+    m = lax.axis_index("member")
+    piece = c * 4 + lax.axis_index("parts") * 2 + m
+    half = down.shape[0] // 2
+    low = up.shape[0]
+    members = low // LOW_DIM
+    skip = skip_stream.reshape(-1, skip_stream.shape[2])
+    grad = grad_stream.reshape(-1, grad_stream.shape[2])
+    scale_row = scales[None, :]
+    local = assignee - m * members
+    place = jnp.stack([c, z, piece, jnp.int32(members)])
+
+    shift = lambda v, r: lax.ppermute(v, "fsdp", [(i, (i + r) % fsdp) for i in range(fsdp)])
+    over = lambda v, axis: lax.ppermute(v, axis, SWAP)
+    gate = lax.optimization_barrier
+    n = down.shape[0]
+    kdim = grad.shape[1]
+    narrow = lambda j: (j * 128, 0, n, 128)
+
+    def base(r, g, spans, ins):
+        return base_call(r, fsdp, place, g, mid, skip, scale_row, spans, ins)
+
+    def cores(values):
+        return tuple(over(v, "dp") for v in values)
+
+    def base_far(r, g, near, far, keep, other):
+        return base(r, g, tuple(narrow(j) for j in range(8)), (*near, *far, keep[r - 1], other[r - 1]))
+
+    unit = lax.dynamic_slice_in_dim(weight, piece * 128, 128, 1)
+    down_half = lax.dynamic_slice_in_dim(down, c * half, half, 0)
+    u1, u3 = shift(unit, -1), shift(unit, 1)
+    inv, mid, turned = norm_call(local, skip, grad, up)
+    u1, u3, unit, down_half, inv, mid, turned = gate((u1, u3, unit, down_half, inv, mid, turned))
+
+    keep = [shift(down_half, -r) for r in range(1, fsdp)]
+    u2 = shift(unit, -2)
+    x1, y1 = over(u1, "member"), over(u1, "parts")
+    x3, y3 = over(u3, "member"), over(u3, "parts")
+    base0 = base(0, grad, ((0, 0, n, kdim),), (weight, down))
+    u1, u3, x1, y1, x3, y3, keep, _ = gate((u1, u3, x1, y1, x3, y3, keep, base0[1]))
+
+    d1, d3 = over(x1, "parts"), over(y3, "member")
+    other = cores(keep)
+    far1, far3 = cores((u1, x1, y1)), cores((u3, x3, y3))
+    terms = terms_call(local, place, skip, inv, scale_row, turned, down, keep, other, grad)
+    d1, d3, far1, far3, terms, u2 = gate((d1, d3, far1, far3, terms, u2))
+
+    own, *sent = both_call(terms[0], over(terms[1], "dp"))
+    x2, y2 = over(u2, "member"), over(u2, "parts")
+    far1 += cores((d1,))
+    far3 += cores((d3,))
+    base1 = base_far(1, grad, (u1, x1, y1, d1), far1, keep, other)
+    base3 = base_far(3, grad, (u3, x3, y3, d3), far3, keep, other)
+    u2, x2, y2, sent, _ = gate((u2, x2, y2, sent, base1[1] + base3[1]))
+
+    others = [shift(v, r) for r, v in enumerate(sent, 1)]
+    rows = n // 2
+    d2 = (over(x2[:rows], "parts"), over(y2[rows:], "member"))
+    far2 = cores((u2, x2, y2))
+    d2, far2 = gate((d2, far2))
+
+    far_d2 = cores(d2)
+    spans = []
+    for j in range(8):
+        spans += [narrow(j)] if j % 4 < 3 else [(j * 128, at, rows, 128) for at in (0, rows)]
+    base2 = base(2, grad, tuple(spans), (u2, x2, y2, *d2, *far2, *far_d2, keep[1], other[1]))
+    grad_down, grad_up = finish_call(local, own, others)
+    bases, sums = zip(base0, base1, base2, base3)
+    residual = residual_call(local, place, skip, inv, bases, sums)
+    return residual.reshape(skip_stream.shape), grad_down, grad_up
+
+
 def solution(mesh):
     placed = (
         P(("parts", "member"), ("fsdp", "dp"), None),
@@ -83,8 +506,10 @@
         P(),
         P(("parts", "member")),
     )
+    sizes = dict(mesh.shape)
+    square = sizes["parts"] == 2 and sizes["member"] == 2 and sizes["dp"] == 2 and sizes["fsdp"] == 4
     return jax.shard_map(
-        per_device,
+        functools.partial(per_device_square, sizes["fsdp"]) if square else per_device_any,
         mesh=mesh,
         in_specs=placed,
         out_specs=(

time: 328 us -> 116 us (0.35)
  the two profiles are of different devices: /device:TPU:0 before, /device:TPU:9 now
where the time goes in v2:
time: 116 us
  waiting for transfers between devices  37 us (32%)
  Pallas kernels  32 us (28%)
  starting transfers between devices  31.3 us (27%)
  local copies, waits for them, and re-layouts  13.5 us (12%)
    ppermute x9, waiting for transfers between devices, per_device_square(): lax.ppermute(v, 'fsdp', [(i, (i + r) % fsdp) for i in range(fsdp)])  27.9 us
    ppermute x27, starting transfers between devices, per_device_square(): over = lambda v, axis: lax.ppermute(v, axis, SWAP)  23.2 us
    pallas_call x4, Pallas kernels, base_call(): pl.pallas_call(functools.partial(base_kernel, r, fsdp, spans), out_shape=...  15.1 us
    unnamed x24, local copies, waits for them, and re-layouts  11.7 us
    ppermute x27, waiting for transfers between devices, per_device_square(): over = lambda v, axis: lax.ppermute(v, axis, SWAP)  9.08 us
    ppermute x9, starting transfers between devices, per_device_square(): lax.ppermute(v, 'fsdp', [(i, (i + r) % fsdp) for i in range(fsdp)])  8.16 us
    pallas_call x1, Pallas kernels, terms_call(): pl.pallas_call(functools.partial(terms_kernel, fsdp), out_shape=(out, out...  7.84 us
    pallas_call x1, Pallas kernels, residual_call(): pl.pallas_call(functools.partial(residual_kernel, fsdp), out_shape=jax.Sh...  4.75 us
  transfers between devices with their start and end apart: 36, of which 11 were waited for; matrix products, arithmetic and copies ran while one was open for 1% of the time, Pallas kernels for 20%

profile of v2, /device:TPU:9, one launch (start us, length us, event | category | flops | bytes accessed | tf_op | source)
XLA Modules:
  0.0 115.6 jit_solution(14389384267232404446)
XLA Ops:
  0.6 1.7 %constant_dynamic-slice_fusion.1 = bf16[1280,128]{1,0:T(8,128)(2,1)} fusion(bf16[1280,1024]{1,0:T(8,128)(2,1)} %rest_0_.1, s32[]{:T(128)S(6)} %select_n.6), kind=kLoop, calls=%fused_computation.2 | loop fusion | bytes 655364 | tf_op jit(solution)/shard_map/dynamic_slice | solution.py:455
  2.4 1.3 %collective-permute-start.1 = (bf16[1280,128]{1,0:T(8,128)(2,1)}, bf16[1280,128]{1,0:T(8,128)(2,1)}, u32[]{:S(2)}, u32[]{:S(2)}) collective-permute-start(bf16[1280,128]{1,0:T(8,128)(2,1)} %constant_dynamic-slice_fusion.1), channel_id=1, source_target_pairs={{0,4},{4,8},{8,12},{12,0},{1,5},{5,9},{9,13},{13,1},{2,6},{6,10},{... | collective-permute-start | bytes 983048 | tf_op jit(solution)/shard_map/ppermute | solution.py:439
  3.7 0.2 collective-permute-start
  3.8 0.7 broadcast_subtract_fusion.slot_ref
  4.5 2.9 %copy-done = bf16[10,64,5120]{2,1,0:T(8,128)(2,1)S(1)} copy-done((bf16[10,64,5120]{2,1,0:T(8,128)(2,1)S(1)}, bf16[10,64,5120]{2,1,0:T(8,128)(2,1)}, u32[]{:S(2)}) %copy-start) | copy-done | bytes 6553624
  7.4 1.3 %copy-done.2 = bf16[10,64,1024]{2,1,0:T(8,128)(2,1)S(1)} copy-done((bf16[10,64,1024]{2,1,0:T(8,128)(2,1)S(1)}, bf16[10,64,1024]{2,1,0:T(8,128)(2,1)}, u32[]{:S(2)}) %copy-start.2) | copy-done | bytes 1310744
  8.7 0.9 copy-done.7
  9.6 2.5 %norm.1 = (f32[640,128]{1,0:T(8,128)S(1)}, bf16[640,128]{1,0:T(8,128)(2,1)S(1)}, bf16[128,640]{1,0:T(8,128)(2,1)S(1)}) custom-call(s32[10]{0:T(128)S(1)} %broadcast_subtract_fusion.slot_ref, bf16[640,5120]{1,0:T(8,128)(2,1)S(1)} %bitcast.7, bf16[640,1024]{1,0:T(8,128)(2,1)S(1)} %bitcast.16, bf16[128,1024]{1,0:T(8,128)(2,1)S(1)} %copy-done.7), custom_call_target="tpu_custom_call" | custom-call | flops 1000 | bytes 1000 | tf_op jit(solution)/shard_map/norm/pallas_call | solution.py:163
  12.1 0.7 copy-done.8
  12.8 7.3 %collective-permute-done.rest_0_ = bf16[1280,128]{1,0:T(8,128)(2,1)} collective-permute-done((bf16[1280,128]{1,0:T(8,128)(2,1)}, bf16[1280,128]{1,0:T(8,128)(2,1)}, u32[]{:S(2)}, u32[]{:S(2)}) %collective-permute-start) | collective-permute-done | bytes 327712 | tf_op jit(solution)/shard_map/ppermute | solution.py:439
  20.2 2.1 %collective-permute-start.7 = (bf16[640,128]{1,0:T(8,128)(2,1)S(1)}, bf16[640,128]{1,0:T(8,128)(2,1)S(1)}, u32[]{:S(2)}, u32[]{:S(2)}) collective-permute-start(bf16[640,128]{1,0:T(8,128)(2,1)S(1)} %constant_dynamic-slice_fusion), channel_id=1, source_target_pairs={{0,8},{4,12},{8,0},{12,4},{1,9},{5,13},{9,1},{13,5},{2,10},{6,14},... | collective-permute-start | bytes 491528 | tf_op jit(solution)/shard_map/ppermute | solution.py:439
  22.3 0.0 collective-permute-start.6
  22.3 1.2 %collective-permute-start.3 = (bf16[1280,128]{1,0:T(8,128)(2,1)}, bf16[1280,128]{1,0:T(8,128)(2,1)}, u32[]{:S(2)}, u32[]{:S(2)}) collective-permute-start(bf16[1280,128]{1,0:T(8,128)(2,1)} %collective-permute-done.rest_0_), channel_id=1, source_target_pairs={{0,16},{16,0},{1,17},{17,1},{2,18},{18,2},{3,19},{19,3},{4,20},{20... | collective-permute-start | bytes 983048 | tf_op jit(solution)/shard_map/ppermute | solution.py:440
  23.5 1.2 %collective-permute-start.2 = (bf16[1280,128]{1,0:T(8,128)(2,1)}, bf16[1280,128]{1,0:T(8,128)(2,1)}, u32[]{:S(2)}, u32[]{:S(2)}) collective-permute-start(bf16[1280,128]{1,0:T(8,128)(2,1)} %collective-permute-done.rest_0_), channel_id=1, source_target_pairs={{0,2},{2,0},{1,3},{3,1},{4,6},{6,4},{5,7},{7,5},{8,10},{10,8},{9,1... | collective-permute-start | bytes 983048 | tf_op jit(solution)/shard_map/ppermute | solution.py:440
  24.7 0.7 collective-permute-done.8.rest_2_.rest_8_
  25.5 1.2 %collective-permute-start.5 = (bf16[1280,128]{1,0:T(8,128)(2,1)}, bf16[1280,128]{1,0:T(8,128)(2,1)}, u32[]{:S(2)}, u32[]{:S(2)}) collective-permute-start(bf16[1280,128]{1,0:T(8,128)(2,1)} %collective-permute-done.1.rest_0_), channel_id=1, source_target_pairs={{0,16},{16,0},{1,17},{17,1},{2,18},{18,2},{3,19},{19,3},{4,20},{20... | collective-permute-start | bytes 983048 | tf_op jit(solution)/shard_map/ppermute | solution.py:440
  26.7 6.6 %collective-permute-done.7.rest_1_.rest_10_ = bf16[640,128]{1,0:T(8,128)(2,1)S(1)} collective-permute-done((bf16[640,128]{1,0:T(8,128)(2,1)S(1)}, bf16[640,128]{1,0:T(8,128)(2,1)S(1)}, u32[]{:S(2)}, u32[]{:S(2)}) %collective-permute-start.7) | collective-permute-done | bytes 163872 | tf_op jit(solution)/shard_map/ppermute | solution.py:439
  33.3 1.2 %collective-permute-start.4 = (bf16[1280,128]{1,0:T(8,128)(2,1)}, bf16[1280,128]{1,0:T(8,128)(2,1)}, u32[]{:S(2)}, u32[]{:S(2)}) collective-permute-start(bf16[1280,128]{1,0:T(8,128)(2,1)} %collective-permute-done.1.rest_0_), channel_id=1, source_target_pairs={{0,2},{2,0},{1,3},{3,1},{4,6},{6,4},{5,7},{7,5},{8,10},{10,8},{9,1... | collective-permute-start | bytes 983048 | tf_op jit(solution)/shard_map/ppermute | solution.py:440
  34.5 3.1 %collective-permute-done.6.rest_0_.rest_8_ = bf16[640,128]{1,0:T(8,128)(2,1)} collective-permute-done((bf16[640,128]{1,0:T(8,128)(2,1)S(1)}, bf16[640,128]{1,0:T(8,128)(2,1)}, u32[]{:S(2)}, u32[]{:S(2)}) %collective-permute-start.6) | collective-permute-done | bytes 163872 | tf_op jit(solution)/shard_map/ppermute | solution.py:439
  37.6 0.0 collective-permute-start.20
  37.6 0.1 pad_add_fusion.place_ref
  37.7 2.9 %copy-done.1 = bf16[10,64,5120]{2,1,0:T(8,128)(2,1)S(1)} copy-done((bf16[10,64,5120]{2,1,0:T(8,128)(2,1)S(1)}, bf16[10,64,5120]{2,1,0:T(8,128)(2,1)}, u32[]{:S(2)}) %copy-start.1) | copy-done | bytes 6553624
  40.6 1.3 %copy-done.3 = bf16[10,64,1024]{2,1,0:T(8,128)(2,1)S(1)} copy-done((bf16[10,64,1024]{2,1,0:T(8,128)(2,1)S(1)}, bf16[10,64,1024]{2,1,0:T(8,128)(2,1)}, u32[]{:S(2)}) %copy-start.3) | copy-done | bytes 1310744
  41.9 1.7 %copy-done.4 = bf16[1280,1024]{1,0:T(8,128)(2,1)S(1)} copy-done((bf16[1280,1024]{1,0:T(8,128)(2,1)S(1)}, bf16[1280,1024]{1,0:T(8,128)(2,1)}, u32[]{:S(2)}) %copy-start.4) | copy-done | bytes 2621464
  43.6 3.0 %base.4 = (bf16[640,1280]{1,0:T(8,128)(2,1)S(1)}, f32[640,128]{1,0:T(8,128)S(1)}) custom-call(s32[4]{0:T(128)S(1)} %pad_add_fusion.place_ref, bf16[640,1024]{1,0:T(8,128)(2,1)S(1)} %bitcast.17, bf16[640,128]{1,0:T(8,128)(2,1)S(1)} %get-tuple-element.64.mid_ref, bf16[640,5120]{1,0:T(8,128)(2,1)S(1)} %bitcast.8, f32[1,5120]{1,0:T(1,128)S(1)} %bitcast.22, ...), custom_call_target="tpu_custom_call" | custom-call | flops 1000 | bytes 1000 | tf_op jit(solution)/shard_map/base/pallas_call | solution.py:282
  46.7 2.4 %collective-permute-start.17 = (bf16[640,128]{1,0:T(8,128)(2,1)}, bf16[640,128]{1,0:T(8,128)(2,1)S(1)}, u32[]{:S(2)}, u32[]{:S(2)}) collective-permute-start(bf16[640,128]{1,0:T(8,128)(2,1)} %collective-permute-done.6.rest_0_.rest_8_), channel_id=1, source_target_pairs={{0,1},{1,0},{2,3},{3,2},{4,5},{5,4},{6,7},{7,6},{8,9},{9,8},{10,11... | collective-permute-start | bytes 491528 | tf_op jit(solution)/shard_map/ppermute | solution.py:440
  49.2 0.1 collective-permute-start.11
  49.2 0.4 collective-permute-start.13
  49.7 0.1 collective-permute-start.14
  49.8 2.6 %collective-permute-done.20.rest_0_ = bf16[1280,128]{1,0:T(8,128)(2,1)} collective-permute-done((bf16[1280,128]{1,0:T(8,128)(2,1)}, bf16[1280,128]{1,0:T(8,128)(2,1)}, u32[]{:S(2)}, u32[]{:S(2)}) %collective-permute-start.20) | collective-permute-done | bytes 327712 | tf_op jit(solution)/shard_map/ppermute | solution.py:439
  52.4 0.5 collective-permute-start.18
  52.9 0.0 collective-permute-start.19
  52.9 1.0 collective-permute-done.18.rest_4_.rest_11_
  53.9 0.4 collective-permute-start.12
  54.3 0.0 collective-permute-done.19.rest_5_.rest_9_
  54.3 1.2 %collective-permute-start.9 = (bf16[1280,128]{1,0:T(8,128)(2,1)}, bf16[1280,128]{1,0:T(8,128)(2,1)S(1)}, u32[]{:S(2)}, u32[]{:S(2)}) collective-permute-start(bf16[1280,128]{1,0:T(8,128)(2,1)} %collective-permute-done.2.rest_1_), channel_id=1, source_target_pairs={{0,16},{16,0},{1,17},{17,1},{2,18},{18,2},{3,19},{19,3},{4,20},{20... | collective-permute-start | bytes 983048 | tf_op jit(solution)/shard_map/ppermute | solution.py:440
  55.5 0.5 collective-permute-start.15
  56.0 0.1 collective-permute-start.16
  56.1 1.2 %collective-permute-start.10 = (bf16[1280,128]{1,0:T(8,128)(2,1)}, bf16[1280,128]{1,0:T(8,128)(2,1)S(1)}, u32[]{:S(2)}, u32[]{:S(2)}) collective-permute-start(bf16[1280,128]{1,0:T(8,128)(2,1)} %collective-permute-done.5.rest_2_), channel_id=1, source_target_pairs={{0,2},{2,0},{1,3},{3,1},{4,6},{6,4},{5,7},{7,5},{8,10},{10,8},{9,1... | collective-permute-start | bytes 983048 | tf_op jit(solution)/shard_map/ppermute | solution.py:440
  57.3 7.8 %terms.1 = (f32[4,128,768]{2,1,0:T(8,128)S(1)}, f32[4,128,768]{2,1,0:T(8,128)S(1)}) custom-call(s32[10]{0:T(128)S(1)} %broadcast_subtract_fusion.slot_ref, s32[4]{0:T(128)S(1)} %pad_add_fusion.place_ref, bf16[640,5120]{1,0:T(8,128)(2,1)S(1)} %bitcast.11, bf16[640,1024]{1,0:T(8,128)(2,1)S(1)} %bitcast.18, f32[640,128]{1,0:T(8,128)S(1)} %get-tuple-element.63.inv_ref, ...), custom_call_target="tpu_custom_call" | custom-call | flops 1000 | bytes 1000 | tf_op jit(solution)/shard_map/terms/pallas_call | solution.py:227
  65.2 1.3 %collective-permute-start.24 = (f32[4,128,768]{2,1,0:T(8,128)S(1)}, f32[4,128,768]{2,1,0:T(8,128)S(1)}, u32[]{:S(2)}, u32[]{:S(2)}) collective-permute-start(f32[4,128,768]{2,1,0:T(8,128)S(1)} %get-tuple-element.90), channel_id=1, source_target_pairs={{0,1},{1,0},{2,3},{3,2},{4,5},{5,4},{6,7},{7,6},{8,9},{9,8},{10,11... | collective-permute-start | bytes 4718600 | tf_op jit(solution)/shard_map/ppermute | solution.py:440
  66.5 0.2 collective-permute-start.23
  66.7 1.2 %collective-permute-start.22 = (bf16[1280,128]{1,0:T(8,128)(2,1)}, bf16[1280,128]{1,0:T(8,128)(2,1)S(1)}, u32[]{:S(2)}, u32[]{:S(2)}) collective-permute-start(bf16[1280,128]{1,0:T(8,128)(2,1)} %collective-permute-done.20.rest_0_), channel_id=1, source_target_pairs={{0,2},{2,0},{1,3},{3,1},{4,6},{6,4},{5,7},{7,5},{8,10},{10,8},{9,1... | collective-permute-start | bytes 983048 | tf_op jit(solution)/shard_map/ppermute | solution.py:440
  67.9 1.6 %collective-permute-done.24.got_ref = f32[4,128,768]{2,1,0:T(8,128)S(1)} collective-permute-done((f32[4,128,768]{2,1,0:T(8,128)S(1)}, f32[4,128,768]{2,1,0:T(8,128)S(1)}, u32[]{:S(2)}, u32[]{:S(2)}) %collective-permute-start.24) | collective-permute-done | bytes 1572896 | tf_op jit(solution)/shard_map/ppermute | solution.py:440
  69.5 0.3 both.1
  69.8 6.3 %collective-permute-done.23.rest_2_ = bf16[1280,128]{1,0:T(8,128)(2,1)S(1)} collective-permute-done((bf16[1280,128]{1,0:T(8,128)(2,1)}, bf16[1280,128]{1,0:T(8,128)(2,1)S(1)}, u32[]{:S(2)}, u32[]{:S(2)}) %collective-permute-start.23) | collective-permute-done | bytes 327712 | tf_op jit(solution)/shard_map/ppermute | solution.py:440
  76.0 1.2 %collective-permute-start.26 = (bf16[640,128]{1,0:T(8,128)(2,1)S(1)}, bf16[640,128]{1,0:T(8,128)(2,1)S(1)}, u32[]{:S(2)}, u32[]{:S(2)}) collective-permute-start(bf16[640,128]{1,0:T(8,128)(2,1)S(1)} %slice.7), channel_id=1, source_target_pairs={{0,2},{2,0},{1,3},{3,1},{4,6},{6,4},{5,7},{7,5},{8,10},{10,8},{9,1... | collective-permute-start | bytes 491528 | tf_op jit(solution)/shard_map/ppermute | solution.py:440
  77.3 1.2 %collective-permute-start.25 = (bf16[640,128]{1,0:T(8,128)(2,1)S(1)}, bf16[640,128]{1,0:T(8,128)(2,1)S(1)}, u32[]{:S(2)}, u32[]{:S(2)}) collective-permute-start(bf16[640,128]{1,0:T(8,128)(2,1)S(1)} %slice.6), channel_id=1, source_target_pairs={{0,16},{16,0},{1,17},{17,1},{2,18},{18,2},{3,19},{19,3},{4,20},{20... | collective-permute-start | bytes 491528 | tf_op jit(solution)/shard_map/ppermute | solution.py:440
  78.5 1.7 %collective-permute-start.27 = (bf16[1280,128]{1,0:T(8,128)(2,1)}, bf16[1280,128]{1,0:T(8,128)(2,1)S(1)}, u32[]{:S(2)}, u32[]{:S(2)}) collective-permute-start(bf16[1280,128]{1,0:T(8,128)(2,1)} %collective-permute-done.20.rest_0_), channel_id=1, source_target_pairs={{0,1},{1,0},{2,3},{3,2},{4,5},{5,4},{6,7},{7,6},{8,9},{9,8},{10,11... | collective-permute-start | bytes 983048 | tf_op jit(solution)/shard_map/ppermute | solution.py:440
  80.2 0.5 collective-permute-start.29
  80.7 0.1 collective-permute-done.26.rest_4_
  80.8 1.9 %collective-permute-start.21 = (bf16[1280,128]{1,0:T(8,128)(2,1)S(1)}, bf16[1280,128]{1,0:T(8,128)(2,1)S(1)}, u32[]{:S(2)}, u32[]{:S(2)}) collective-permute-start(bf16[1280,128]{1,0:T(8,128)(2,1)S(1)} %collective-permute-done.9.rest_3_), channel_id=1, source_target_pairs={{0,1},{1,0},{2,3},{3,2},{4,5},{5,4},{6,7},{7,6},{8,9},{9,8},{10,11... | collective-permute-start | bytes 983048 | tf_op jit(solution)/shard_map/ppermute | solution.py:440
  82.7 1.2 %collective-permute-start.32 = (bf16[1280,128]{1,0:T(8,128)(2,1)S(1)}, bf16[1280,128]{1,0:T(8,128)(2,1)S(1)}, u32[]{:S(2)}, u32[]{:S(2)}) collective-permute-start(bf16[1280,128]{1,0:T(8,128)(2,1)S(1)} %collective-permute-done.10.rest_3_), channel_id=1, source_target_pairs={{0,1},{1,0},{2,3},{3,2},{4,5},{5,4},{6,7},{7,6},{8,9},{9,8},{10,11... | collective-permute-start | bytes 983048 | tf_op jit(solution)/shard_map/ppermute | solution.py:440
  84.0 3.2 %collective-permute-start.34 = (bf16[128,768]{1,0:T(8,128)(2,1)S(1)}, bf16[128,768]{1,0:T(8,128)(2,1)S(1)}, u32[]{:S(2)}, u32[]{:S(2)}) collective-permute-start(bf16[128,768]{1,0:T(8,128)(2,1)S(1)} %get-tuple-element.113), channel_id=1, source_target_pairs={{0,8},{4,12},{8,0},{12,4},{1,9},{5,13},{9,1},{13,5},{2,10},{6,14},... | collective-permute-start | bytes 589832 | tf_op jit(solution)/shard_map/ppermute | solution.py:439
  87.1 1.4 %collective-permute-start.35 = (bf16[128,768]{1,0:T(8,128)(2,1)S(1)}, bf16[128,768]{1,0:T(8,128)(2,1)S(1)}, u32[]{:S(2)}, u32[]{:S(2)}) collective-permute-start(bf16[128,768]{1,0:T(8,128)(2,1)S(1)} %get-tuple-element.114), channel_id=1, source_target_pairs={{0,12},{4,0},{8,4},{12,8},{1,13},{5,1},{9,5},{13,9},{2,14},{6,2},{... | collective-permute-start | bytes 589832 | tf_op jit(solution)/shard_map/ppermute | solution.py:439
  88.5 0.8 collective-permute-start.30
  89.4 0.1 collective-permute-start.31
  89.5 4.1 %base.5 = (bf16[640,1280]{1,0:T(8,128)(2,1)S(1)}, f32[640,128]{1,0:T(8,128)S(1)}) custom-call(s32[4]{0:T(128)S(1)} %pad_add_fusion.place_ref, bf16[640,1024]{1,0:T(8,128)(2,1)S(1)} %bitcast.19, bf16[640,128]{1,0:T(8,128)(2,1)S(1)} %get-tuple-element.64.mid_ref, bf16[640,5120]{1,0:T(8,128)(2,1)S(1)} %bitcast.12, f32[1,5120]{1,0:T(1,128)S(1)} %bitcast.24, ...), custom_call_target="tpu_custom_call" | custom-call | flops 1000 | bytes 1000 | tf_op jit(solution)/shard_map/base/pallas_call | solution.py:282
  93.6 4.1 %base.7 = (bf16[640,1280]{1,0:T(8,128)(2,1)S(1)}, f32[640,128]{1,0:T(8,128)S(1)}) custom-call(s32[4]{0:T(128)S(1)} %pad_add_fusion.place_ref, bf16[640,1024]{1,0:T(8,128)(2,1)S(1)} %bitcast.20, bf16[640,128]{1,0:T(8,128)(2,1)S(1)} %get-tuple-element.64.mid_ref, bf16[640,5120]{1,0:T(8,128)(2,1)S(1)} %bitcast.13, f32[1,5120]{1,0:T(1,128)S(1)} %bitcast.25, ...), custom_call_target="tpu_custom_call" | custom-call | flops 1000 | bytes 1000 | tf_op jit(solution)/shard_map/base/pallas_call | solution.py:282
  97.7 3.5 %collective-permute-done.34.rest_1_ = bf16[128,768]{1,0:T(8,128)(2,1)S(1)} collective-permute-done((bf16[128,768]{1,0:T(8,128)(2,1)S(1)}, bf16[128,768]{1,0:T(8,128)(2,1)S(1)}, u32[]{:S(2)}, u32[]{:S(2)}) %collective-permute-start.34) | collective-permute-done | bytes 196640 | tf_op jit(solution)/shard_map/ppermute | solution.py:439
  101.1 4.1 %collective-permute-done.35.rest_2_ = bf16[128,768]{1,0:T(8,128)(2,1)S(1)} collective-permute-done((bf16[128,768]{1,0:T(8,128)(2,1)S(1)}, bf16[128,768]{1,0:T(8,128)(2,1)S(1)}, u32[]{:S(2)}, u32[]{:S(2)}) %collective-permute-start.35) | collective-permute-done | bytes 196640 | tf_op jit(solution)/shard_map/ppermute | solution.py:439
  105.2 1.5 %finish.1 = (f32[640,128]{1,0:T(8,128)}, f32[128,128]{1,0:T(8,128)}) custom-call(s32[10]{0:T(128)S(1)} %broadcast_subtract_fusion.slot_ref, f32[128,768]{1,0:T(8,128)S(1)} %get-tuple-element.111.own_ref, bf16[128,768]{1,0:T(8,128)(2,1)S(1)} %collective-permute-done.33.rest_0_, bf16[128,768]{1,0:T(8,128)(2,1)S(1)} %collective-permute-done.34.rest_1_, ...), custom_call_target="tpu_custom_call" | custom-call | flops 1000 | bytes 1000 | tf_op jit(solution)/shard_map/finish/pallas_call | solution.py:398
  106.8 3.9 %base.6 = (bf16[640,1280]{1,0:T(8,128)(2,1)S(1)}, f32[640,128]{1,0:T(8,128)S(1)}) custom-call(s32[4]{0:T(128)S(1)} %pad_add_fusion.place_ref, bf16[640,1024]{1,0:T(8,128)(2,1)S(1)} %bitcast.21, bf16[640,128]{1,0:T(8,128)(2,1)S(1)} %get-tuple-element.64.mid_ref, bf16[640,5120]{1,0:T(8,128)(2,1)S(1)} %bitcast.14, f32[1,5120]{1,0:T(1,128)S(1)} %bitcast.26, ...), custom_call_target="tpu_custom_call" | custom-call | flops 1000 | bytes 1000 | tf_op jit(solution)/shard_map/base/pallas_call | solution.py:282
  110.6 4.8 %residual.1 = bf16[640,5120]{1,0:T(8,128)(2,1)} custom-call(s32[10]{0:T(128)S(1)} %broadcast_subtract_fusion.slot_ref, s32[4]{0:T(128)S(1)} %pad_add_fusion.place_ref, bf16[640,5120]{1,0:T(8,128)(2,1)S(1)} %bitcast.15, f32[640,128]{1,0:T(8,128)S(1)} %get-tuple-element.63.inv_ref, bf16[640,1280]{1,0:T(8,128)(2,1)S(1)} %get-tuple-element.65.rest_0_, ...), custom_call_target="tpu_custom_call" | custom-call | flops 1000 | bytes 1000 | tf_op jit(solution)/shard_map/residual/pallas_call | solution.py:340
  (48 shorter events, 0.1 us)
Async XLA Ops:
  2.4 10.5 %collective-permute-start.1 = (bf16[1280,128]{1,0:T(8,128)(2,1)}, bf16[1280,128]{1,0:T(8,128)(2,1)}, u32[]{:S(2)}, u32[]{:S(2)}) collective-permute-start(bf16[1280,128]{1,0:T(8,128)(2,1)} %constant_dynamic-slice_fusion.1), channel_id=1, source_target_pairs={{0,4},{4,8},{8,12},{12,0},{1,5},{5,9},{9,13},{13,1},{2,6},{6,10},{... | collective-permute-start | bytes 983048 | tf_op jit(solution)/shard_map/ppermute | solution.py:439
  3.7 16.5 %collective-permute-start = (bf16[1280,128]{1,0:T(8,128)(2,1)}, bf16[1280,128]{1,0:T(8,128)(2,1)}, u32[]{:S(2)}, u32[]{:S(2)}) collective-permute-start(bf16[1280,128]{1,0:T(8,128)(2,1)} %constant_dynamic-slice_fusion.1), channel_id=1, source_target_pairs={{0,12},{4,0},{8,4},{12,8},{1,13},{5,1},{9,5},{13,9},{2,14},{6,2},{... | collective-permute-start | bytes 983048 | tf_op jit(solution)/shard_map/ppermute | solution.py:439
  4.5 2.9 %copy-start = (bf16[10,64,5120]{2,1,0:T(8,128)(2,1)S(1)}, bf16[10,64,5120]{2,1,0:T(8,128)(2,1)}, u32[]{:S(2)}) copy-start(bf16[10,64,5120]{2,1,0:T(8,128)(2,1)} %param.7) | copy-start | bytes 19660804
  7.4 1.3 %copy-start.2 = (bf16[10,64,1024]{2,1,0:T(8,128)(2,1)S(1)}, bf16[10,64,1024]{2,1,0:T(8,128)(2,1)}, u32[]{:S(2)}) copy-start(bf16[10,64,1024]{2,1,0:T(8,128)(2,1)} %param.8) | copy-start | bytes 3932164
  8.7 0.9 copy-start.7
  9.6 3.2 %copy-start.5 = (bf16[1280,128]{1,0:T(8,128)(2,1)S(1)}, bf16[1280,128]{1,0:T(8,128)(2,1)}, u32[]{:S(2)}) copy-start(bf16[1280,128]{1,0:T(8,128)(2,1)} %own_ref.1) | copy-start | bytes 983044
  9.6 28.1 %copy-start.6 = (f32[5120]{0:T(1024)S(1)}, f32[5120]{0:T(1024)}, u32[]{:S(2)}) copy-start(f32[5120]{0:T(1024)} %param.12) | copy-start | bytes 61444
  9.6 47.7 %slice-start = ((s8[6553600]{0:T(1024)(128)(4,1)}), s8[2359296]{0:T(1024)(128)(4,1)S(1)}, s32[]{:S(2)}) async-start(s8[6553600]{0:T(1024)(128)(4,1)} %bitcast.9), calls=%async_computation | async-start | bytes 4718592
  12.1 0.7 copy-start.8
  20.2 5.3 %collective-permute-start.8 = (bf16[640,128]{1,0:T(8,128)(2,1)S(1)}, bf16[640,128]{1,0:T(8,128)(2,1)S(1)}, u32[]{:S(2)}, u32[]{:S(2)}) collective-permute-start(bf16[640,128]{1,0:T(8,128)(2,1)S(1)} %constant_dynamic-slice_fusion), channel_id=1, source_target_pairs={{0,4},{4,8},{8,12},{12,0},{1,5},{5,9},{9,13},{13,1},{2,6},{6,10},{... | collective-permute-start | bytes 491528 | tf_op jit(solution)/shard_map/ppermute | solution.py:439
  20.2 13.1 %collective-permute-start.7 = (bf16[640,128]{1,0:T(8,128)(2,1)S(1)}, bf16[640,128]{1,0:T(8,128)(2,1)S(1)}, u32[]{:S(2)}, u32[]{:S(2)}) collective-permute-start(bf16[640,128]{1,0:T(8,128)(2,1)S(1)} %constant_dynamic-slice_fusion), channel_id=1, source_target_pairs={{0,8},{4,12},{8,0},{12,4},{1,9},{5,13},{9,1},{13,5},{2,10},{6,14},... | collective-permute-start | bytes 491528 | tf_op jit(solution)/shard_map/ppermute | solution.py:439
  22.3 15.3 %collective-permute-start.6 = (bf16[640,128]{1,0:T(8,128)(2,1)S(1)}, bf16[640,128]{1,0:T(8,128)(2,1)}, u32[]{:S(2)}, u32[]{:S(2)}) collective-permute-start(bf16[640,128]{1,0:T(8,128)(2,1)S(1)} %constant_dynamic-slice_fusion), channel_id=1, source_target_pairs={{0,12},{4,0},{8,4},{12,8},{1,13},{5,1},{9,5},{13,9},{2,14},{6,2},{... | collective-permute-start | bytes 491528 | tf_op jit(solution)/shard_map/ppermute | solution.py:439
  22.3 24.4 %collective-permute-start.3 = (bf16[1280,128]{1,0:T(8,128)(2,1)}, bf16[1280,128]{1,0:T(8,128)(2,1)}, u32[]{:S(2)}, u32[]{:S(2)}) collective-permute-start(bf16[1280,128]{1,0:T(8,128)(2,1)} %collective-permute-done.rest_0_), channel_id=1, source_target_pairs={{0,16},{16,0},{1,17},{17,1},{2,18},{18,2},{3,19},{19,3},{4,20},{20... | collective-permute-start | bytes 983048 | tf_op jit(solution)/shard_map/ppermute | solution.py:440
  23.5 23.2 %collective-permute-start.2 = (bf16[1280,128]{1,0:T(8,128)(2,1)}, bf16[1280,128]{1,0:T(8,128)(2,1)}, u32[]{:S(2)}, u32[]{:S(2)}) collective-permute-start(bf16[1280,128]{1,0:T(8,128)(2,1)} %collective-permute-done.rest_0_), channel_id=1, source_target_pairs={{0,2},{2,0},{1,3},{3,1},{4,6},{6,4},{5,7},{7,5},{8,10},{10,8},{9,1... | collective-permute-start | bytes 983048 | tf_op jit(solution)/shard_map/ppermute | solution.py:440
  25.5 21.2 %collective-permute-start.5 = (bf16[1280,128]{1,0:T(8,128)(2,1)}, bf16[1280,128]{1,0:T(8,128)(2,1)}, u32[]{:S(2)}, u32[]{:S(2)}) collective-permute-start(bf16[1280,128]{1,0:T(8,128)(2,1)} %collective-permute-done.1.rest_0_), channel_id=1, source_target_pairs={{0,16},{16,0},{1,17},{17,1},{2,18},{18,2},{3,19},{19,3},{4,20},{20... | collective-permute-start | bytes 983048 | tf_op jit(solution)/shard_map/ppermute | solution.py:440
  33.3 13.4 %collective-permute-start.4 = (bf16[1280,128]{1,0:T(8,128)(2,1)}, bf16[1280,128]{1,0:T(8,128)(2,1)}, u32[]{:S(2)}, u32[]{:S(2)}) collective-permute-start(bf16[1280,128]{1,0:T(8,128)(2,1)} %collective-permute-done.1.rest_0_), channel_id=1, source_target_pairs={{0,2},{2,0},{1,3},{3,1},{4,6},{6,4},{5,7},{7,5},{8,10},{10,8},{9,1... | collective-permute-start | bytes 983048 | tf_op jit(solution)/shard_map/ppermute | solution.py:440
  37.6 14.8 %collective-permute-start.20 = (bf16[1280,128]{1,0:T(8,128)(2,1)}, bf16[1280,128]{1,0:T(8,128)(2,1)}, u32[]{:S(2)}, u32[]{:S(2)}) collective-permute-start(bf16[1280,128]{1,0:T(8,128)(2,1)} %constant_dynamic-slice_fusion.1), channel_id=1, source_target_pairs={{0,8},{4,12},{8,0},{12,4},{1,9},{5,13},{9,1},{13,5},{2,10},{6,14},... | collective-permute-start | bytes 983048 | tf_op jit(solution)/shard_map/ppermute | solution.py:439
  37.7 2.9 %copy-start.1 = (bf16[10,64,5120]{2,1,0:T(8,128)(2,1)S(1)}, bf16[10,64,5120]{2,1,0:T(8,128)(2,1)}, u32[]{:S(2)}) copy-start(bf16[10,64,5120]{2,1,0:T(8,128)(2,1)} %param.7) | copy-start | bytes 19660804
  40.6 1.3 %copy-start.3 = (bf16[10,64,1024]{2,1,0:T(8,128)(2,1)S(1)}, bf16[10,64,1024]{2,1,0:T(8,128)(2,1)}, u32[]{:S(2)}) copy-start(bf16[10,64,1024]{2,1,0:T(8,128)(2,1)} %param.8) | copy-start | bytes 3932164
  41.9 1.7 %copy-start.4 = (bf16[1280,1024]{1,0:T(8,128)(2,1)S(1)}, bf16[1280,1024]{1,0:T(8,128)(2,1)}, u32[]{:S(2)}) copy-start(bf16[1280,1024]{1,0:T(8,128)(2,1)} %rest_0_.1) | copy-start | bytes 7864324
  43.6 13.7 %slice-start.1 = ((s8[6553600]{0:T(1024)(128)(4,1)}), s8[4194304]{0:T(1024)(128)(4,1)S(1)}, s32[]{:S(2)}) async-start(s8[6553600]{0:T(1024)(128)(4,1)} %bitcast.9), calls=%async_computation.1 | async-start | bytes 8388608
  43.6 13.7 %copy-start.9 = (bf16[128,640]{1,0:T(8,128)(2,1)S(1)}, bf16[128,640]{1,0:T(8,128)(2,1)}, u32[]{:S(2)}) copy-start(bf16[128,640]{1,0:T(8,128)(2,1)} %copy-done.8) | copy-start | bytes 491524
  46.7 6.2 %collective-permute-start.17 = (bf16[640,128]{1,0:T(8,128)(2,1)}, bf16[640,128]{1,0:T(8,128)(2,1)S(1)}, u32[]{:S(2)}, u32[]{:S(2)}) collective-permute-start(bf16[640,128]{1,0:T(8,128)(2,1)} %collective-permute-done.6.rest_0_.rest_8_), channel_id=1, source_target_pairs={{0,1},{1,0},{2,3},{3,2},{4,5},{5,4},{6,7},{7,6},{8,9},{9,8},{10,11... | collective-permute-start | bytes 491528 | tf_op jit(solution)/shard_map/ppermute | solution.py:440
  49.2 6.4 %collective-permute-start.11 = (bf16[1280,128]{1,0:T(8,128)(2,1)}, bf16[1280,128]{1,0:T(8,128)(2,1)S(1)}, u32[]{:S(2)}, u32[]{:S(2)}) collective-permute-start(bf16[1280,128]{1,0:T(8,128)(2,1)} %collective-permute-done.rest_0_), channel_id=1, source_target_pairs={{0,1},{1,0},{2,3},{3,2},{4,5},{5,4},{6,7},{7,6},{8,9},{9,8},{10,11... | collective-permute-start | bytes 983048 | tf_op jit(solution)/shard_map/ppermute | solution.py:440
  49.2 6.8 %collective-permute-start.13 = (bf16[1280,128]{1,0:T(8,128)(2,1)}, bf16[1280,128]{1,0:T(8,128)(2,1)S(1)}, u32[]{:S(2)}, u32[]{:S(2)}) collective-permute-start(bf16[1280,128]{1,0:T(8,128)(2,1)} %collective-permute-done.3.rest_2_), channel_id=1, source_target_pairs={{0,1},{1,0},{2,3},{3,2},{4,5},{5,4},{6,7},{7,6},{8,9},{9,8},{10,11... | collective-permute-start | bytes 983048 | tf_op jit(solution)/shard_map/ppermute | solution.py:440
  49.7 6.4 %collective-permute-start.14 = (bf16[1280,128]{1,0:T(8,128)(2,1)}, bf16[1280,128]{1,0:T(8,128)(2,1)S(1)}, u32[]{:S(2)}, u32[]{:S(2)}) collective-permute-start(bf16[1280,128]{1,0:T(8,128)(2,1)} %collective-permute-done.1.rest_0_), channel_id=1, source_target_pairs={{0,1},{1,0},{2,3},{3,2},{4,5},{5,4},{6,7},{7,6},{8,9},{9,8},{10,11... | collective-permute-start | bytes 983048 | tf_op jit(solution)/shard_map/ppermute | solution.py:440
  52.4 1.5 %collective-permute-start.18 = (bf16[640,128]{1,0:T(8,128)(2,1)S(1)}, bf16[640,128]{1,0:T(8,128)(2,1)S(1)}, u32[]{:S(2)}, u32[]{:S(2)}) collective-permute-start(bf16[640,128]{1,0:T(8,128)(2,1)S(1)} %collective-permute-done.7.rest_1_.rest_10_), channel_id=1, source_target_pairs={{0,1},{1,0},{2,3},{3,2},{4,5},{5,4},{6,7},{7,6},{8,9},{9,8},{10,11... | collective-permute-start | bytes 491528 | tf_op jit(solution)/shard_map/ppermute | solution.py:440
  52.9 1.4 %collective-permute-start.19 = (bf16[640,128]{1,0:T(8,128)(2,1)S(1)}, bf16[640,128]{1,0:T(8,128)(2,1)S(1)}, u32[]{:S(2)}, u32[]{:S(2)}) collective-permute-start(bf16[640,128]{1,0:T(8,128)(2,1)S(1)} %collective-permute-done.8.rest_2_.rest_8_), channel_id=1, source_target_pairs={{0,1},{1,0},{2,3},{3,2},{4,5},{5,4},{6,7},{7,6},{8,9},{9,8},{10,11... | collective-permute-start | bytes 491528 | tf_op jit(solution)/shard_map/ppermute | solution.py:440
  53.9 11.2 %collective-permute-start.12 = (bf16[1280,128]{1,0:T(8,128)(2,1)}, bf16[1280,128]{1,0:T(8,128)(2,1)S(1)}, u32[]{:S(2)}, u32[]{:S(2)}) collective-permute-start(bf16[1280,128]{1,0:T(8,128)(2,1)} %collective-permute-done.2.rest_1_), channel_id=1, source_target_pairs={{0,1},{1,0},{2,3},{3,2},{4,5},{5,4},{6,7},{7,6},{8,9},{9,8},{10,11... | collective-permute-start | bytes 983048 | tf_op jit(solution)/shard_map/ppermute | solution.py:440
  54.3 10.9 %collective-permute-start.9 = (bf16[1280,128]{1,0:T(8,128)(2,1)}, bf16[1280,128]{1,0:T(8,128)(2,1)S(1)}, u32[]{:S(2)}, u32[]{:S(2)}) collective-permute-start(bf16[1280,128]{1,0:T(8,128)(2,1)} %collective-permute-done.2.rest_1_), channel_id=1, source_target_pairs={{0,16},{16,0},{1,17},{17,1},{2,18},{18,2},{3,19},{19,3},{4,20},{20... | collective-permute-start | bytes 983048 | tf_op jit(solution)/shard_map/ppermute | solution.py:440
  55.5 9.6 %collective-permute-start.15 = (bf16[1280,128]{1,0:T(8,128)(2,1)}, bf16[1280,128]{1,0:T(8,128)(2,1)S(1)}, u32[]{:S(2)}, u32[]{:S(2)}) collective-permute-start(bf16[1280,128]{1,0:T(8,128)(2,1)} %collective-permute-done.4.rest_1_), channel_id=1, source_target_pairs={{0,1},{1,0},{2,3},{3,2},{4,5},{5,4},{6,7},{7,6},{8,9},{9,8},{10,11... | collective-permute-start | bytes 983048 | tf_op jit(solution)/shard_map/ppermute | solution.py:440
  56.0 9.1 %collective-permute-start.16 = (bf16[1280,128]{1,0:T(8,128)(2,1)}, bf16[1280,128]{1,0:T(8,128)(2,1)S(1)}, u32[]{:S(2)}, u32[]{:S(2)}) collective-permute-start(bf16[1280,128]{1,0:T(8,128)(2,1)} %collective-permute-done.5.rest_2_), channel_id=1, source_target_pairs={{0,1},{1,0},{2,3},{3,2},{4,5},{5,4},{6,7},{7,6},{8,9},{9,8},{10,11... | collective-permute-start | bytes 983048 | tf_op jit(solution)/shard_map/ppermute | solution.py:440
  56.1 9.1 %collective-permute-start.10 = (bf16[1280,128]{1,0:T(8,128)(2,1)}, bf16[1280,128]{1,0:T(8,128)(2,1)S(1)}, u32[]{:S(2)}, u32[]{:S(2)}) collective-permute-start(bf16[1280,128]{1,0:T(8,128)(2,1)} %collective-permute-done.5.rest_2_), channel_id=1, source_target_pairs={{0,2},{2,0},{1,3},{3,1},{4,6},{6,4},{5,7},{7,5},{8,10},{10,8},{9,1... | collective-permute-start | bytes 983048 | tf_op jit(solution)/shard_map/ppermute | solution.py:440
  65.2 4.3 %collective-permute-start.24 = (f32[4,128,768]{2,1,0:T(8,128)S(1)}, f32[4,128,768]{2,1,0:T(8,128)S(1)}, u32[]{:S(2)}, u32[]{:S(2)}) collective-permute-start(f32[4,128,768]{2,1,0:T(8,128)S(1)} %get-tuple-element.90), channel_id=1, source_target_pairs={{0,1},{1,0},{2,3},{3,2},{4,5},{5,4},{6,7},{7,6},{8,9},{9,8},{10,11... | collective-permute-start | bytes 4718600 | tf_op jit(solution)/shard_map/ppermute | solution.py:440
  66.5 9.6 %collective-permute-start.23 = (bf16[1280,128]{1,0:T(8,128)(2,1)}, bf16[1280,128]{1,0:T(8,128)(2,1)S(1)}, u32[]{:S(2)}, u32[]{:S(2)}) collective-permute-start(bf16[1280,128]{1,0:T(8,128)(2,1)} %collective-permute-done.20.rest_0_), channel_id=1, source_target_pairs={{0,16},{16,0},{1,17},{17,1},{2,18},{18,2},{3,19},{19,3},{4,20},{20... | collective-permute-start | bytes 983048 | tf_op jit(solution)/shard_map/ppermute | solution.py:440
  66.7 9.3 %collective-permute-start.22 = (bf16[1280,128]{1,0:T(8,128)(2,1)}, bf16[1280,128]{1,0:T(8,128)(2,1)S(1)}, u32[]{:S(2)}, u32[]{:S(2)}) collective-permute-start(bf16[1280,128]{1,0:T(8,128)(2,1)} %collective-permute-done.20.rest_0_), channel_id=1, source_target_pairs={{0,2},{2,0},{1,3},{3,1},{4,6},{6,4},{5,7},{7,5},{8,10},{10,8},{9,1... | collective-permute-start | bytes 983048 | tf_op jit(solution)/shard_map/ppermute | solution.py:440
  76.0 4.7 %collective-permute-start.26 = (bf16[640,128]{1,0:T(8,128)(2,1)S(1)}, bf16[640,128]{1,0:T(8,128)(2,1)S(1)}, u32[]{:S(2)}, u32[]{:S(2)}) collective-permute-start(bf16[640,128]{1,0:T(8,128)(2,1)S(1)} %slice.7), channel_id=1, source_target_pairs={{0,2},{2,0},{1,3},{3,1},{4,6},{6,4},{5,7},{7,5},{8,10},{10,8},{9,1... | collective-permute-start | bytes 491528 | tf_op jit(solution)/shard_map/ppermute | solution.py:440
  77.3 5.4 %collective-permute-start.25 = (bf16[640,128]{1,0:T(8,128)(2,1)S(1)}, bf16[640,128]{1,0:T(8,128)(2,1)S(1)}, u32[]{:S(2)}, u32[]{:S(2)}) collective-permute-start(bf16[640,128]{1,0:T(8,128)(2,1)S(1)} %slice.6), channel_id=1, source_target_pairs={{0,16},{16,0},{1,17},{17,1},{2,18},{18,2},{3,19},{19,3},{4,20},{20... | collective-permute-start | bytes 491528 | tf_op jit(solution)/shard_map/ppermute | solution.py:440
  78.5 5.5 %collective-permute-start.27 = (bf16[1280,128]{1,0:T(8,128)(2,1)}, bf16[1280,128]{1,0:T(8,128)(2,1)S(1)}, u32[]{:S(2)}, u32[]{:S(2)}) collective-permute-start(bf16[1280,128]{1,0:T(8,128)(2,1)} %collective-permute-done.20.rest_0_), channel_id=1, source_target_pairs={{0,1},{1,0},{2,3},{3,2},{4,5},{5,4},{6,7},{7,6},{8,9},{9,8},{10,11... | collective-permute-start | bytes 983048 | tf_op jit(solution)/shard_map/ppermute | solution.py:440
  80.2 3.8 %collective-permute-start.28 = (bf16[1280,128]{1,0:T(8,128)(2,1)S(1)}, bf16[1280,128]{1,0:T(8,128)(2,1)S(1)}, u32[]{:S(2)}, u32[]{:S(2)}) collective-permute-start(bf16[1280,128]{1,0:T(8,128)(2,1)S(1)} %collective-permute-done.22.rest_1_), channel_id=1, source_target_pairs={{0,1},{1,0},{2,3},{3,2},{4,5},{5,4},{6,7},{7,6},{8,9},{9,8},{10,11... | collective-permute-start | bytes 983048 | tf_op jit(solution)/shard_map/ppermute | solution.py:440
  80.2 7.0 %collective-permute-start.29 = (bf16[1280,128]{1,0:T(8,128)(2,1)S(1)}, bf16[1280,128]{1,0:T(8,128)(2,1)S(1)}, u32[]{:S(2)}, u32[]{:S(2)}) collective-permute-start(bf16[1280,128]{1,0:T(8,128)(2,1)S(1)} %collective-permute-done.23.rest_2_), channel_id=1, source_target_pairs={{0,1},{1,0},{2,3},{3,2},{4,5},{5,4},{6,7},{7,6},{8,9},{9,8},{10,11... | collective-permute-start | bytes 983048 | tf_op jit(solution)/shard_map/ppermute | solution.py:440
  80.8 7.8 %collective-permute-start.21 = (bf16[1280,128]{1,0:T(8,128)(2,1)S(1)}, bf16[1280,128]{1,0:T(8,128)(2,1)S(1)}, u32[]{:S(2)}, u32[]{:S(2)}) collective-permute-start(bf16[1280,128]{1,0:T(8,128)(2,1)S(1)} %collective-permute-done.9.rest_3_), channel_id=1, source_target_pairs={{0,1},{1,0},{2,3},{3,2},{4,5},{5,4},{6,7},{7,6},{8,9},{9,8},{10,11... | collective-permute-start | bytes 983048 | tf_op jit(solution)/shard_map/ppermute | solution.py:440
  82.7 6.7 %collective-permute-start.32 = (bf16[1280,128]{1,0:T(8,128)(2,1)S(1)}, bf16[1280,128]{1,0:T(8,128)(2,1)S(1)}, u32[]{:S(2)}, u32[]{:S(2)}) collective-permute-start(bf16[1280,128]{1,0:T(8,128)(2,1)S(1)} %collective-permute-done.10.rest_3_), channel_id=1, source_target_pairs={{0,1},{1,0},{2,3},{3,2},{4,5},{5,4},{6,7},{7,6},{8,9},{9,8},{10,11... | collective-permute-start | bytes 983048 | tf_op jit(solution)/shard_map/ppermute | solution.py:440
  84.0 13.7 %collective-permute-start.33 = (bf16[128,768]{1,0:T(8,128)(2,1)S(1)}, bf16[128,768]{1,0:T(8,128)(2,1)S(1)}, u32[]{:S(2)}, u32[]{:S(2)}) collective-permute-start(bf16[128,768]{1,0:T(8,128)(2,1)S(1)} %get-tuple-element.112), channel_id=1, source_target_pairs={{0,4},{4,8},{8,12},{12,0},{1,5},{5,9},{9,13},{13,1},{2,6},{6,10},{... | collective-permute-start | bytes 589832 | tf_op jit(solution)/shard_map/ppermute | solution.py:439
  84.0 17.2 %collective-permute-start.34 = (bf16[128,768]{1,0:T(8,128)(2,1)S(1)}, bf16[128,768]{1,0:T(8,128)(2,1)S(1)}, u32[]{:S(2)}, u32[]{:S(2)}) collective-permute-start(bf16[128,768]{1,0:T(8,128)(2,1)S(1)} %get-tuple-element.113), channel_id=1, source_target_pairs={{0,8},{4,12},{8,0},{12,4},{1,9},{5,13},{9,1},{13,5},{2,10},{6,14},... | collective-permute-start | bytes 589832 | tf_op jit(solution)/shard_map/ppermute | solution.py:439
  87.1 18.1 %collective-permute-start.35 = (bf16[128,768]{1,0:T(8,128)(2,1)S(1)}, bf16[128,768]{1,0:T(8,128)(2,1)S(1)}, u32[]{:S(2)}, u32[]{:S(2)}) collective-permute-start(bf16[128,768]{1,0:T(8,128)(2,1)S(1)} %get-tuple-element.114), channel_id=1, source_target_pairs={{0,12},{4,0},{8,4},{12,8},{1,13},{5,1},{9,5},{13,9},{2,14},{6,2},{... | collective-permute-start | bytes 589832 | tf_op jit(solution)/shard_map/ppermute | solution.py:439
  88.5 18.2 %collective-permute-start.30 = (bf16[640,128]{1,0:T(8,128)(2,1)S(1)}, bf16[640,128]{1,0:T(8,128)(2,1)S(1)}, u32[]{:S(2)}, u32[]{:S(2)}) collective-permute-start(bf16[640,128]{1,0:T(8,128)(2,1)S(1)} %collective-permute-done.25.rest_3_), channel_id=1, source_target_pairs={{0,1},{1,0},{2,3},{3,2},{4,5},{5,4},{6,7},{7,6},{8,9},{9,8},{10,11... | collective-permute-start | bytes 491528 | tf_op jit(solution)/shard_map/ppermute | solution.py:440
  89.4 17.4 %collective-permute-start.31 = (bf16[640,128]{1,0:T(8,128)(2,1)S(1)}, bf16[640,128]{1,0:T(8,128)(2,1)S(1)}, u32[]{:S(2)}, u32[]{:S(2)}) collective-permute-start(bf16[640,128]{1,0:T(8,128)(2,1)S(1)} %collective-permute-done.26.rest_4_), channel_id=1, source_target_pairs={{0,1},{1,0},{2,3},{3,2},{4,5},{5,4},{6,7},{7,6},{8,9},{9,8},{10,11... | collective-permute-start | bytes 491528 | tf_op jit(solution)/shard_map/ppermute | solution.py:440

commit v3 on v2

--- a/solution.py
+++ b/solution.py
@@ -89,7 +89,8 @@
     return lax.dot_general(a, b, (((0,), (0,)), ((), ())), preferred_element_type=F32)
 
 
-COST = pl.CostEstimate(flops=1000, bytes_accessed=1000, transcendentals=0)
+def cost(microseconds):
+    return pl.CostEstimate(flops=int(microseconds * 1000), bytes_accessed=1000, transcendentals=0)
 
 
 def params(mib=20):
@@ -170,7 +171,7 @@
         in_specs=[SMEM, VMEM, VMEM, VMEM],
         out_specs=[VMEM] * 3,
         compiler_params=params(),
-        cost_estimate=COST,
+        cost_estimate=cost(2.5),
         name="norm",
     )(slots_local, skip, grad, up)
 
@@ -198,12 +199,12 @@
             down = down_ref[...].reshape(n, low)
         for j in range(n // 128):
             cols = pl.ds(pl.multiple_of(start + j * 128, 128), 128)
-            hidden_ref[:, j * 128 : (j + 1) * 128] = (skip_ref[:, cols].astype(F32) * inverse * scale_ref[:, cols]).astype(BF16)
+            hidden_ref[r, :, j * 128 : (j + 1) * 128] = (skip_ref[:, cols].astype(F32) * inverse * scale_ref[:, cols]).astype(BF16)
+        term = jnp.dot(turned_ref[...], hidden_ref[r], preferred_element_type=F32)
         for h in range(2):
-            cols = slice(h * half, (h + 1) * half)
-            term_ref[core ^ h, r, :, :half] = jnp.dot(turned_ref[...], hidden_ref[:, cols], preferred_element_type=F32)
+            term_ref[core ^ h, r, :, :half] = term[:, h * half : (h + 1) * half]
         stores += copies.start([(term_ref.at[h, r, :, pl.ds(0, half)], outs[h].at[r, :, pl.ds(0, half)]) for h in range(2)])
-        projected += jnp.dot(hidden_ref[...], down, preferred_element_type=F32)
+        projected += jnp.dot(hidden_ref[r], down, preferred_element_type=F32)
     count = slot_ref.shape[0]
     mask = member_mask([slot_ref[s] for s in range(count)], tokens // count, (tokens, low), 0)
     projected = jnp.where(mask, projected, 0.0).astype(BF16)
@@ -231,19 +232,19 @@
         out_specs=[pl.BlockSpec(memory_space=pl.ANY)] * 2,
         scratch_shapes=[
             pltpu.VMEM((2, fsdp, low, both), F32),
-            pltpu.VMEM((tokens, n), BF16),
+            pltpu.VMEM((fsdp, tokens, n), BF16),
             pltpu.VMEM((2, n // 2, low), BF16),
             pltpu.VMEM((low, grad.shape[1]), F32),
             pltpu.SemaphoreType.DMA((2 * fsdp + 2,)),
         ],
         compiler_params=params(),
-        cost_estimate=COST,
+        cost_estimate=cost(7.5),
         name="terms",
     )(slots_local, place, skip, grad, inv, scales, turned, down, *keep, *other)
 
 
 def base_kernel(r, fsdp, spans, place_ref, grad_ref, mid_ref, skip_ref, scale_ref, *rest):
-    *ins, out_ref, sum_ref, both_ref, weight_ref, down_ref = rest
+    *ins, out_ref, sum_ref, both_ref, down_ref = rest
     tokens, n = out_ref.shape
     kdim = grad_ref.shape[1]
     core = place_ref[0]
@@ -256,8 +257,6 @@
         for k in range(2):
             at = pl.multiple_of((core ^ k) * half, half)
             down_ref[pl.ds(at, half), :] = ins[len(spans) + k][...]
-        for ref, (column, first, count, wide) in zip(ins, spans):
-            weight_ref[first : first + count, column : column + wide] = ref[...]
     else:
         both_ref[:, :kdim] = grad_ref[...]
         down_ref[...] = ins[1][...]
@@ -265,7 +264,8 @@
     total = jnp.zeros(sum_ref.shape, F32)
     for i in range(n // COLUMNS):
         rows = slice(i * COLUMNS, (i + 1) * COLUMNS)
-        weight = jnp.concatenate([(weight_ref if r else ins[0])[rows, :], down_ref[rows, :]], axis=-1)
+        parts = [ref[first + rows.start : first + rows.stop, :] for ref, first in zip(ins, spans)]
+        weight = jnp.concatenate(parts + [down_ref[rows, :]], axis=-1)
         scale = scale_ref[:, pl.ds(pl.multiple_of(start + i * COLUMNS, 128), COLUMNS)]
         scaled = nt_dot(both_ref[...], weight) * scale
         out_ref[:, rows] = scaled.astype(BF16)
@@ -286,18 +286,17 @@
         out_specs=[VMEM] * 2,
         scratch_shapes=[
             pltpu.VMEM((tokens, kdim + low), BF16),
-            pltpu.VMEM((n, kdim) if r else (8, 128), BF16),
             pltpu.VMEM((n, low), BF16),
         ],
         compiler_params=params(),
-        cost_estimate=COST,
+        cost_estimate=cost(3.4),
         name="base",
     )(place, grad, mid, skip, scales, *ins)
 
 
 def residual_kernel(fsdp, slot_ref, place_ref, skip_ref, inv_ref, *rest):
     base_refs, sum_refs, rest = rest[:fsdp], rest[fsdp : 2 * fsdp], rest[2 * fsdp :]
-    out_hbm, out_ref, keep_ref, pull_ref, sems = rest
+    out_hbm, done_ref, out_ref, keep_ref, pull_ref, sems = rest
     tokens, width = skip_ref.shape
     n = width // fsdp
     rows = tokens // slot_ref.shape[0]
@@ -313,6 +312,7 @@
         alive = jnp.logical_and(local >= 0, local < place_ref[3])
         at = slice(s * rows, (s + 1) * rows)
         keep_ref[at, :] = inverse[at, :] * jnp.where(alive, 1.0, 0.0)
+    done_ref[...] = jnp.zeros_like(done_ref)
     stores = []
     for first in range(0, tokens, ROWS):
 
@@ -339,9 +339,9 @@
     small = pltpu.VMEM((tokens, 128), F32)
     return pl.pallas_call(
         functools.partial(residual_kernel, fsdp),
-        out_shape=jax.ShapeDtypeStruct(skip.shape, BF16),
+        out_shape=(jax.ShapeDtypeStruct(skip.shape, BF16), jax.ShapeDtypeStruct((8, 128), F32)),
         in_specs=[SMEM, SMEM] + [VMEM] * (2 + 2 * fsdp),
-        out_specs=HBM,
+        out_specs=(HBM, VMEM),
         scratch_shapes=[
             pltpu.VMEM((tokens, width), BF16),
             small,
@@ -349,36 +349,49 @@
             pltpu.SemaphoreType.DMA((4 * (tokens // ROWS),)),
         ],
         compiler_params=params(),
-        cost_estimate=COST,
+        cost_estimate=cost(4.7),
         name="residual",
     )(slots_local, place, skip, inv, *bases, *sums)
 
 
-def both_kernel(keep_ref, got_ref, own_ref, *sent_refs):
-    own_ref[...] = keep_ref[0] + got_ref[0]
-    for r, ref in enumerate(sent_refs, 1):
-        ref[...] = (keep_ref[r] + got_ref[r]).astype(BF16)
+def both_kernel(keep_ref, got_ref, *out_refs):
+    for r, ref in enumerate(out_refs):
+        ref[...] = (keep_ref[r] + got_ref[r]).astype(ref.dtype)
 
 
 def both_call(keep, got):
     fsdp, low, both = keep.shape
-    sent = jax.ShapeDtypeStruct((low, both), BF16)
+    held = jax.ShapeDtypeStruct((low, both), F32)
     return pl.pallas_call(
         both_kernel,
-        out_shape=(jax.ShapeDtypeStruct((low, both), F32),) + (sent,) * (fsdp - 1),
+        out_shape=(held,) * (fsdp - 1) + (jax.ShapeDtypeStruct((low, both), BF16),),
         in_specs=[VMEM] * 2,
         out_specs=[VMEM] * fsdp,
         compiler_params=params(),
-        cost_estimate=COST,
+        cost_estimate=cost(0.4),
         name="both",
     )(keep, got)
 
 
-def finish_kernel(slot_ref, own_ref, *rest):
-    *others, down_ref, up_ref = rest
-    total = own_ref[...]
-    for ref in others:
-        total = total + ref[...].astype(F32)
+def add_kernel(held_ref, got_ref, out_ref):
+    out_ref[...] = (held_ref[...] + got_ref[...].astype(F32)).astype(BF16)
+
+
+def add_call(held, got):
+    return pl.pallas_call(
+        add_kernel,
+        out_shape=jax.ShapeDtypeStruct(held.shape, BF16),
+        in_specs=[VMEM] * 2,
+        out_specs=VMEM,
+        compiler_params=params(),
+        cost_estimate=cost(0.4),
+        name="add",
+    )(held, got)
+
+
+def finish_kernel(slot_ref, held_ref, got_ref, done_ref, down_ref, up_ref):
+    del done_ref
+    total = held_ref[...] + got_ref[...].astype(F32)
     low = total.shape[0]
     member = lax.broadcasted_iota(jnp.int32, (low, 128), 0) // LOW_DIM
     counts = jnp.zeros((low, 128), F32)
@@ -392,18 +405,18 @@
     up_ref[...] = total[:, half:] * inverse
 
 
-def finish_call(slots_local, own, others):
-    low, both = own.shape
+def finish_call(slots_local, held, got, done):
+    low, both = held.shape
     half = both - 128
     return pl.pallas_call(
         finish_kernel,
         out_shape=(jax.ShapeDtypeStruct((half, low), F32), jax.ShapeDtypeStruct((low, 128), F32)),
-        in_specs=[SMEM] + [VMEM] * (1 + len(others)),
+        in_specs=[SMEM] + [VMEM] * 3,
         out_specs=[VMEM] * 2,
         compiler_params=params(),
-        cost_estimate=COST,
+        cost_estimate=cost(1.5),
         name="finish",
-    )(slots_local, own, *others)
+    )(slots_local, held, got, done)
 
 
 SWAP = [(0, 1), (1, 0)]
@@ -440,59 +453,49 @@
     over = lambda v, axis: lax.ppermute(v, axis, SWAP)
     gate = lax.optimization_barrier
     n = down.shape[0]
-    kdim = grad.shape[1]
-    narrow = lambda j: (j * 128, 0, n, 128)
-
-    def base(r, g, spans, ins):
-        return base_call(r, fsdp, place, g, mid, skip, scale_row, spans, ins)
-
-    def cores(values):
-        return tuple(over(v, "dp") for v in values)
-
-    def base_far(r, g, near, far, keep, other):
-        return base(r, g, tuple(narrow(j) for j in range(8)), (*near, *far, keep[r - 1], other[r - 1]))
+
+    def base(r, spans, ins):
+        return base_call(r, fsdp, place, grad, mid, skip, scale_row, spans, ins)
+
+    def core(value):
+        return over(value, "dp")
 
     unit = lax.dynamic_slice_in_dim(weight, piece * 128, 128, 1)
     down_half = lax.dynamic_slice_in_dim(down, c * half, half, 0)
     u1, u3 = shift(unit, -1), shift(unit, 1)
     inv, mid, turned = norm_call(local, skip, grad, up)
-    u1, u3, unit, down_half, inv, mid, turned = gate((u1, u3, unit, down_half, inv, mid, turned))
-
+    u1, u3, down_half, inv, mid, turned = gate((u1, u3, down_half, inv, mid, turned))
+
+    u = jnp.concatenate([u1, u3], axis=0)
+    x, y = over(u, "member"), over(u, "parts")
     keep = [shift(down_half, -r) for r in range(1, fsdp)]
-    u2 = shift(unit, -2)
-    x1, y1 = over(u1, "member"), over(u1, "parts")
-    x3, y3 = over(u3, "member"), over(u3, "parts")
-    base0 = base(0, grad, ((0, 0, n, kdim),), (weight, down))
-    u1, u3, x1, y1, x3, y3, keep, _ = gate((u1, u3, x1, y1, x3, y3, keep, base0[1]))
-
-    d1, d3 = over(x1, "parts"), over(y3, "member")
-    other = cores(keep)
-    far1, far3 = cores((u1, x1, y1)), cores((u3, x3, y3))
+    base0, sum0 = base(0, (0,), (weight, down))
+    u, x, y, keep, u3, sum0 = gate((u, x, y, keep, u3, sum0))
+
+    u2 = shift(u3, 1)
+    d1, d3 = over(x[:n], "parts"), over(y[n:], "member")
+    other = [core(v) for v in keep]
+    far_u, far_x, far_y = core(u), core(x), core(y)
+    turned, far_u, far_x, far_y = gate((turned, far_u, far_x, far_y))
     terms = terms_call(local, place, skip, inv, scale_row, turned, down, keep, other, grad)
-    d1, d3, far1, far3, terms, u2 = gate((d1, d3, far1, far3, terms, u2))
-
-    own, *sent = both_call(terms[0], over(terms[1], "dp"))
+    d1, d3, far_u, far_x, far_y, terms, u2 = gate((d1, d3, far_u, far_x, far_y, terms, u2))
+
+    *held, sent = both_call(terms[0], core(terms[1]))
     x2, y2 = over(u2, "member"), over(u2, "parts")
-    far1 += cores((d1,))
-    far3 += cores((d3,))
-    base1 = base_far(1, grad, (u1, x1, y1, d1), far1, keep, other)
-    base3 = base_far(3, grad, (u3, x3, y3, d3), far3, keep, other)
-    u2, x2, y2, sent, _ = gate((u2, x2, y2, sent, base1[1] + base3[1]))
-
-    others = [shift(v, r) for r, v in enumerate(sent, 1)]
-    rows = n // 2
-    d2 = (over(x2[:rows], "parts"), over(y2[rows:], "member"))
-    far2 = cores((u2, x2, y2))
-    d2, far2 = gate((d2, far2))
-
-    far_d2 = cores(d2)
-    spans = []
-    for j in range(8):
-        spans += [narrow(j)] if j % 4 < 3 else [(j * 128, at, rows, 128) for at in (0, rows)]
-    base2 = base(2, grad, tuple(spans), (u2, x2, y2, *d2, *far2, *far_d2, keep[1], other[1]))
-    grad_down, grad_up = finish_call(local, own, others)
-    bases, sums = zip(base0, base1, base2, base3)
-    residual = residual_call(local, place, skip, inv, bases, sums)
+    got = shift(sent, 1)
+    base1, sum1 = base(1, (0, 0, 0, 0) * 2, (u, x, y, d1, far_u, far_x, far_y, core(d1), keep[0], other[0]))
+    u2, x2, y2, d3, got, sum1 = gate((u2, x2, y2, d3, got, sum1))
+
+    d2 = over(x2, "parts")
+    got = shift(add_call(held[2], got), 1)
+    far2 = [core(v) for v in (u2, x2, y2)]
+    base3, sum3 = base(3, (n, n, n, 0) * 2, (u, x, y, d3, far_u, far_x, far_y, core(d3), keep[2], other[2]))
+    d2, far2, sum3 = gate((d2, far2, sum3))
+
+    got = shift(add_call(held[1], got), 1)
+    base2, sum2 = base(2, (0,) * 8, (u2, x2, y2, d2, *far2, core(d2), keep[1], other[1]))
+    residual, done = residual_call(local, place, skip, inv, (base0, base1, base2, base3), (sum0, sum1, sum2, sum3))
+    grad_down, grad_up = finish_call(local, held[0], got, done)
     return residual.reshape(skip_stream.shape), grad_down, grad_up
 
 

time: 116 us -> 96 us (0.83)
  the two profiles are of different devices: /device:TPU:9 before, /device:TPU:0 now
where the time goes in v3:
time: 96 us; the launch traced here: 95.5 us
  Pallas kernels  31.7 us (33%)
  starting transfers between devices  25 us (26%)
  waiting for transfers between devices  19.4 us (20%)
  local copies, waits for them, and re-layouts  17.8 us (19%)
    pallas_call x4, Pallas kernels, base_call(): pl.pallas_call(functools.partial(base_kernel, r, fsdp, spans), out_shape=...  14.5 us
    unnamed x33, local copies, waits for them, and re-layouts  13.5 us
    ppermute x9, starting transfers between devices, per_device_square(): lax.ppermute(v, 'fsdp', [(i, (i + r) % fsdp) for i in range(fsdp)])  13.3 us
    ppermute x20, waiting for transfers between devices, per_device_square(): over = lambda v, axis: lax.ppermute(v, axis, SWAP)  12.3 us
    ppermute x20, starting transfers between devices, per_device_square(): over = lambda v, axis: lax.ppermute(v, axis, SWAP)  11.8 us
    pallas_call x1, Pallas kernels, terms_call(): pl.pallas_call(functools.partial(terms_kernel, fsdp), out_shape=(out, out...  8.12 us
    ppermute x9, waiting for transfers between devices, per_device_square(): lax.ppermute(v, 'fsdp', [(i, (i + r) % fsdp) for i in range(fsdp)])  7.04 us
    pallas_call x1, Pallas kernels, residual_call(): pl.pallas_call(functools.partial(residual_kernel, fsdp), out_shape=(jax.S...  4.78 us
  transfers between devices with their start and end apart: 29, of which 13 were waited for; matrix products, arithmetic and copies ran while one was open for 3% of the time, Pallas kernels for 32%

profile of v3, /device:TPU:0, one launch (start us, length us, event | category | flops | bytes accessed | tf_op | source)
XLA Modules:
  0.0 95.5 jit_solution(14073382480015857817)
XLA Ops:
  0.6 1.7 %constant_dynamic-slice_fusion.1 = bf16[1280,128]{1,0:T(8,128)(2,1)} fusion(bf16[1280,1024]{1,0:T(8,128)(2,1)} %rest_0_.1, s32[]{:T(128)S(6)} %select_n.6), kind=kLoop, calls=%fused_computation.4 | loop fusion | bytes 655364 | tf_op jit(solution)/shard_map/dynamic_slice | solution.py:463
  2.4 3.0 %collective-permute-start.1 = (bf16[1280,128]{1,0:T(8,128)(2,1)}, bf16[1280,128]{1,0:T(8,128)(2,1)S(1)}, u32[]{:S(2)}, u32[]{:S(2)}) collective-permute-start(bf16[1280,128]{1,0:T(8,128)(2,1)} %constant_dynamic-slice_fusion.1), channel_id=1, source_target_pairs={{0,4},{4,8},{8,12},{12,0},{1,5},{5,9},{9,13},{13,1},{2,6},{6,10},{... | collective-permute-start | bytes 983048 | tf_op jit(solution)/shard_map/ppermute | solution.py:452
  5.4 2.0 %collective-permute-start = (bf16[1280,128]{1,0:T(8,128)(2,1)}, bf16[1280,128]{1,0:T(8,128)(2,1)}, u32[]{:S(2)}, u32[]{:S(2)}) collective-permute-start(bf16[1280,128]{1,0:T(8,128)(2,1)} %constant_dynamic-slice_fusion.1), channel_id=1, source_target_pairs={{0,12},{4,0},{8,4},{12,8},{1,13},{5,1},{9,5},{13,9},{2,14},{6,2},{... | collective-permute-start | bytes 983048 | tf_op jit(solution)/shard_map/ppermute | solution.py:452
  7.4 0.7 broadcast_subtract_fusion.slot_ref
  8.1 2.9 %copy-done = bf16[10,64,5120]{2,1,0:T(8,128)(2,1)S(1)} copy-done((bf16[10,64,5120]{2,1,0:T(8,128)(2,1)S(1)}, bf16[10,64,5120]{2,1,0:T(8,128)(2,1)}, u32[]{:S(2)}) %copy-start) | copy-done | bytes 6553624
  10.9 1.3 %copy-done.2 = bf16[10,64,1024]{2,1,0:T(8,128)(2,1)S(1)} copy-done((bf16[10,64,1024]{2,1,0:T(8,128)(2,1)S(1)}, bf16[10,64,1024]{2,1,0:T(8,128)(2,1)}, u32[]{:S(2)}) %copy-start.2) | copy-done | bytes 1310744
  12.3 0.9 copy-done.9
  13.2 2.5 %norm.1 = (f32[640,128]{1,0:T(8,128)S(1)}, bf16[640,128]{1,0:T(8,128)(2,1)S(1)}, bf16[128,640]{1,0:T(8,128)(2,1)S(1)}) custom-call(s32[10]{0:T(128)S(1)} %broadcast_subtract_fusion.slot_ref, bf16[640,5120]{1,0:T(8,128)(2,1)S(1)} %bitcast.7, bf16[640,1024]{1,0:T(8,128)(2,1)S(1)} %bitcast.16, bf16[128,1024]{1,0:T(8,128)(2,1)S(1)} %copy-done.9), custom_call_target="tpu_custom_call" | custom-call | flops 2500 | bytes 1000 | tf_op jit(solution)/shard_map/norm/pallas_call | solution.py:164
  15.7 0.7 copy-done.6
  16.5 0.7 constant_dynamic-slice_fusion
  17.2 4.7 %collective-permute-done = bf16[1280,128]{1,0:T(8,128)(2,1)} collective-permute-done((bf16[1280,128]{1,0:T(8,128)(2,1)}, bf16[1280,128]{1,0:T(8,128)(2,1)}, u32[]{:S(2)}, u32[]{:S(2)}) %collective-permute-start) | collective-permute-done | bytes 327712 | tf_op jit(solution)/shard_map/ppermute | solution.py:452
  21.9 1.7 %constant_dynamic-update-slice_fusion.1 = bf16[2560,128]{1,0:T(8,128)(2,1)} fusion(bf16[1280,128]{1,0:T(8,128)(2,1)} %collective-permute-done), kind=kLoop, calls=%fused_computation.1 | loop fusion | bytes 655360
  23.6 0.7 constant_dynamic-update-slice_fusion.rest_0_
  24.4 1.5 %collective-permute-start.3 = (bf16[2560,128]{1,0:T(8,128)(2,1)}, bf16[2560,128]{1,0:T(8,128)(2,1)S(1)}, u32[]{:S(2)}, u32[]{:S(2)}) collective-permute-start(bf16[2560,128]{1,0:T(8,128)(2,1)} %constant_dynamic-update-slice_fusion.rest_0_), channel_id=1, source_target_pairs={{0,16},{16,0},{1,17},{17,1},{2,18},{18,2},{3,19},{19,3},{4,20},{20... | collective-permute-start | bytes 1966088 | tf_op jit(solution)/shard_map/ppermute | solution.py:453
  25.9 1.5 %collective-permute-start.2 = (bf16[2560,128]{1,0:T(8,128)(2,1)}, bf16[2560,128]{1,0:T(8,128)(2,1)}, u32[]{:S(2)}, u32[]{:S(2)}) collective-permute-start(bf16[2560,128]{1,0:T(8,128)(2,1)} %constant_dynamic-update-slice_fusion.rest_0_), channel_id=1, source_target_pairs={{0,2},{2,0},{1,3},{3,1},{4,6},{6,4},{5,7},{7,5},{8,10},{10,8},{9,1... | collective-permute-start | bytes 1966088 | tf_op jit(solution)/shard_map/ppermute | solution.py:453
  27.4 1.1 %collective-permute-start.6 = (bf16[640,128]{1,0:T(8,128)(2,1)}, bf16[640,128]{1,0:T(8,128)(2,1)}, u32[]{:S(2)}, u32[]{:S(2)}) collective-permute-start(bf16[640,128]{1,0:T(8,128)(2,1)} %constant_dynamic-slice_fusion), channel_id=1, source_target_pairs={{0,4},{4,8},{8,12},{12,0},{1,5},{5,9},{9,13},{13,1},{2,6},{6,10},{... | collective-permute-start | bytes 491528 | tf_op jit(solution)/shard_map/ppermute | solution.py:452
  28.5 1.8 %collective-permute-start.5 = (bf16[640,128]{1,0:T(8,128)(2,1)}, bf16[640,128]{1,0:T(8,128)(2,1)}, u32[]{:S(2)}, u32[]{:S(2)}) collective-permute-start(bf16[640,128]{1,0:T(8,128)(2,1)} %constant_dynamic-slice_fusion), channel_id=1, source_target_pairs={{0,8},{4,12},{8,0},{12,4},{1,9},{5,13},{9,1},{13,5},{2,10},{6,14},... | collective-permute-start | bytes 491528 | tf_op jit(solution)/shard_map/ppermute | solution.py:452
  30.3 1.3 %collective-permute-start.4 = (bf16[640,128]{1,0:T(8,128)(2,1)}, bf16[640,128]{1,0:T(8,128)(2,1)}, u32[]{:S(2)}, u32[]{:S(2)}) collective-permute-start(bf16[640,128]{1,0:T(8,128)(2,1)} %constant_dynamic-slice_fusion), channel_id=1, source_target_pairs={{0,12},{4,0},{8,4},{12,8},{1,13},{5,1},{9,5},{13,9},{2,14},{6,2},{... | collective-permute-start | bytes 491528 | tf_op jit(solution)/shard_map/ppermute | solution.py:452
  31.6 0.1 pad_add_fusion.place_ref
  31.7 2.9 %copy-done.1 = bf16[10,64,5120]{2,1,0:T(8,128)(2,1)S(1)} copy-done((bf16[10,64,5120]{2,1,0:T(8,128)(2,1)S(1)}, bf16[10,64,5120]{2,1,0:T(8,128)(2,1)}, u32[]{:S(2)}) %copy-start.1) | copy-done | bytes 6553624
  34.6 1.3 %copy-done.3 = bf16[10,64,1024]{2,1,0:T(8,128)(2,1)S(1)} copy-done((bf16[10,64,1024]{2,1,0:T(8,128)(2,1)S(1)}, bf16[10,64,1024]{2,1,0:T(8,128)(2,1)}, u32[]{:S(2)}) %copy-start.3) | copy-done | bytes 1310744
  35.9 1.7 %copy-done.4 = bf16[1280,1024]{1,0:T(8,128)(2,1)S(1)} copy-done((bf16[1280,1024]{1,0:T(8,128)(2,1)S(1)}, bf16[1280,1024]{1,0:T(8,128)(2,1)}, u32[]{:S(2)}) %copy-start.4) | copy-done | bytes 2621464
  37.6 3.0 %base.4 = (bf16[640,1280]{1,0:T(8,128)(2,1)S(1)}, f32[640,128]{1,0:T(8,128)S(1)}) custom-call(s32[4]{0:T(128)S(1)} %pad_add_fusion.place_ref, bf16[640,1024]{1,0:T(8,128)(2,1)S(1)} %bitcast.17, bf16[640,128]{1,0:T(8,128)(2,1)S(1)} %get-tuple-element.65.mid_ref, bf16[640,5120]{1,0:T(8,128)(2,1)S(1)} %bitcast.8, f32[1,5120]{1,0:T(1,128)S(1)} %bitcast.22, ...), custom_call_target="tpu_custom_call" | custom-call | flops 3400 | bytes 1000 | tf_op jit(solution)/shard_map/base/pallas_call | solution.py:282
  40.7 0.0 collective-permute-done.6.rest_2_.rest_8_
  40.7 0.9 collective-permute-done.5.rest_1_.rest_8_
  41.6 0.0 collective-permute-done.3.rest_2_
  41.6 0.4 collective-permute-done.2.rest_1_
  42.0 0.5 collective-permute-start.10
  42.5 0.0 collective-permute-start.11
  42.5 0.5 collective-permute-start.12
  43.0 1.0 %slice.6 = bf16[1280,128]{1,0:T(8,128)(2,1)S(1)} slice(bf16[2560,128]{1,0:T(8,128)(2,1)} %collective-permute-done.2.rest_1_), slice={[0:1280], [0:128]} | slice | bytes 655360 | tf_op jit(solution)/shard_map/slice | solution.py:476
  44.0 1.6 %collective-permute-start.8 = (bf16[1280,128]{1,0:T(8,128)(2,1)S(1)}, bf16[1280,128]{1,0:T(8,128)(2,1)S(1)}, u32[]{:S(2)}, u32[]{:S(2)}) collective-permute-start(bf16[1280,128]{1,0:T(8,128)(2,1)S(1)} %slice.7), channel_id=1, source_target_pairs={{0,2},{2,0},{1,3},{3,1},{4,6},{6,4},{5,7},{7,5},{8,10},{10,8},{9,1... | collective-permute-start | bytes 983048 | tf_op jit(solution)/shard_map/ppermute | solution.py:453
  45.6 0.8 collective-permute-done.12.rest_3_.rest_9_
  46.4 0.5 collective-permute-start.7
  46.9 3.6 %collective-permute-start.15 = (bf16[1280,128]{1,0:T(8,128)(2,1)S(1)}, bf16[1280,128]{1,0:T(8,128)(2,1)S(1)}, u32[]{:S(2)}, u32[]{:S(2)}) collective-permute-start(bf16[1280,128]{1,0:T(8,128)(2,1)S(1)} %copy-done.13), channel_id=1, source_target_pairs={{0,4},{4,8},{8,12},{12,0},{1,5},{5,9},{9,13},{13,1},{2,6},{6,10},{... | collective-permute-start | bytes 983048 | tf_op jit(solution)/shard_map/ppermute | solution.py:452
  50.5 0.5 collective-permute-start.14
  51.0 1.1 %collective-permute-done.13.rest_4_.rest_9_ = bf16[640,128]{1,0:T(8,128)(2,1)S(1)} collective-permute-done((bf16[640,128]{1,0:T(8,128)(2,1)}, bf16[640,128]{1,0:T(8,128)(2,1)S(1)}, u32[]{:S(2)}, u32[]{:S(2)}) %collective-permute-start.13) | collective-permute-done | bytes 163872 | tf_op jit(solution)/shard_map/ppermute | solution.py:453
  52.1 0.2 collective-permute-done.14.rest_5_.rest_9_
  52.4 8.1 %terms.1 = (f32[4,128,768]{2,1,0:T(8,128)S(1)}, f32[4,128,768]{2,1,0:T(8,128)S(1)}) custom-call(s32[10]{0:T(128)S(1)} %broadcast_subtract_fusion.slot_ref, s32[4]{0:T(128)S(1)} %pad_add_fusion.place_ref, bf16[640,5120]{1,0:T(8,128)(2,1)S(1)} %bitcast.11, bf16[640,1024]{1,0:T(8,128)(2,1)S(1)} %bitcast.18, f32[640,128]{1,0:T(8,128)S(1)} %copy-done.7, ...), custom_call_target="tpu_custom_call" | custom-call | flops 7500 | bytes 1000 | tf_op jit(solution)/shard_map/terms/pallas_call | solution.py:228
  60.5 0.0 collective-permute-done.7.rest_3_
  60.5 0.3 collective-permute-start.19
  60.9 0.2 collective-permute-start.16
  61.1 1.5 %collective-permute-start.18 = (bf16[1280,128]{1,0:T(8,128)(2,1)S(1)}, bf16[1280,128]{1,0:T(8,128)(2,1)S(1)}, u32[]{:S(2)}, u32[]{:S(2)}) collective-permute-start(bf16[1280,128]{1,0:T(8,128)(2,1)S(1)} %collective-permute-done.15.rest_0_), channel_id=1, source_target_pairs={{0,16},{16,0},{1,17},{17,1},{2,18},{18,2},{3,19},{19,3},{4,20},{20... | collective-permute-start | bytes 983048 | tf_op jit(solution)/shard_map/ppermute | solution.py:453
  62.6 0.5 collective-permute-start.17
  63.1 0.8 collective-permute-done.19.got_ref
  64.0 0.2 both.1
  64.2 0.3 collective-permute-start.20
  64.5 3.9 %base.5 = (bf16[640,1280]{1,0:T(8,128)(2,1)S(1)}, f32[640,128]{1,0:T(8,128)S(1)}) custom-call(s32[4]{0:T(128)S(1)} %pad_add_fusion.place_ref, bf16[640,1024]{1,0:T(8,128)(2,1)S(1)} %bitcast.19, bf16[640,128]{1,0:T(8,128)(2,1)S(1)} %get-tuple-element.65.mid_ref, bf16[640,5120]{1,0:T(8,128)(2,1)S(1)} %bitcast.12, f32[1,5120]{1,0:T(1,128)S(1)} %bitcast.24, ...), custom_call_target="tpu_custom_call" | custom-call | flops 3400 | bytes 1000 | tf_op jit(solution)/shard_map/base/pallas_call | solution.py:282
  68.5 2.5 %collective-permute-done.18.rest_2_ = bf16[1280,128]{1,0:T(8,128)(2,1)S(1)} collective-permute-done((bf16[1280,128]{1,0:T(8,128)(2,1)S(1)}, bf16[1280,128]{1,0:T(8,128)(2,1)S(1)}, u32[]{:S(2)}, u32[]{:S(2)}) %collective-permute-start.18) | collective-permute-done | bytes 327712 | tf_op jit(solution)/shard_map/ppermute | solution.py:453
  71.0 1.2 %collective-permute-done.17.rest_1_ = bf16[1280,128]{1,0:T(8,128)(2,1)S(1)} collective-permute-done((bf16[1280,128]{1,0:T(8,128)(2,1)S(1)}, bf16[1280,128]{1,0:T(8,128)(2,1)S(1)}, u32[]{:S(2)}, u32[]{:S(2)}) %collective-permute-start.17) | collective-permute-done | bytes 327712 | tf_op jit(solution)/shard_map/ppermute | solution.py:453
  72.2 1.1 %collective-permute-done.20.got_ref = bf16[128,768]{1,0:T(8,128)(2,1)S(1)} collective-permute-done((bf16[128,768]{1,0:T(8,128)(2,1)S(1)}, bf16[128,768]{1,0:T(8,128)(2,1)S(1)}, u32[]{:S(2)}, u32[]{:S(2)}) %collective-permute-start.20) | collective-permute-done | bytes 196640 | tf_op jit(solution)/shard_map/ppermute | solution.py:452
  73.3 0.5 collective-permute-start.22
  73.8 0.0 collective-permute-start.24
  73.9 0.5 collective-permute-start.23
  74.4 1.5 %collective-permute-start.21 = (bf16[1280,128]{1,0:T(8,128)(2,1)S(1)}, bf16[1280,128]{1,0:T(8,128)(2,1)S(1)}, u32[]{:S(2)}, u32[]{:S(2)}) collective-permute-start(bf16[1280,128]{1,0:T(8,128)(2,1)S(1)} %collective-permute-done.17.rest_1_), channel_id=1, source_target_pairs={{0,16},{16,0},{1,17},{17,1},{2,18},{18,2},{3,19},{19,3},{4,20},{20... | collective-permute-start | bytes 983048 | tf_op jit(solution)/shard_map/ppermute | solution.py:453
  75.9 0.1 collective-permute-start.27
  76.0 3.9 %base.6 = (bf16[640,1280]{1,0:T(8,128)(2,1)S(1)}, f32[640,128]{1,0:T(8,128)S(1)}) custom-call(s32[4]{0:T(128)S(1)} %pad_add_fusion.place_ref, bf16[640,1024]{1,0:T(8,128)(2,1)S(1)} %bitcast.20, bf16[640,128]{1,0:T(8,128)(2,1)S(1)} %get-tuple-element.65.mid_ref, bf16[640,5120]{1,0:T(8,128)(2,1)S(1)} %bitcast.13, f32[1,5120]{1,0:T(1,128)S(1)} %bitcast.25, ...), custom_call_target="tpu_custom_call" | custom-call | flops 3400 | bytes 1000 | tf_op jit(solution)/shard_map/base/pallas_call | solution.py:282
  80.0 4.0 %collective-permute-done.21.rest_3_ = bf16[1280,128]{1,0:T(8,128)(2,1)S(1)} collective-permute-done((bf16[1280,128]{1,0:T(8,128)(2,1)S(1)}, bf16[1280,128]{1,0:T(8,128)(2,1)S(1)}, u32[]{:S(2)}, u32[]{:S(2)}) %collective-permute-start.21) | collective-permute-done | bytes 327712 | tf_op jit(solution)/shard_map/ppermute | solution.py:453
  84.0 0.3 collective-permute-done.27.got_ref
  84.4 0.1 collective-permute-start.28
  84.4 1.2 %collective-permute-done.26.rest_7_ = bf16[1280,128]{1,0:T(8,128)(2,1)S(1)} collective-permute-done((bf16[1280,128]{1,0:T(8,128)(2,1)S(1)}, bf16[1280,128]{1,0:T(8,128)(2,1)S(1)}, u32[]{:S(2)}, u32[]{:S(2)}) %collective-permute-start.26) | collective-permute-done | bytes 327712 | tf_op jit(solution)/shard_map/ppermute | solution.py:453
  85.6 3.6 %base.7 = (bf16[640,1280]{1,0:T(8,128)(2,1)S(1)}, f32[640,128]{1,0:T(8,128)S(1)}) custom-call(s32[4]{0:T(128)S(1)} %pad_add_fusion.place_ref, bf16[640,1024]{1,0:T(8,128)(2,1)S(1)} %bitcast.21, bf16[640,128]{1,0:T(8,128)(2,1)S(1)} %get-tuple-element.65.mid_ref, bf16[640,5120]{1,0:T(8,128)(2,1)S(1)} %bitcast.14, f32[1,5120]{1,0:T(1,128)S(1)} %bitcast.26, ...), custom_call_target="tpu_custom_call" | custom-call | flops 3400 | bytes 1000 | tf_op jit(solution)/shard_map/base/pallas_call | solution.py:282
  89.2 4.8 %residual.1 = (bf16[640,5120]{1,0:T(8,128)(2,1)}, f32[8,128]{1,0:T(8,128)S(1)}) custom-call(s32[10]{0:T(128)S(1)} %broadcast_subtract_fusion.slot_ref, s32[4]{0:T(128)S(1)} %pad_add_fusion.place_ref, bf16[640,5120]{1,0:T(8,128)(2,1)S(1)} %bitcast.15, f32[640,128]{1,0:T(8,128)S(1)} %copy-done.7, bf16[640,1280]{1,0:T(8,128)(2,1)S(1)} %get-tuple-element.66.rest_0_, ...), custom_call_target="tpu_custom_call" | custom-call | flops 4700 | bytes 1000 | tf_op jit(solution)/shard_map/residual/pallas_call | solution.py:340
  94.0 1.5 %finish.1 = (f32[640,128]{1,0:T(8,128)}, f32[128,128]{1,0:T(8,128)}) custom-call(s32[10]{0:T(128)S(1)} %broadcast_subtract_fusion.slot_ref, f32[128,768]{1,0:T(8,128)S(1)} %get-tuple-element.112.held_ref, bf16[128,768]{1,0:T(8,128)(2,1)S(1)} %collective-permute-done.28.got_ref, f32[8,128]{1,0:T(8,128)S(1)} %get-tuple-element.116.done_ref), custom_call_target="tpu_custom_call" | custom-call | flops 1500 | bytes 1000 | tf_op jit(solution)/shard_map/finish/pallas_call | solution.py:411
  (46 shorter events, 0.2 us)
Async XLA Ops:
  2.4 14.8 %collective-permute-start.1 = (bf16[1280,128]{1,0:T(8,128)(2,1)}, bf16[1280,128]{1,0:T(8,128)(2,1)S(1)}, u32[]{:S(2)}, u32[]{:S(2)}) collective-permute-start(bf16[1280,128]{1,0:T(8,128)(2,1)} %constant_dynamic-slice_fusion.1), channel_id=1, source_target_pairs={{0,4},{4,8},{8,12},{12,0},{1,5},{5,9},{9,13},{13,1},{2,6},{6,10},{... | collective-permute-start | bytes 983048 | tf_op jit(solution)/shard_map/ppermute | solution.py:452
  5.4 16.5 %collective-permute-start = (bf16[1280,128]{1,0:T(8,128)(2,1)}, bf16[1280,128]{1,0:T(8,128)(2,1)}, u32[]{:S(2)}, u32[]{:S(2)}) collective-permute-start(bf16[1280,128]{1,0:T(8,128)(2,1)} %constant_dynamic-slice_fusion.1), channel_id=1, source_target_pairs={{0,12},{4,0},{8,4},{12,8},{1,13},{5,1},{9,5},{13,9},{2,14},{6,2},{... | collective-permute-start | bytes 983048 | tf_op jit(solution)/shard_map/ppermute | solution.py:452
  8.1 2.9 %copy-start = (bf16[10,64,5120]{2,1,0:T(8,128)(2,1)S(1)}, bf16[10,64,5120]{2,1,0:T(8,128)(2,1)}, u32[]{:S(2)}) copy-start(bf16[10,64,5120]{2,1,0:T(8,128)(2,1)} %param.7) | copy-start | bytes 19660804
  10.9 1.3 %copy-start.2 = (bf16[10,64,1024]{2,1,0:T(8,128)(2,1)S(1)}, bf16[10,64,1024]{2,1,0:T(8,128)(2,1)}, u32[]{:S(2)}) copy-start(bf16[10,64,1024]{2,1,0:T(8,128)(2,1)} %param.8) | copy-start | bytes 3932164
  12.3 0.9 copy-start.9
  13.2 3.3 %copy-start.5 = (bf16[1280,128]{1,0:T(8,128)(2,1)S(1)}, bf16[1280,128]{1,0:T(8,128)(2,1)}, u32[]{:S(2)}) copy-start(bf16[1280,128]{1,0:T(8,128)(2,1)} %own_ref.1) | copy-start | bytes 983044
  13.2 39.1 %slice-start = ((s8[6553600]{0:T(1024)(128)(4,1)}), s8[2359296]{0:T(1024)(128)(4,1)S(1)}, s32[]{:S(2)}) async-start(s8[6553600]{0:T(1024)(128)(4,1)} %bitcast.9), calls=%async_computation | async-start | bytes 4718592
  15.7 0.7 copy-start.6
  16.4 7.2 %copy-start.10 = (bf16[128,640]{1,0:T(8,128)(2,1)}, bf16[128,640]{1,0:T(8,128)(2,1)S(1)}, u32[]{:S(2)}) copy-start(bf16[128,640]{1,0:T(8,128)(2,1)S(1)} %get-tuple-element.78.turned_ref) | copy-start | bytes 491524
  16.5 15.2 %copy-start.8 = (f32[5120]{0:T(1024)S(1)}, f32[5120]{0:T(1024)}, u32[]{:S(2)}) copy-start(f32[5120]{0:T(1024)} %param.12) | copy-start | bytes 61444
  17.2 6.4 %copy-start.12 = (bf16[1280,128]{1,0:T(8,128)(2,1)}, bf16[1280,128]{1,0:T(8,128)(2,1)S(1)}, u32[]{:S(2)}) copy-start(bf16[1280,128]{1,0:T(8,128)(2,1)S(1)} %collective-permute-done.1) | copy-start | bytes 983044
  24.4 17.2 %collective-permute-start.3 = (bf16[2560,128]{1,0:T(8,128)(2,1)}, bf16[2560,128]{1,0:T(8,128)(2,1)S(1)}, u32[]{:S(2)}, u32[]{:S(2)}) collective-permute-start(bf16[2560,128]{1,0:T(8,128)(2,1)} %constant_dynamic-update-slice_fusion.rest_0_), channel_id=1, source_target_pairs={{0,16},{16,0},{1,17},{17,1},{2,18},{18,2},{3,19},{19,3},{4,20},{20... | collective-permute-start | bytes 1966088 | tf_op jit(solution)/shard_map/ppermute | solution.py:453
  25.9 16.1 %collective-permute-start.2 = (bf16[2560,128]{1,0:T(8,128)(2,1)}, bf16[2560,128]{1,0:T(8,128)(2,1)}, u32[]{:S(2)}, u32[]{:S(2)}) collective-permute-start(bf16[2560,128]{1,0:T(8,128)(2,1)} %constant_dynamic-update-slice_fusion.rest_0_), channel_id=1, source_target_pairs={{0,2},{2,0},{1,3},{3,1},{4,6},{6,4},{5,7},{7,5},{8,10},{10,8},{9,1... | collective-permute-start | bytes 1966088 | tf_op jit(solution)/shard_map/ppermute | solution.py:453
  27.4 13.3 %collective-permute-start.6 = (bf16[640,128]{1,0:T(8,128)(2,1)}, bf16[640,128]{1,0:T(8,128)(2,1)}, u32[]{:S(2)}, u32[]{:S(2)}) collective-permute-start(bf16[640,128]{1,0:T(8,128)(2,1)} %constant_dynamic-slice_fusion), channel_id=1, source_target_pairs={{0,4},{4,8},{8,12},{12,0},{1,5},{5,9},{9,13},{13,1},{2,6},{6,10},{... | collective-permute-start | bytes 491528 | tf_op jit(solution)/shard_map/ppermute | solution.py:452
  28.5 13.0 %collective-permute-start.5 = (bf16[640,128]{1,0:T(8,128)(2,1)}, bf16[640,128]{1,0:T(8,128)(2,1)}, u32[]{:S(2)}, u32[]{:S(2)}) collective-permute-start(bf16[640,128]{1,0:T(8,128)(2,1)} %constant_dynamic-slice_fusion), channel_id=1, source_target_pairs={{0,8},{4,12},{8,0},{12,4},{1,9},{5,13},{9,1},{13,5},{2,10},{6,14},... | collective-permute-start | bytes 491528 | tf_op jit(solution)/shard_map/ppermute | solution.py:452
  30.3 11.3 %collective-permute-start.4 = (bf16[640,128]{1,0:T(8,128)(2,1)}, bf16[640,128]{1,0:T(8,128)(2,1)}, u32[]{:S(2)}, u32[]{:S(2)}) collective-permute-start(bf16[640,128]{1,0:T(8,128)(2,1)} %constant_dynamic-slice_fusion), channel_id=1, source_target_pairs={{0,12},{4,0},{8,4},{12,8},{1,13},{5,1},{9,5},{13,9},{2,14},{6,2},{... | collective-permute-start | bytes 491528 | tf_op jit(solution)/shard_map/ppermute | solution.py:452
  31.7 2.9 %copy-start.1 = (bf16[10,64,5120]{2,1,0:T(8,128)(2,1)S(1)}, bf16[10,64,5120]{2,1,0:T(8,128)(2,1)}, u32[]{:S(2)}) copy-start(bf16[10,64,5120]{2,1,0:T(8,128)(2,1)} %param.7) | copy-start | bytes 19660804
  34.6 1.3 %copy-start.3 = (bf16[10,64,1024]{2,1,0:T(8,128)(2,1)S(1)}, bf16[10,64,1024]{2,1,0:T(8,128)(2,1)}, u32[]{:S(2)}) copy-start(bf16[10,64,1024]{2,1,0:T(8,128)(2,1)} %param.8) | copy-start | bytes 3932164
  35.9 1.7 %copy-start.4 = (bf16[1280,1024]{1,0:T(8,128)(2,1)S(1)}, bf16[1280,1024]{1,0:T(8,128)(2,1)}, u32[]{:S(2)}) copy-start(bf16[1280,1024]{1,0:T(8,128)(2,1)} %rest_0_.1) | copy-start | bytes 7864324
  37.6 9.3 %copy-start.13 = (bf16[1280,128]{1,0:T(8,128)(2,1)S(1)}, bf16[1280,128]{1,0:T(8,128)(2,1)}, u32[]{:S(2)}) copy-start(bf16[1280,128]{1,0:T(8,128)(2,1)} %copy-done.12) | copy-start | bytes 983044
  37.6 14.7 %slice-start.1 = ((s8[6553600]{0:T(1024)(128)(4,1)}), s8[4194304]{0:T(1024)(128)(4,1)S(1)}, s32[]{:S(2)}) async-start(s8[6553600]{0:T(1024)(128)(4,1)} %bitcast.9), calls=%async_computation.1 | async-start | bytes 8388608
  37.6 14.7 %copy-start.7 = (f32[640,128]{1,0:T(8,128)S(1)}, f32[640,128]{1,0:T(8,128)}, u32[]{:S(2)}) copy-start(f32[640,128]{1,0:T(8,128)} %copy-done.6) | copy-start | bytes 983044
  37.6 14.7 %copy-start.11 = (bf16[128,640]{1,0:T(8,128)(2,1)S(1)}, bf16[128,640]{1,0:T(8,128)(2,1)}, u32[]{:S(2)}) copy-start(bf16[128,640]{1,0:T(8,128)(2,1)} %copy-done.10) | copy-start | bytes 491524
  42.0 4.9 %collective-permute-start.9 = (bf16[2560,128]{1,0:T(8,128)(2,1)}, bf16[2560,128]{1,0:T(8,128)(2,1)S(1)}, u32[]{:S(2)}, u32[]{:S(2)}) collective-permute-start(bf16[2560,128]{1,0:T(8,128)(2,1)} %constant_dynamic-update-slice_fusion.rest_0_), channel_id=1, source_target_pairs={{0,1},{1,0},{2,3},{3,2},{4,5},{5,4},{6,7},{7,6},{8,9},{9,8},{10,11... | collective-permute-start | bytes 1966088 | tf_op jit(solution)/shard_map/ppermute | solution.py:453
  42.0 8.5 %collective-permute-start.10 = (bf16[2560,128]{1,0:T(8,128)(2,1)}, bf16[2560,128]{1,0:T(8,128)(2,1)S(1)}, u32[]{:S(2)}, u32[]{:S(2)}) collective-permute-start(bf16[2560,128]{1,0:T(8,128)(2,1)} %collective-permute-done.2.rest_1_), channel_id=1, source_target_pairs={{0,1},{1,0},{2,3},{3,2},{4,5},{5,4},{6,7},{7,6},{8,9},{9,8},{10,11... | collective-permute-start | bytes 1966088 | tf_op jit(solution)/shard_map/ppermute | solution.py:453
  42.5 8.0 %collective-permute-start.11 = (bf16[2560,128]{1,0:T(8,128)(2,1)S(1)}, bf16[2560,128]{1,0:T(8,128)(2,1)S(1)}, u32[]{:S(2)}, u32[]{:S(2)}) collective-permute-start(bf16[2560,128]{1,0:T(8,128)(2,1)S(1)} %collective-permute-done.3.rest_2_), channel_id=1, source_target_pairs={{0,1},{1,0},{2,3},{3,2},{4,5},{5,4},{6,7},{7,6},{8,9},{9,8},{10,11... | collective-permute-start | bytes 1966088 | tf_op jit(solution)/shard_map/ppermute | solution.py:453
  42.5 3.9 %collective-permute-start.12 = (bf16[640,128]{1,0:T(8,128)(2,1)}, bf16[640,128]{1,0:T(8,128)(2,1)S(1)}, u32[]{:S(2)}, u32[]{:S(2)}) collective-permute-start(bf16[640,128]{1,0:T(8,128)(2,1)} %collective-permute-done.4.rest_0_.rest_8_), channel_id=1, source_target_pairs={{0,1},{1,0},{2,3},{3,2},{4,5},{5,4},{6,7},{7,6},{8,9},{9,8},{10,11... | collective-permute-start | bytes 491528 | tf_op jit(solution)/shard_map/ppermute | solution.py:453
  44.0 16.5 %collective-permute-start.8 = (bf16[1280,128]{1,0:T(8,128)(2,1)S(1)}, bf16[1280,128]{1,0:T(8,128)(2,1)S(1)}, u32[]{:S(2)}, u32[]{:S(2)}) collective-permute-start(bf16[1280,128]{1,0:T(8,128)(2,1)S(1)} %slice.7), channel_id=1, source_target_pairs={{0,2},{2,0},{1,3},{3,1},{4,6},{6,4},{5,7},{7,5},{8,10},{10,8},{9,1... | collective-permute-start | bytes 983048 | tf_op jit(solution)/shard_map/ppermute | solution.py:453
  46.4 14.1 %collective-permute-start.7 = (bf16[1280,128]{1,0:T(8,128)(2,1)S(1)}, bf16[1280,128]{1,0:T(8,128)(2,1)S(1)}, u32[]{:S(2)}, u32[]{:S(2)}) collective-permute-start(bf16[1280,128]{1,0:T(8,128)(2,1)S(1)} %slice.6), channel_id=1, source_target_pairs={{0,16},{16,0},{1,17},{17,1},{2,18},{18,2},{3,19},{19,3},{4,20},{20... | collective-permute-start | bytes 983048 | tf_op jit(solution)/shard_map/ppermute | solution.py:453
  46.9 13.6 %collective-permute-start.15 = (bf16[1280,128]{1,0:T(8,128)(2,1)S(1)}, bf16[1280,128]{1,0:T(8,128)(2,1)S(1)}, u32[]{:S(2)}, u32[]{:S(2)}) collective-permute-start(bf16[1280,128]{1,0:T(8,128)(2,1)S(1)} %copy-done.13), channel_id=1, source_target_pairs={{0,4},{4,8},{8,12},{12,0},{1,5},{5,9},{9,13},{13,1},{2,6},{6,10},{... | collective-permute-start | bytes 983048 | tf_op jit(solution)/shard_map/ppermute | solution.py:452
  50.5 1.6 %collective-permute-start.13 = (bf16[640,128]{1,0:T(8,128)(2,1)}, bf16[640,128]{1,0:T(8,128)(2,1)S(1)}, u32[]{:S(2)}, u32[]{:S(2)}) collective-permute-start(bf16[640,128]{1,0:T(8,128)(2,1)} %collective-permute-done.5.rest_1_.rest_8_), channel_id=1, source_target_pairs={{0,1},{1,0},{2,3},{3,2},{4,5},{5,4},{6,7},{7,6},{8,9},{9,8},{10,11... | collective-permute-start | bytes 491528 | tf_op jit(solution)/shard_map/ppermute | solution.py:453
  50.5 1.8 %collective-permute-start.14 = (bf16[640,128]{1,0:T(8,128)(2,1)}, bf16[640,128]{1,0:T(8,128)(2,1)S(1)}, u32[]{:S(2)}, u32[]{:S(2)}) collective-permute-start(bf16[640,128]{1,0:T(8,128)(2,1)} %collective-permute-done.6.rest_2_.rest_8_), channel_id=1, source_target_pairs={{0,1},{1,0},{2,3},{3,2},{4,5},{5,4},{6,7},{7,6},{8,9},{9,8},{10,11... | collective-permute-start | bytes 491528 | tf_op jit(solution)/shard_map/ppermute | solution.py:453
  60.5 3.5 %collective-permute-start.19 = (f32[4,128,768]{2,1,0:T(8,128)S(1)}, f32[4,128,768]{2,1,0:T(8,128)S(1)}, u32[]{:S(2)}, u32[]{:S(2)}) collective-permute-start(f32[4,128,768]{2,1,0:T(8,128)S(1)} %get-tuple-element.93), channel_id=1, source_target_pairs={{0,1},{1,0},{2,3},{3,2},{4,5},{5,4},{6,7},{7,6},{8,9},{9,8},{10,11... | collective-permute-start | bytes 4718600 | tf_op jit(solution)/shard_map/ppermute | solution.py:453
  60.9 3.7 %collective-permute-start.16 = (bf16[1280,128]{1,0:T(8,128)(2,1)S(1)}, bf16[1280,128]{1,0:T(8,128)(2,1)S(1)}, u32[]{:S(2)}, u32[]{:S(2)}) collective-permute-start(bf16[1280,128]{1,0:T(8,128)(2,1)S(1)} %collective-permute-done.7.rest_3_), channel_id=1, source_target_pairs={{0,1},{1,0},{2,3},{3,2},{4,5},{5,4},{6,7},{7,6},{8,9},{9,8},{10,11... | collective-permute-start | bytes 983048 | tf_op jit(solution)/shard_map/ppermute | solution.py:453
  61.1 9.9 %collective-permute-start.18 = (bf16[1280,128]{1,0:T(8,128)(2,1)S(1)}, bf16[1280,128]{1,0:T(8,128)(2,1)S(1)}, u32[]{:S(2)}, u32[]{:S(2)}) collective-permute-start(bf16[1280,128]{1,0:T(8,128)(2,1)S(1)} %collective-permute-done.15.rest_0_), channel_id=1, source_target_pairs={{0,16},{16,0},{1,17},{17,1},{2,18},{18,2},{3,19},{19,3},{4,20},{20... | collective-permute-start | bytes 983048 | tf_op jit(solution)/shard_map/ppermute | solution.py:453
  62.6 9.6 %collective-permute-start.17 = (bf16[1280,128]{1,0:T(8,128)(2,1)S(1)}, bf16[1280,128]{1,0:T(8,128)(2,1)S(1)}, u32[]{:S(2)}, u32[]{:S(2)}) collective-permute-start(bf16[1280,128]{1,0:T(8,128)(2,1)S(1)} %collective-permute-done.15.rest_0_), channel_id=1, source_target_pairs={{0,2},{2,0},{1,3},{3,1},{4,6},{6,4},{5,7},{7,5},{8,10},{10,8},{9,1... | collective-permute-start | bytes 983048 | tf_op jit(solution)/shard_map/ppermute | solution.py:453
  64.2 9.1 %collective-permute-start.20 = (bf16[128,768]{1,0:T(8,128)(2,1)S(1)}, bf16[128,768]{1,0:T(8,128)(2,1)S(1)}, u32[]{:S(2)}, u32[]{:S(2)}) collective-permute-start(bf16[128,768]{1,0:T(8,128)(2,1)S(1)} %get-tuple-element.94), channel_id=1, source_target_pairs={{0,4},{4,8},{8,12},{12,0},{1,5},{5,9},{9,13},{13,1},{2,6},{6,10},{... | collective-permute-start | bytes 589832 | tf_op jit(solution)/shard_map/ppermute | solution.py:452
  73.3 2.6 %collective-permute-start.25 = (bf16[1280,128]{1,0:T(8,128)(2,1)S(1)}, bf16[1280,128]{1,0:T(8,128)(2,1)S(1)}, u32[]{:S(2)}, u32[]{:S(2)}) collective-permute-start(bf16[1280,128]{1,0:T(8,128)(2,1)S(1)} %collective-permute-done.8.rest_3_), channel_id=1, source_target_pairs={{0,1},{1,0},{2,3},{3,2},{4,5},{5,4},{6,7},{7,6},{8,9},{9,8},{10,11... | collective-permute-start | bytes 983048 | tf_op jit(solution)/shard_map/ppermute | solution.py:453
  73.3 6.6 %collective-permute-start.22 = (bf16[1280,128]{1,0:T(8,128)(2,1)S(1)}, bf16[1280,128]{1,0:T(8,128)(2,1)S(1)}, u32[]{:S(2)}, u32[]{:S(2)}) collective-permute-start(bf16[1280,128]{1,0:T(8,128)(2,1)S(1)} %collective-permute-done.15.rest_0_), channel_id=1, source_target_pairs={{0,1},{1,0},{2,3},{3,2},{4,5},{5,4},{6,7},{7,6},{8,9},{9,8},{10,11... | collective-permute-start | bytes 983048 | tf_op jit(solution)/shard_map/ppermute | solution.py:453
  73.8 6.1 %collective-permute-start.24 = (bf16[1280,128]{1,0:T(8,128)(2,1)S(1)}, bf16[1280,128]{1,0:T(8,128)(2,1)S(1)}, u32[]{:S(2)}, u32[]{:S(2)}) collective-permute-start(bf16[1280,128]{1,0:T(8,128)(2,1)S(1)} %collective-permute-done.18.rest_2_), channel_id=1, source_target_pairs={{0,1},{1,0},{2,3},{3,2},{4,5},{5,4},{6,7},{7,6},{8,9},{9,8},{10,11... | collective-permute-start | bytes 983048 | tf_op jit(solution)/shard_map/ppermute | solution.py:453
  73.9 6.1 %collective-permute-start.23 = (bf16[1280,128]{1,0:T(8,128)(2,1)S(1)}, bf16[1280,128]{1,0:T(8,128)(2,1)S(1)}, u32[]{:S(2)}, u32[]{:S(2)}) collective-permute-start(bf16[1280,128]{1,0:T(8,128)(2,1)S(1)} %collective-permute-done.17.rest_1_), channel_id=1, source_target_pairs={{0,1},{1,0},{2,3},{3,2},{4,5},{5,4},{6,7},{7,6},{8,9},{9,8},{10,11... | collective-permute-start | bytes 983048 | tf_op jit(solution)/shard_map/ppermute | solution.py:453
  74.4 9.6 %collective-permute-start.21 = (bf16[1280,128]{1,0:T(8,128)(2,1)S(1)}, bf16[1280,128]{1,0:T(8,128)(2,1)S(1)}, u32[]{:S(2)}, u32[]{:S(2)}) collective-permute-start(bf16[1280,128]{1,0:T(8,128)(2,1)S(1)} %collective-permute-done.17.rest_1_), channel_id=1, source_target_pairs={{0,16},{16,0},{1,17},{17,1},{2,18},{18,2},{3,19},{19,3},{4,20},{20... | collective-permute-start | bytes 983048 | tf_op jit(solution)/shard_map/ppermute | solution.py:453
  75.9 8.4 %collective-permute-start.27 = (bf16[128,768]{1,0:T(8,128)(2,1)S(1)}, bf16[128,768]{1,0:T(8,128)(2,1)S(1)}, u32[]{:S(2)}, u32[]{:S(2)}) collective-permute-start(bf16[128,768]{1,0:T(8,128)(2,1)S(1)} %add.24), channel_id=1, source_target_pairs={{0,4},{4,8},{8,12},{12,0},{1,5},{5,9},{9,13},{13,1},{2,6},{6,10},{... | collective-permute-start | bytes 589832 | tf_op jit(solution)/shard_map/ppermute | solution.py:452
  84.0 1.6 %collective-permute-start.26 = (bf16[1280,128]{1,0:T(8,128)(2,1)S(1)}, bf16[1280,128]{1,0:T(8,128)(2,1)S(1)}, u32[]{:S(2)}, u32[]{:S(2)}) collective-permute-start(bf16[1280,128]{1,0:T(8,128)(2,1)S(1)} %collective-permute-done.21.rest_3_), channel_id=1, source_target_pairs={{0,1},{1,0},{2,3},{3,2},{4,5},{5,4},{6,7},{7,6},{8,9},{9,8},{10,11... | collective-permute-start | bytes 983048 | tf_op jit(solution)/shard_map/ppermute | solution.py:453
  84.4 9.6 %collective-permute-start.28 = (bf16[128,768]{1,0:T(8,128)(2,1)S(1)}, bf16[128,768]{1,0:T(8,128)(2,1)S(1)}, u32[]{:S(2)}, u32[]{:S(2)}) collective-permute-start(bf16[128,768]{1,0:T(8,128)(2,1)S(1)} %add.25), channel_id=1, source_target_pairs={{0,4},{4,8},{8,12},{12,0},{1,5},{5,9},{9,13},{13,1},{2,6},{6,10},{... | collective-permute-start | bytes 589832 | tf_op jit(solution)/shard_map/ppermute | solution.py:452

commit v4 on v3

--- a/solution.py
+++ b/solution.py
@@ -178,32 +178,32 @@
 
 def terms_kernel(fsdp, slot_ref, place_ref, skip_ref, grad_ref, inv_ref, scale_ref, turned_ref, own_ref, *rest):
     far_refs, rest = rest[: 2 * (fsdp - 1)], rest[2 * (fsdp - 1) :]
-    keep_out, send_out, term_ref, hidden_ref, down_ref, up_ref, sems = rest
+    keep_out, send_out, hidden_ref, down_ref, up_ref = rest
     outs = (keep_out, send_out)
     core = place_ref[0]
     tokens, width = skip_ref.shape
     n = width // fsdp
     half = n // 2
     low = turned_ref.shape[0]
-    copies = Copies(sems)
+    first = core == 0
     inverse = inv_ref[...]
     projected = jnp.zeros((tokens, low), F32)
-    stores = []
     for r in range(fsdp):
         start = lax.rem(place_ref[1] + r, fsdp) * n
         if r == 0:
             down = own_ref[...]
         else:
-            for k in range(2):
-                down_ref[core ^ k] = far_refs[k * (fsdp - 1) + r - 1][...]
-            down = down_ref[...].reshape(n, low)
+            mine, theirs = far_refs[r - 1][...], far_refs[fsdp - 1 + r - 1][...]
+            down_ref[:half, :] = jnp.where(first, mine, theirs)
+            down_ref[half:, :] = jnp.where(first, theirs, mine)
+            down = down_ref[...]
         for j in range(n // 128):
             cols = pl.ds(pl.multiple_of(start + j * 128, 128), 128)
             hidden_ref[r, :, j * 128 : (j + 1) * 128] = (skip_ref[:, cols].astype(F32) * inverse * scale_ref[:, cols]).astype(BF16)
         term = jnp.dot(turned_ref[...], hidden_ref[r], preferred_element_type=F32)
-        for h in range(2):
-            term_ref[core ^ h, r, :, :half] = term[:, h * half : (h + 1) * half]
-        stores += copies.start([(term_ref.at[h, r, :, pl.ds(0, half)], outs[h].at[r, :, pl.ds(0, half)]) for h in range(2)])
+        low_half, high_half = term[:, :half], term[:, half:]
+        keep_out[r, :, :half] = jnp.where(first, low_half, high_half)
+        send_out[r, :, :half] = jnp.where(first, high_half, low_half)
         projected += jnp.dot(hidden_ref[r], down, preferred_element_type=F32)
     count = slot_ref.shape[0]
     mask = member_mask([slot_ref[s] for s in range(count)], tokens // count, (tokens, low), 0)
@@ -213,9 +213,7 @@
         shard = lax.rem(place_ref[1] + r, fsdp)
         for h in range(2):
             at = pl.multiple_of((shard * 2 + (core ^ h)) * 128, 128)
-            term_ref[h, r, :, half:] = up_ref[:, pl.ds(at, 128)]
-    stores += copies.start([(term_ref.at[h, :, :, pl.ds(half, 128)], outs[h].at[:, :, pl.ds(half, 128)]) for h in range(2)])
-    wait(stores)
+            outs[h][r, :, half:] = up_ref[:, pl.ds(at, 128)]
 
 
 def terms_call(slots_local, place, skip, inv, scales, turned, down, keep, other, grad):
@@ -229,13 +227,11 @@
         functools.partial(terms_kernel, fsdp),
         out_shape=(out, out),
         in_specs=[SMEM, SMEM] + [VMEM] * (6 + 2 * (fsdp - 1)),
-        out_specs=[pl.BlockSpec(memory_space=pl.ANY)] * 2,
+        out_specs=[VMEM] * 2,
         scratch_shapes=[
-            pltpu.VMEM((2, fsdp, low, both), F32),
             pltpu.VMEM((fsdp, tokens, n), BF16),
-            pltpu.VMEM((2, n // 2, low), BF16),
+            pltpu.VMEM((n, low), BF16),
             pltpu.VMEM((low, grad.shape[1]), F32),
-            pltpu.SemaphoreType.DMA((2 * fsdp + 2,)),
         ],
         compiler_params=params(),
         cost_estimate=cost(7.5),

time: 96 us -> 94.3 us (0.982)
  Pallas kernels: 31.7 us -> 30 us
  starting transfers between devices: 25 us -> 26.3 us
  waiting for transfers between devices: 19.4 us -> 18.1 us
    pallas_call x1, Pallas kernels: 8.12 us -> 6.41 us  [terms_call(): pl.pallas_call(functools.partial(terms_kernel, fsdp), out_shape=(out, out...]
    ppermute x20, waiting for transfers between devices: 12.3 us -> 11.1 us  [per_device_square(): over = lambda v, axis: lax.ppermute(v, axis, SWAP)]
    ppermute x9, starting transfers between devices: 13.3 us -> 14.3 us  [per_device_square(): lax.ppermute(v, 'fsdp', [(i, (i + r) % fsdp) for i in range(fsdp)])]
  transfers between devices with their start and end apart: 29 -> 29, of which waited for: 13 -> 13; matrix products, arithmetic and copies ran while one was open for 3% -> 3% of each run, Pallas kernels for 32% -> 30%
where the time goes in v4:
time: 94.3 us; the launch traced here: 93.8 us
  Pallas kernels  30 us (32%)
  starting transfers between devices  26.3 us (28%)
  waiting for transfers between devices  18.1 us (19%)
  local copies, waits for them, and re-layouts  17.8 us (19%)
    pallas_call x4, Pallas kernels, base_call(): pl.pallas_call(functools.partial(base_kernel, r, fsdp, spans), out_shape=...  14.5 us
    ppermute x9, starting transfers between devices, per_device_square(): lax.ppermute(v, 'fsdp', [(i, (i + r) % fsdp) for i in range(fsdp)])  14.3 us
    unnamed x33, local copies, waits for them, and re-layouts  13.5 us
    ppermute x20, starting transfers between devices, per_device_square(): over = lambda v, axis: lax.ppermute(v, axis, SWAP)  12 us
    ppermute x20, waiting for transfers between devices, per_device_square(): over = lambda v, axis: lax.ppermute(v, axis, SWAP)  11.1 us
    ppermute x9, waiting for transfers between devices, per_device_square(): lax.ppermute(v, 'fsdp', [(i, (i + r) % fsdp) for i in range(fsdp)])  7.04 us
    pallas_call x1, Pallas kernels, terms_call(): pl.pallas_call(functools.partial(terms_kernel, fsdp), out_shape=(out, out...  6.41 us
    pallas_call x1, Pallas kernels, residual_call(): pl.pallas_call(functools.partial(residual_kernel, fsdp), out_shape=(jax.S...  4.78 us
  transfers between devices with their start and end apart: 29, of which 13 were waited for; matrix products, arithmetic and copies ran while one was open for 3% of the time, Pallas kernels for 30%

profile of v4, /device:TPU:0, one launch (start us, length us, event | category | flops | bytes accessed | tf_op | source)
XLA Modules:
  0.0 93.8 jit_solution(14174142674232077872)
XLA Ops:
  0.6 1.7 %constant_dynamic-slice_fusion.1 = bf16[1280,128]{1,0:T(8,128)(2,1)} fusion(bf16[1280,1024]{1,0:T(8,128)(2,1)} %rest_0_.1, s32[]{:T(128)S(6)} %select_n.6), kind=kLoop, calls=%fused_computation.4 | loop fusion | bytes 655364 | tf_op jit(solution)/shard_map/dynamic_slice | solution.py:459
  2.4 3.0 %collective-permute-start.1 = (bf16[1280,128]{1,0:T(8,128)(2,1)}, bf16[1280,128]{1,0:T(8,128)(2,1)S(1)}, u32[]{:S(2)}, u32[]{:S(2)}) collective-permute-start(bf16[1280,128]{1,0:T(8,128)(2,1)} %constant_dynamic-slice_fusion.1), channel_id=1, source_target_pairs={{0,4},{4,8},{8,12},{12,0},{1,5},{5,9},{9,13},{13,1},{2,6},{6,10},{... | collective-permute-start | bytes 983048 | tf_op jit(solution)/shard_map/ppermute | solution.py:448
  5.4 2.0 %collective-permute-start = (bf16[1280,128]{1,0:T(8,128)(2,1)}, bf16[1280,128]{1,0:T(8,128)(2,1)}, u32[]{:S(2)}, u32[]{:S(2)}) collective-permute-start(bf16[1280,128]{1,0:T(8,128)(2,1)} %constant_dynamic-slice_fusion.1), channel_id=1, source_target_pairs={{0,12},{4,0},{8,4},{12,8},{1,13},{5,1},{9,5},{13,9},{2,14},{6,2},{... | collective-permute-start | bytes 983048 | tf_op jit(solution)/shard_map/ppermute | solution.py:448
  7.4 0.7 broadcast_subtract_fusion.slot_ref
  8.1 2.9 %copy-done = bf16[10,64,5120]{2,1,0:T(8,128)(2,1)S(1)} copy-done((bf16[10,64,5120]{2,1,0:T(8,128)(2,1)S(1)}, bf16[10,64,5120]{2,1,0:T(8,128)(2,1)}, u32[]{:S(2)}) %copy-start) | copy-done | bytes 6553624
  10.9 1.3 %copy-done.2 = bf16[10,64,1024]{2,1,0:T(8,128)(2,1)S(1)} copy-done((bf16[10,64,1024]{2,1,0:T(8,128)(2,1)S(1)}, bf16[10,64,1024]{2,1,0:T(8,128)(2,1)}, u32[]{:S(2)}) %copy-start.2) | copy-done | bytes 1310744
  12.3 0.9 %copy-done.9 = bf16[128,1024]{1,0:T(8,128)(2,1)S(1)} copy-done((bf16[128,1024]{1,0:T(8,128)(2,1)S(1)}, bf16[128,1024]{1,0:T(8,128)(2,1)}, u32[]{:S(2)}) %copy-start.9) | copy-done | bytes 262168
  13.2 2.5 %norm.1 = (f32[640,128]{1,0:T(8,128)S(1)}, bf16[640,128]{1,0:T(8,128)(2,1)S(1)}, bf16[128,640]{1,0:T(8,128)(2,1)S(1)}) custom-call(s32[10]{0:T(128)S(1)} %broadcast_subtract_fusion.slot_ref, bf16[640,5120]{1,0:T(8,128)(2,1)S(1)} %bitcast.7, bf16[640,1024]{1,0:T(8,128)(2,1)S(1)} %bitcast.16, bf16[128,1024]{1,0:T(8,128)(2,1)S(1)} %copy-done.9), custom_call_target="tpu_custom_call" | custom-call | flops 2500 | bytes 1000 | tf_op jit(solution)/shard_map/norm/pallas_call | solution.py:164
  15.7 0.7 copy-done.6
  16.5 0.7 constant_dynamic-slice_fusion
  17.2 0.0 collective-permute-done.1
  17.2 4.7 %collective-permute-done = bf16[1280,128]{1,0:T(8,128)(2,1)} collective-permute-done((bf16[1280,128]{1,0:T(8,128)(2,1)}, bf16[1280,128]{1,0:T(8,128)(2,1)}, u32[]{:S(2)}, u32[]{:S(2)}) %collective-permute-start) | collective-permute-done | bytes 327712 | tf_op jit(solution)/shard_map/ppermute | solution.py:448
  21.9 1.7 %constant_dynamic-update-slice_fusion.1 = bf16[2560,128]{1,0:T(8,128)(2,1)} fusion(bf16[1280,128]{1,0:T(8,128)(2,1)} %collective-permute-done), kind=kLoop, calls=%fused_computation.1 | loop fusion | bytes 655360
  23.6 0.7 constant_dynamic-update-slice_fusion.rest_0_
  24.4 1.5 %collective-permute-start.3 = (bf16[2560,128]{1,0:T(8,128)(2,1)}, bf16[2560,128]{1,0:T(8,128)(2,1)S(1)}, u32[]{:S(2)}, u32[]{:S(2)}) collective-permute-start(bf16[2560,128]{1,0:T(8,128)(2,1)} %constant_dynamic-update-slice_fusion.rest_0_), channel_id=1, source_target_pairs={{0,16},{16,0},{1,17},{17,1},{2,18},{18,2},{3,19},{19,3},{4,20},{20... | collective-permute-start | bytes 1966088 | tf_op jit(solution)/shard_map/ppermute | solution.py:449
  25.9 1.5 %collective-permute-start.2 = (bf16[2560,128]{1,0:T(8,128)(2,1)}, bf16[2560,128]{1,0:T(8,128)(2,1)}, u32[]{:S(2)}, u32[]{:S(2)}) collective-permute-start(bf16[2560,128]{1,0:T(8,128)(2,1)} %constant_dynamic-update-slice_fusion.rest_0_), channel_id=1, source_target_pairs={{0,2},{2,0},{1,3},{3,1},{4,6},{6,4},{5,7},{7,5},{8,10},{10,8},{9,1... | collective-permute-start | bytes 1966088 | tf_op jit(solution)/shard_map/ppermute | solution.py:449
  27.4 1.1 %collective-permute-start.6 = (bf16[640,128]{1,0:T(8,128)(2,1)}, bf16[640,128]{1,0:T(8,128)(2,1)}, u32[]{:S(2)}, u32[]{:S(2)}) collective-permute-start(bf16[640,128]{1,0:T(8,128)(2,1)} %constant_dynamic-slice_fusion), channel_id=1, source_target_pairs={{0,4},{4,8},{8,12},{12,0},{1,5},{5,9},{9,13},{13,1},{2,6},{6,10},{... | collective-permute-start | bytes 491528 | tf_op jit(solution)/shard_map/ppermute | solution.py:448
  28.5 1.8 %collective-permute-start.5 = (bf16[640,128]{1,0:T(8,128)(2,1)}, bf16[640,128]{1,0:T(8,128)(2,1)}, u32[]{:S(2)}, u32[]{:S(2)}) collective-permute-start(bf16[640,128]{1,0:T(8,128)(2,1)} %constant_dynamic-slice_fusion), channel_id=1, source_target_pairs={{0,8},{4,12},{8,0},{12,4},{1,9},{5,13},{9,1},{13,5},{2,10},{6,14},... | collective-permute-start | bytes 491528 | tf_op jit(solution)/shard_map/ppermute | solution.py:448
  30.3 1.3 %collective-permute-start.4 = (bf16[640,128]{1,0:T(8,128)(2,1)}, bf16[640,128]{1,0:T(8,128)(2,1)}, u32[]{:S(2)}, u32[]{:S(2)}) collective-permute-start(bf16[640,128]{1,0:T(8,128)(2,1)} %constant_dynamic-slice_fusion), channel_id=1, source_target_pairs={{0,12},{4,0},{8,4},{12,8},{1,13},{5,1},{9,5},{13,9},{2,14},{6,2},{... | collective-permute-start | bytes 491528 | tf_op jit(solution)/shard_map/ppermute | solution.py:448
  31.6 0.1 pad_add_fusion.place_ref
  31.7 2.9 %copy-done.1 = bf16[10,64,5120]{2,1,0:T(8,128)(2,1)S(1)} copy-done((bf16[10,64,5120]{2,1,0:T(8,128)(2,1)S(1)}, bf16[10,64,5120]{2,1,0:T(8,128)(2,1)}, u32[]{:S(2)}) %copy-start.1) | copy-done | bytes 6553624
  34.6 1.3 %copy-done.3 = bf16[10,64,1024]{2,1,0:T(8,128)(2,1)S(1)} copy-done((bf16[10,64,1024]{2,1,0:T(8,128)(2,1)S(1)}, bf16[10,64,1024]{2,1,0:T(8,128)(2,1)}, u32[]{:S(2)}) %copy-start.3) | copy-done | bytes 1310744
  35.9 1.7 %copy-done.4 = bf16[1280,1024]{1,0:T(8,128)(2,1)S(1)} copy-done((bf16[1280,1024]{1,0:T(8,128)(2,1)S(1)}, bf16[1280,1024]{1,0:T(8,128)(2,1)}, u32[]{:S(2)}) %copy-start.4) | copy-done | bytes 2621464
  37.6 3.0 %base.4 = (bf16[640,1280]{1,0:T(8,128)(2,1)S(1)}, f32[640,128]{1,0:T(8,128)S(1)}) custom-call(s32[4]{0:T(128)S(1)} %pad_add_fusion.place_ref, bf16[640,1024]{1,0:T(8,128)(2,1)S(1)} %bitcast.17, bf16[640,128]{1,0:T(8,128)(2,1)S(1)} %get-tuple-element.65.mid_ref, bf16[640,5120]{1,0:T(8,128)(2,1)S(1)} %bitcast.8, f32[1,5120]{1,0:T(1,128)S(1)} %bitcast.22, ...), custom_call_target="tpu_custom_call" | custom-call | flops 3400 | bytes 1000 | tf_op jit(solution)/shard_map/base/pallas_call | solution.py:278
  40.7 0.0 collective-permute-done.6.rest_2_.rest_8_
  40.7 0.9 collective-permute-done.5.rest_1_.rest_8_
  41.6 0.0 collective-permute-done.4.rest_0_.rest_8_
  41.6 0.4 collective-permute-done.2.rest_1_
  42.0 0.5 collective-permute-start.10
  42.5 0.0 collective-permute-start.11
  42.5 0.5 collective-permute-start.12
  43.0 1.0 %slice.6 = bf16[1280,128]{1,0:T(8,128)(2,1)S(1)} slice(bf16[2560,128]{1,0:T(8,128)(2,1)} %collective-permute-done.2.rest_1_), slice={[0:1280], [0:128]} | slice | bytes 655360 | tf_op jit(solution)/shard_map/slice | solution.py:472
  44.0 1.6 %collective-permute-start.8 = (bf16[1280,128]{1,0:T(8,128)(2,1)S(1)}, bf16[1280,128]{1,0:T(8,128)(2,1)S(1)}, u32[]{:S(2)}, u32[]{:S(2)}) collective-permute-start(bf16[1280,128]{1,0:T(8,128)(2,1)S(1)} %slice.7), channel_id=1, source_target_pairs={{0,2},{2,0},{1,3},{3,1},{4,6},{6,4},{5,7},{7,5},{8,10},{10,8},{9,1... | collective-permute-start | bytes 983048 | tf_op jit(solution)/shard_map/ppermute | solution.py:449
  45.6 0.8 collective-permute-done.12.rest_3_.rest_9_
  46.4 0.5 collective-permute-start.7
  46.9 3.6 %collective-permute-start.15 = (bf16[1280,128]{1,0:T(8,128)(2,1)S(1)}, bf16[1280,128]{1,0:T(8,128)(2,1)S(1)}, u32[]{:S(2)}, u32[]{:S(2)}) collective-permute-start(bf16[1280,128]{1,0:T(8,128)(2,1)S(1)} %copy-done.13), channel_id=1, source_target_pairs={{0,4},{4,8},{8,12},{12,0},{1,5},{5,9},{9,13},{13,1},{2,6},{6,10},{... | collective-permute-start | bytes 983048 | tf_op jit(solution)/shard_map/ppermute | solution.py:448
  50.5 0.5 collective-permute-start.14
  51.0 1.1 %collective-permute-done.13.rest_4_.rest_9_ = bf16[640,128]{1,0:T(8,128)(2,1)S(1)} collective-permute-done((bf16[640,128]{1,0:T(8,128)(2,1)}, bf16[640,128]{1,0:T(8,128)(2,1)S(1)}, u32[]{:S(2)}, u32[]{:S(2)}) %collective-permute-start.13) | collective-permute-done | bytes 163872 | tf_op jit(solution)/shard_map/ppermute | solution.py:449
  52.1 0.2 collective-permute-done.14.rest_5_.rest_9_
  52.4 6.4 %terms.1 = (f32[4,128,768]{2,1,0:T(8,128)S(1)}, f32[4,128,768]{2,1,0:T(8,128)S(1)}) custom-call(s32[10]{0:T(128)S(1)} %broadcast_subtract_fusion.slot_ref, s32[4]{0:T(128)S(1)} %pad_add_fusion.place_ref, bf16[640,5120]{1,0:T(8,128)(2,1)S(1)} %bitcast.11, bf16[640,1024]{1,0:T(8,128)(2,1)S(1)} %bitcast.18, f32[640,128]{1,0:T(8,128)S(1)} %copy-done.7, ...), custom_call_target="tpu_custom_call" | custom-call | flops 7500 | bytes 1000 | tf_op jit(solution)/shard_map/terms/pallas_call | solution.py:226
  58.8 0.4 collective-permute-start.19
  59.2 0.2 collective-permute-start.16
  59.4 1.5 %collective-permute-start.18 = (bf16[1280,128]{1,0:T(8,128)(2,1)S(1)}, bf16[1280,128]{1,0:T(8,128)(2,1)S(1)}, u32[]{:S(2)}, u32[]{:S(2)}) collective-permute-start(bf16[1280,128]{1,0:T(8,128)(2,1)S(1)} %collective-permute-done.15.rest_0_), channel_id=1, source_target_pairs={{0,16},{16,0},{1,17},{17,1},{2,18},{18,2},{3,19},{19,3},{4,20},{20... | collective-permute-start | bytes 983048 | tf_op jit(solution)/shard_map/ppermute | solution.py:449
  60.9 0.8 collective-permute-start.17
  61.7 0.6 collective-permute-done.19.got_ref
  62.3 0.2 both.1
  62.5 1.3 %collective-permute-start.20 = (bf16[128,768]{1,0:T(8,128)(2,1)S(1)}, bf16[128,768]{1,0:T(8,128)(2,1)S(1)}, u32[]{:S(2)}, u32[]{:S(2)}) collective-permute-start(bf16[128,768]{1,0:T(8,128)(2,1)S(1)} %get-tuple-element.94), channel_id=1, source_target_pairs={{0,4},{4,8},{8,12},{12,0},{1,5},{5,9},{9,13},{13,1},{2,6},{6,10},{... | collective-permute-start | bytes 589832 | tf_op jit(solution)/shard_map/ppermute | solution.py:448
  63.8 3.9 %base.5 = (bf16[640,1280]{1,0:T(8,128)(2,1)S(1)}, f32[640,128]{1,0:T(8,128)S(1)}) custom-call(s32[4]{0:T(128)S(1)} %pad_add_fusion.place_ref, bf16[640,1024]{1,0:T(8,128)(2,1)S(1)} %bitcast.19, bf16[640,128]{1,0:T(8,128)(2,1)S(1)} %get-tuple-element.65.mid_ref, bf16[640,5120]{1,0:T(8,128)(2,1)S(1)} %bitcast.12, f32[1,5120]{1,0:T(1,128)S(1)} %bitcast.24, ...), custom_call_target="tpu_custom_call" | custom-call | flops 3400 | bytes 1000 | tf_op jit(solution)/shard_map/base/pallas_call | solution.py:278
  67.8 1.5 %collective-permute-done.18.rest_2_ = bf16[1280,128]{1,0:T(8,128)(2,1)S(1)} collective-permute-done((bf16[1280,128]{1,0:T(8,128)(2,1)S(1)}, bf16[1280,128]{1,0:T(8,128)(2,1)S(1)}, u32[]{:S(2)}, u32[]{:S(2)}) %collective-permute-start.18) | collective-permute-done | bytes 327712 | tf_op jit(solution)/shard_map/ppermute | solution.py:449
  69.3 1.2 %collective-permute-done.17.rest_1_ = bf16[1280,128]{1,0:T(8,128)(2,1)S(1)} collective-permute-done((bf16[1280,128]{1,0:T(8,128)(2,1)S(1)}, bf16[1280,128]{1,0:T(8,128)(2,1)S(1)}, u32[]{:S(2)}, u32[]{:S(2)}) %collective-permute-start.17) | collective-permute-done | bytes 327712 | tf_op jit(solution)/shard_map/ppermute | solution.py:449
  70.5 1.1 %collective-permute-done.20.got_ref = bf16[128,768]{1,0:T(8,128)(2,1)S(1)} collective-permute-done((bf16[128,768]{1,0:T(8,128)(2,1)S(1)}, bf16[128,768]{1,0:T(8,128)(2,1)S(1)}, u32[]{:S(2)}, u32[]{:S(2)}) %collective-permute-start.20) | collective-permute-done | bytes 196640 | tf_op jit(solution)/shard_map/ppermute | solution.py:448
  71.6 0.5 collective-permute-start.22
  72.2 0.0 collective-permute-start.24
  72.2 0.5 collective-permute-start.23
  72.7 1.5 %collective-permute-start.21 = (bf16[1280,128]{1,0:T(8,128)(2,1)S(1)}, bf16[1280,128]{1,0:T(8,128)(2,1)S(1)}, u32[]{:S(2)}, u32[]{:S(2)}) collective-permute-start(bf16[1280,128]{1,0:T(8,128)(2,1)S(1)} %collective-permute-done.17.rest_1_), channel_id=1, source_target_pairs={{0,16},{16,0},{1,17},{17,1},{2,18},{18,2},{3,19},{19,3},{4,20},{20... | collective-permute-start | bytes 983048 | tf_op jit(solution)/shard_map/ppermute | solution.py:449
  74.2 0.1 collective-permute-start.27
  74.3 3.9 %base.6 = (bf16[640,1280]{1,0:T(8,128)(2,1)S(1)}, f32[640,128]{1,0:T(8,128)S(1)}) custom-call(s32[4]{0:T(128)S(1)} %pad_add_fusion.place_ref, bf16[640,1024]{1,0:T(8,128)(2,1)S(1)} %bitcast.20, bf16[640,128]{1,0:T(8,128)(2,1)S(1)} %get-tuple-element.65.mid_ref, bf16[640,5120]{1,0:T(8,128)(2,1)S(1)} %bitcast.13, f32[1,5120]{1,0:T(1,128)S(1)} %bitcast.25, ...), custom_call_target="tpu_custom_call" | custom-call | flops 3400 | bytes 1000 | tf_op jit(solution)/shard_map/base/pallas_call | solution.py:278
  78.3 4.0 %collective-permute-done.21.rest_3_ = bf16[1280,128]{1,0:T(8,128)(2,1)S(1)} collective-permute-done((bf16[1280,128]{1,0:T(8,128)(2,1)S(1)}, bf16[1280,128]{1,0:T(8,128)(2,1)S(1)}, u32[]{:S(2)}, u32[]{:S(2)}) %collective-permute-start.21) | collective-permute-done | bytes 327712 | tf_op jit(solution)/shard_map/ppermute | solution.py:449
  82.3 0.3 collective-permute-done.27.got_ref
  82.7 0.1 collective-permute-start.28
  82.7 1.2 %collective-permute-done.26.rest_7_ = bf16[1280,128]{1,0:T(8,128)(2,1)S(1)} collective-permute-done((bf16[1280,128]{1,0:T(8,128)(2,1)S(1)}, bf16[1280,128]{1,0:T(8,128)(2,1)S(1)}, u32[]{:S(2)}, u32[]{:S(2)}) %collective-permute-start.26) | collective-permute-done | bytes 327712 | tf_op jit(solution)/shard_map/ppermute | solution.py:449
  83.9 3.6 %base.7 = (bf16[640,1280]{1,0:T(8,128)(2,1)S(1)}, f32[640,128]{1,0:T(8,128)S(1)}) custom-call(s32[4]{0:T(128)S(1)} %pad_add_fusion.place_ref, bf16[640,1024]{1,0:T(8,128)(2,1)S(1)} %bitcast.21, bf16[640,128]{1,0:T(8,128)(2,1)S(1)} %get-tuple-element.65.mid_ref, bf16[640,5120]{1,0:T(8,128)(2,1)S(1)} %bitcast.14, f32[1,5120]{1,0:T(1,128)S(1)} %bitcast.26, ...), custom_call_target="tpu_custom_call" | custom-call | flops 3400 | bytes 1000 | tf_op jit(solution)/shard_map/base/pallas_call | solution.py:278
  87.5 4.8 %residual.1 = (bf16[640,5120]{1,0:T(8,128)(2,1)}, f32[8,128]{1,0:T(8,128)S(1)}) custom-call(s32[10]{0:T(128)S(1)} %broadcast_subtract_fusion.slot_ref, s32[4]{0:T(128)S(1)} %pad_add_fusion.place_ref, bf16[640,5120]{1,0:T(8,128)(2,1)S(1)} %bitcast.15, f32[640,128]{1,0:T(8,128)S(1)} %copy-done.7, bf16[640,1280]{1,0:T(8,128)(2,1)S(1)} %get-tuple-element.66.rest_0_, ...), custom_call_target="tpu_custom_call" | custom-call | flops 4700 | bytes 1000 | tf_op jit(solution)/shard_map/residual/pallas_call | solution.py:336
  92.3 1.5 %finish.1 = (f32[640,128]{1,0:T(8,128)}, f32[128,128]{1,0:T(8,128)}) custom-call(s32[10]{0:T(128)S(1)} %broadcast_subtract_fusion.slot_ref, f32[128,768]{1,0:T(8,128)S(1)} %get-tuple-element.112.held_ref, bf16[128,768]{1,0:T(8,128)(2,1)S(1)} %collective-permute-done.28.got_ref, f32[8,128]{1,0:T(8,128)S(1)} %get-tuple-element.116.done_ref), custom_call_target="tpu_custom_call" | custom-call | flops 1500 | bytes 1000 | tf_op jit(solution)/shard_map/finish/pallas_call | solution.py:407
  (46 shorter events, 0.2 us)
Async XLA Ops:
  2.4 14.8 %collective-permute-start.1 = (bf16[1280,128]{1,0:T(8,128)(2,1)}, bf16[1280,128]{1,0:T(8,128)(2,1)S(1)}, u32[]{:S(2)}, u32[]{:S(2)}) collective-permute-start(bf16[1280,128]{1,0:T(8,128)(2,1)} %constant_dynamic-slice_fusion.1), channel_id=1, source_target_pairs={{0,4},{4,8},{8,12},{12,0},{1,5},{5,9},{9,13},{13,1},{2,6},{6,10},{... | collective-permute-start | bytes 983048 | tf_op jit(solution)/shard_map/ppermute | solution.py:448
  5.4 16.5 %collective-permute-start = (bf16[1280,128]{1,0:T(8,128)(2,1)}, bf16[1280,128]{1,0:T(8,128)(2,1)}, u32[]{:S(2)}, u32[]{:S(2)}) collective-permute-start(bf16[1280,128]{1,0:T(8,128)(2,1)} %constant_dynamic-slice_fusion.1), channel_id=1, source_target_pairs={{0,12},{4,0},{8,4},{12,8},{1,13},{5,1},{9,5},{13,9},{2,14},{6,2},{... | collective-permute-start | bytes 983048 | tf_op jit(solution)/shard_map/ppermute | solution.py:448
  8.1 2.9 %copy-start = (bf16[10,64,5120]{2,1,0:T(8,128)(2,1)S(1)}, bf16[10,64,5120]{2,1,0:T(8,128)(2,1)}, u32[]{:S(2)}) copy-start(bf16[10,64,5120]{2,1,0:T(8,128)(2,1)} %param.7) | copy-start | bytes 19660804
  10.9 1.3 %copy-start.2 = (bf16[10,64,1024]{2,1,0:T(8,128)(2,1)S(1)}, bf16[10,64,1024]{2,1,0:T(8,128)(2,1)}, u32[]{:S(2)}) copy-start(bf16[10,64,1024]{2,1,0:T(8,128)(2,1)} %param.8) | copy-start | bytes 3932164
  12.3 0.9 %copy-start.9 = (bf16[128,1024]{1,0:T(8,128)(2,1)S(1)}, bf16[128,1024]{1,0:T(8,128)(2,1)}, u32[]{:S(2)}) copy-start(bf16[128,1024]{1,0:T(8,128)(2,1)} %up_ref.1) | copy-start | bytes 786436
  13.2 3.3 %copy-start.5 = (bf16[1280,128]{1,0:T(8,128)(2,1)S(1)}, bf16[1280,128]{1,0:T(8,128)(2,1)}, u32[]{:S(2)}) copy-start(bf16[1280,128]{1,0:T(8,128)(2,1)} %own_ref.1) | copy-start | bytes 983044
  13.2 39.1 %slice-start = ((s8[6553600]{0:T(1024)(128)(4,1)}), s8[2359296]{0:T(1024)(128)(4,1)S(1)}, s32[]{:S(2)}) async-start(s8[6553600]{0:T(1024)(128)(4,1)} %bitcast.9), calls=%async_computation | async-start | bytes 4718592
  15.7 0.7 copy-start.6
  16.4 7.2 %copy-start.10 = (bf16[128,640]{1,0:T(8,128)(2,1)}, bf16[128,640]{1,0:T(8,128)(2,1)S(1)}, u32[]{:S(2)}) copy-start(bf16[128,640]{1,0:T(8,128)(2,1)S(1)} %get-tuple-element.78.turned_ref) | copy-start | bytes 491524
  16.5 15.2 %copy-start.8 = (f32[5120]{0:T(1024)S(1)}, f32[5120]{0:T(1024)}, u32[]{:S(2)}) copy-start(f32[5120]{0:T(1024)} %param.12) | copy-start | bytes 61444
  17.2 6.4 %copy-start.12 = (bf16[1280,128]{1,0:T(8,128)(2,1)}, bf16[1280,128]{1,0:T(8,128)(2,1)S(1)}, u32[]{:S(2)}) copy-start(bf16[1280,128]{1,0:T(8,128)(2,1)S(1)} %collective-permute-done.1) | copy-start | bytes 983044
  24.4 17.2 %collective-permute-start.3 = (bf16[2560,128]{1,0:T(8,128)(2,1)}, bf16[2560,128]{1,0:T(8,128)(2,1)S(1)}, u32[]{:S(2)}, u32[]{:S(2)}) collective-permute-start(bf16[2560,128]{1,0:T(8,128)(2,1)} %constant_dynamic-update-slice_fusion.rest_0_), channel_id=1, source_target_pairs={{0,16},{16,0},{1,17},{17,1},{2,18},{18,2},{3,19},{19,3},{4,20},{20... | collective-permute-start | bytes 1966088 | tf_op jit(solution)/shard_map/ppermute | solution.py:449
  25.9 16.1 %collective-permute-start.2 = (bf16[2560,128]{1,0:T(8,128)(2,1)}, bf16[2560,128]{1,0:T(8,128)(2,1)}, u32[]{:S(2)}, u32[]{:S(2)}) collective-permute-start(bf16[2560,128]{1,0:T(8,128)(2,1)} %constant_dynamic-update-slice_fusion.rest_0_), channel_id=1, source_target_pairs={{0,2},{2,0},{1,3},{3,1},{4,6},{6,4},{5,7},{7,5},{8,10},{10,8},{9,1... | collective-permute-start | bytes 1966088 | tf_op jit(solution)/shard_map/ppermute | solution.py:449
  27.4 13.3 %collective-permute-start.6 = (bf16[640,128]{1,0:T(8,128)(2,1)}, bf16[640,128]{1,0:T(8,128)(2,1)}, u32[]{:S(2)}, u32[]{:S(2)}) collective-permute-start(bf16[640,128]{1,0:T(8,128)(2,1)} %constant_dynamic-slice_fusion), channel_id=1, source_target_pairs={{0,4},{4,8},{8,12},{12,0},{1,5},{5,9},{9,13},{13,1},{2,6},{6,10},{... | collective-permute-start | bytes 491528 | tf_op jit(solution)/shard_map/ppermute | solution.py:448
  28.5 13.0 %collective-permute-start.5 = (bf16[640,128]{1,0:T(8,128)(2,1)}, bf16[640,128]{1,0:T(8,128)(2,1)}, u32[]{:S(2)}, u32[]{:S(2)}) collective-permute-start(bf16[640,128]{1,0:T(8,128)(2,1)} %constant_dynamic-slice_fusion), channel_id=1, source_target_pairs={{0,8},{4,12},{8,0},{12,4},{1,9},{5,13},{9,1},{13,5},{2,10},{6,14},... | collective-permute-start | bytes 491528 | tf_op jit(solution)/shard_map/ppermute | solution.py:448
  30.3 11.3 %collective-permute-start.4 = (bf16[640,128]{1,0:T(8,128)(2,1)}, bf16[640,128]{1,0:T(8,128)(2,1)}, u32[]{:S(2)}, u32[]{:S(2)}) collective-permute-start(bf16[640,128]{1,0:T(8,128)(2,1)} %constant_dynamic-slice_fusion), channel_id=1, source_target_pairs={{0,12},{4,0},{8,4},{12,8},{1,13},{5,1},{9,5},{13,9},{2,14},{6,2},{... | collective-permute-start | bytes 491528 | tf_op jit(solution)/shard_map/ppermute | solution.py:448
  31.7 2.9 %copy-start.1 = (bf16[10,64,5120]{2,1,0:T(8,128)(2,1)S(1)}, bf16[10,64,5120]{2,1,0:T(8,128)(2,1)}, u32[]{:S(2)}) copy-start(bf16[10,64,5120]{2,1,0:T(8,128)(2,1)} %param.7) | copy-start | bytes 19660804
  34.6 1.3 %copy-start.3 = (bf16[10,64,1024]{2,1,0:T(8,128)(2,1)S(1)}, bf16[10,64,1024]{2,1,0:T(8,128)(2,1)}, u32[]{:S(2)}) copy-start(bf16[10,64,1024]{2,1,0:T(8,128)(2,1)} %param.8) | copy-start | bytes 3932164
  35.9 1.7 %copy-start.4 = (bf16[1280,1024]{1,0:T(8,128)(2,1)S(1)}, bf16[1280,1024]{1,0:T(8,128)(2,1)}, u32[]{:S(2)}) copy-start(bf16[1280,1024]{1,0:T(8,128)(2,1)} %rest_0_.1) | copy-start | bytes 7864324
  37.6 9.3 %copy-start.13 = (bf16[1280,128]{1,0:T(8,128)(2,1)S(1)}, bf16[1280,128]{1,0:T(8,128)(2,1)}, u32[]{:S(2)}) copy-start(bf16[1280,128]{1,0:T(8,128)(2,1)} %copy-done.12) | copy-start | bytes 983044
  37.6 14.7 %slice-start.1 = ((s8[6553600]{0:T(1024)(128)(4,1)}), s8[4194304]{0:T(1024)(128)(4,1)S(1)}, s32[]{:S(2)}) async-start(s8[6553600]{0:T(1024)(128)(4,1)} %bitcast.9), calls=%async_computation.1 | async-start | bytes 8388608
  37.6 14.7 %copy-start.7 = (f32[640,128]{1,0:T(8,128)S(1)}, f32[640,128]{1,0:T(8,128)}, u32[]{:S(2)}) copy-start(f32[640,128]{1,0:T(8,128)} %copy-done.6) | copy-start | bytes 983044
  37.6 14.7 %copy-start.11 = (bf16[128,640]{1,0:T(8,128)(2,1)S(1)}, bf16[128,640]{1,0:T(8,128)(2,1)}, u32[]{:S(2)}) copy-start(bf16[128,640]{1,0:T(8,128)(2,1)} %copy-done.10) | copy-start | bytes 491524
  42.0 4.9 %collective-permute-start.9 = (bf16[2560,128]{1,0:T(8,128)(2,1)}, bf16[2560,128]{1,0:T(8,128)(2,1)S(1)}, u32[]{:S(2)}, u32[]{:S(2)}) collective-permute-start(bf16[2560,128]{1,0:T(8,128)(2,1)} %constant_dynamic-update-slice_fusion.rest_0_), channel_id=1, source_target_pairs={{0,1},{1,0},{2,3},{3,2},{4,5},{5,4},{6,7},{7,6},{8,9},{9,8},{10,11... | collective-permute-start | bytes 1966088 | tf_op jit(solution)/shard_map/ppermute | solution.py:449
  42.0 8.5 %collective-permute-start.10 = (bf16[2560,128]{1,0:T(8,128)(2,1)}, bf16[2560,128]{1,0:T(8,128)(2,1)S(1)}, u32[]{:S(2)}, u32[]{:S(2)}) collective-permute-start(bf16[2560,128]{1,0:T(8,128)(2,1)} %collective-permute-done.2.rest_1_), channel_id=1, source_target_pairs={{0,1},{1,0},{2,3},{3,2},{4,5},{5,4},{6,7},{7,6},{8,9},{9,8},{10,11... | collective-permute-start | bytes 1966088 | tf_op jit(solution)/shard_map/ppermute | solution.py:449
  42.5 8.0 %collective-permute-start.11 = (bf16[2560,128]{1,0:T(8,128)(2,1)S(1)}, bf16[2560,128]{1,0:T(8,128)(2,1)S(1)}, u32[]{:S(2)}, u32[]{:S(2)}) collective-permute-start(bf16[2560,128]{1,0:T(8,128)(2,1)S(1)} %collective-permute-done.3.rest_2_), channel_id=1, source_target_pairs={{0,1},{1,0},{2,3},{3,2},{4,5},{5,4},{6,7},{7,6},{8,9},{9,8},{10,11... | collective-permute-start | bytes 1966088 | tf_op jit(solution)/shard_map/ppermute | solution.py:449
  42.5 3.9 %collective-permute-start.12 = (bf16[640,128]{1,0:T(8,128)(2,1)}, bf16[640,128]{1,0:T(8,128)(2,1)S(1)}, u32[]{:S(2)}, u32[]{:S(2)}) collective-permute-start(bf16[640,128]{1,0:T(8,128)(2,1)} %collective-permute-done.4.rest_0_.rest_8_), channel_id=1, source_target_pairs={{0,1},{1,0},{2,3},{3,2},{4,5},{5,4},{6,7},{7,6},{8,9},{9,8},{10,11... | collective-permute-start | bytes 491528 | tf_op jit(solution)/shard_map/ppermute | solution.py:449
  44.0 14.8 %collective-permute-start.8 = (bf16[1280,128]{1,0:T(8,128)(2,1)S(1)}, bf16[1280,128]{1,0:T(8,128)(2,1)S(1)}, u32[]{:S(2)}, u32[]{:S(2)}) collective-permute-start(bf16[1280,128]{1,0:T(8,128)(2,1)S(1)} %slice.7), channel_id=1, source_target_pairs={{0,2},{2,0},{1,3},{3,1},{4,6},{6,4},{5,7},{7,5},{8,10},{10,8},{9,1... | collective-permute-start | bytes 983048 | tf_op jit(solution)/shard_map/ppermute | solution.py:449
  46.4 12.4 %collective-permute-start.7 = (bf16[1280,128]{1,0:T(8,128)(2,1)S(1)}, bf16[1280,128]{1,0:T(8,128)(2,1)S(1)}, u32[]{:S(2)}, u32[]{:S(2)}) collective-permute-start(bf16[1280,128]{1,0:T(8,128)(2,1)S(1)} %slice.6), channel_id=1, source_target_pairs={{0,16},{16,0},{1,17},{17,1},{2,18},{18,2},{3,19},{19,3},{4,20},{20... | collective-permute-start | bytes 983048 | tf_op jit(solution)/shard_map/ppermute | solution.py:449
  46.9 11.9 %collective-permute-start.15 = (bf16[1280,128]{1,0:T(8,128)(2,1)S(1)}, bf16[1280,128]{1,0:T(8,128)(2,1)S(1)}, u32[]{:S(2)}, u32[]{:S(2)}) collective-permute-start(bf16[1280,128]{1,0:T(8,128)(2,1)S(1)} %copy-done.13), channel_id=1, source_target_pairs={{0,4},{4,8},{8,12},{12,0},{1,5},{5,9},{9,13},{13,1},{2,6},{6,10},{... | collective-permute-start | bytes 983048 | tf_op jit(solution)/shard_map/ppermute | solution.py:448
  50.5 1.6 %collective-permute-start.13 = (bf16[640,128]{1,0:T(8,128)(2,1)}, bf16[640,128]{1,0:T(8,128)(2,1)S(1)}, u32[]{:S(2)}, u32[]{:S(2)}) collective-permute-start(bf16[640,128]{1,0:T(8,128)(2,1)} %collective-permute-done.5.rest_1_.rest_8_), channel_id=1, source_target_pairs={{0,1},{1,0},{2,3},{3,2},{4,5},{5,4},{6,7},{7,6},{8,9},{9,8},{10,11... | collective-permute-start | bytes 491528 | tf_op jit(solution)/shard_map/ppermute | solution.py:449
  50.5 1.8 %collective-permute-start.14 = (bf16[640,128]{1,0:T(8,128)(2,1)}, bf16[640,128]{1,0:T(8,128)(2,1)S(1)}, u32[]{:S(2)}, u32[]{:S(2)}) collective-permute-start(bf16[640,128]{1,0:T(8,128)(2,1)} %collective-permute-done.6.rest_2_.rest_8_), channel_id=1, source_target_pairs={{0,1},{1,0},{2,3},{3,2},{4,5},{5,4},{6,7},{7,6},{8,9},{9,8},{10,11... | collective-permute-start | bytes 491528 | tf_op jit(solution)/shard_map/ppermute | solution.py:449
  58.8 3.5 %collective-permute-start.19 = (f32[4,128,768]{2,1,0:T(8,128)S(1)}, f32[4,128,768]{2,1,0:T(8,128)S(1)}, u32[]{:S(2)}, u32[]{:S(2)}) collective-permute-start(f32[4,128,768]{2,1,0:T(8,128)S(1)} %get-tuple-element.93), channel_id=1, source_target_pairs={{0,1},{1,0},{2,3},{3,2},{4,5},{5,4},{6,7},{7,6},{8,9},{9,8},{10,11... | collective-permute-start | bytes 4718600 | tf_op jit(solution)/shard_map/ppermute | solution.py:449
  59.2 4.7 %collective-permute-start.16 = (bf16[1280,128]{1,0:T(8,128)(2,1)S(1)}, bf16[1280,128]{1,0:T(8,128)(2,1)S(1)}, u32[]{:S(2)}, u32[]{:S(2)}) collective-permute-start(bf16[1280,128]{1,0:T(8,128)(2,1)S(1)} %collective-permute-done.7.rest_3_), channel_id=1, source_target_pairs={{0,1},{1,0},{2,3},{3,2},{4,5},{5,4},{6,7},{7,6},{8,9},{9,8},{10,11... | collective-permute-start | bytes 983048 | tf_op jit(solution)/shard_map/ppermute | solution.py:449
  59.4 9.9 %collective-permute-start.18 = (bf16[1280,128]{1,0:T(8,128)(2,1)S(1)}, bf16[1280,128]{1,0:T(8,128)(2,1)S(1)}, u32[]{:S(2)}, u32[]{:S(2)}) collective-permute-start(bf16[1280,128]{1,0:T(8,128)(2,1)S(1)} %collective-permute-done.15.rest_0_), channel_id=1, source_target_pairs={{0,16},{16,0},{1,17},{17,1},{2,18},{18,2},{3,19},{19,3},{4,20},{20... | collective-permute-start | bytes 983048 | tf_op jit(solution)/shard_map/ppermute | solution.py:449
  60.9 9.6 %collective-permute-start.17 = (bf16[1280,128]{1,0:T(8,128)(2,1)S(1)}, bf16[1280,128]{1,0:T(8,128)(2,1)S(1)}, u32[]{:S(2)}, u32[]{:S(2)}) collective-permute-start(bf16[1280,128]{1,0:T(8,128)(2,1)S(1)} %collective-permute-done.15.rest_0_), channel_id=1, source_target_pairs={{0,2},{2,0},{1,3},{3,1},{4,6},{6,4},{5,7},{7,5},{8,10},{10,8},{9,1... | collective-permute-start | bytes 983048 | tf_op jit(solution)/shard_map/ppermute | solution.py:449
  62.5 9.1 %collective-permute-start.20 = (bf16[128,768]{1,0:T(8,128)(2,1)S(1)}, bf16[128,768]{1,0:T(8,128)(2,1)S(1)}, u32[]{:S(2)}, u32[]{:S(2)}) collective-permute-start(bf16[128,768]{1,0:T(8,128)(2,1)S(1)} %get-tuple-element.94), channel_id=1, source_target_pairs={{0,4},{4,8},{8,12},{12,0},{1,5},{5,9},{9,13},{13,1},{2,6},{6,10},{... | collective-permute-start | bytes 589832 | tf_op jit(solution)/shard_map/ppermute | solution.py:448
  71.6 2.6 %collective-permute-start.25 = (bf16[1280,128]{1,0:T(8,128)(2,1)S(1)}, bf16[1280,128]{1,0:T(8,128)(2,1)S(1)}, u32[]{:S(2)}, u32[]{:S(2)}) collective-permute-start(bf16[1280,128]{1,0:T(8,128)(2,1)S(1)} %collective-permute-done.8.rest_3_), channel_id=1, source_target_pairs={{0,1},{1,0},{2,3},{3,2},{4,5},{5,4},{6,7},{7,6},{8,9},{9,8},{10,11... | collective-permute-start | bytes 983048 | tf_op jit(solution)/shard_map/ppermute | solution.py:449
  71.6 6.6 %collective-permute-start.22 = (bf16[1280,128]{1,0:T(8,128)(2,1)S(1)}, bf16[1280,128]{1,0:T(8,128)(2,1)S(1)}, u32[]{:S(2)}, u32[]{:S(2)}) collective-permute-start(bf16[1280,128]{1,0:T(8,128)(2,1)S(1)} %collective-permute-done.15.rest_0_), channel_id=1, source_target_pairs={{0,1},{1,0},{2,3},{3,2},{4,5},{5,4},{6,7},{7,6},{8,9},{9,8},{10,11... | collective-permute-start | bytes 983048 | tf_op jit(solution)/shard_map/ppermute | solution.py:449
  72.2 6.1 %collective-permute-start.24 = (bf16[1280,128]{1,0:T(8,128)(2,1)S(1)}, bf16[1280,128]{1,0:T(8,128)(2,1)S(1)}, u32[]{:S(2)}, u32[]{:S(2)}) collective-permute-start(bf16[1280,128]{1,0:T(8,128)(2,1)S(1)} %collective-permute-done.18.rest_2_), channel_id=1, source_target_pairs={{0,1},{1,0},{2,3},{3,2},{4,5},{5,4},{6,7},{7,6},{8,9},{9,8},{10,11... | collective-permute-start | bytes 983048 | tf_op jit(solution)/shard_map/ppermute | solution.py:449
  72.2 6.1 %collective-permute-start.23 = (bf16[1280,128]{1,0:T(8,128)(2,1)S(1)}, bf16[1280,128]{1,0:T(8,128)(2,1)S(1)}, u32[]{:S(2)}, u32[]{:S(2)}) collective-permute-start(bf16[1280,128]{1,0:T(8,128)(2,1)S(1)} %collective-permute-done.17.rest_1_), channel_id=1, source_target_pairs={{0,1},{1,0},{2,3},{3,2},{4,5},{5,4},{6,7},{7,6},{8,9},{9,8},{10,11... | collective-permute-start | bytes 983048 | tf_op jit(solution)/shard_map/ppermute | solution.py:449
  72.7 9.6 %collective-permute-start.21 = (bf16[1280,128]{1,0:T(8,128)(2,1)S(1)}, bf16[1280,128]{1,0:T(8,128)(2,1)S(1)}, u32[]{:S(2)}, u32[]{:S(2)}) collective-permute-start(bf16[1280,128]{1,0:T(8,128)(2,1)S(1)} %collective-permute-done.17.rest_1_), channel_id=1, source_target_pairs={{0,16},{16,0},{1,17},{17,1},{2,18},{18,2},{3,19},{19,3},{4,20},{20... | collective-permute-start | bytes 983048 | tf_op jit(solution)/shard_map/ppermute | solution.py:449
  74.2 8.4 %collective-permute-start.27 = (bf16[128,768]{1,0:T(8,128)(2,1)S(1)}, bf16[128,768]{1,0:T(8,128)(2,1)S(1)}, u32[]{:S(2)}, u32[]{:S(2)}) collective-permute-start(bf16[128,768]{1,0:T(8,128)(2,1)S(1)} %add.24), channel_id=1, source_target_pairs={{0,4},{4,8},{8,12},{12,0},{1,5},{5,9},{9,13},{13,1},{2,6},{6,10},{... | collective-permute-start | bytes 589832 | tf_op jit(solution)/shard_map/ppermute | solution.py:448
  82.3 1.6 %collective-permute-start.26 = (bf16[1280,128]{1,0:T(8,128)(2,1)S(1)}, bf16[1280,128]{1,0:T(8,128)(2,1)S(1)}, u32[]{:S(2)}, u32[]{:S(2)}) collective-permute-start(bf16[1280,128]{1,0:T(8,128)(2,1)S(1)} %collective-permute-done.21.rest_3_), channel_id=1, source_target_pairs={{0,1},{1,0},{2,3},{3,2},{4,5},{5,4},{6,7},{7,6},{8,9},{9,8},{10,11... | collective-permute-start | bytes 983048 | tf_op jit(solution)/shard_map/ppermute | solution.py:449
  82.7 9.6 %collective-permute-start.28 = (bf16[128,768]{1,0:T(8,128)(2,1)S(1)}, bf16[128,768]{1,0:T(8,128)(2,1)S(1)}, u32[]{:S(2)}, u32[]{:S(2)}) collective-permute-start(bf16[128,768]{1,0:T(8,128)(2,1)S(1)} %add.25), channel_id=1, source_target_pairs={{0,4},{4,8},{8,12},{12,0},{1,5},{5,9},{9,13},{13,1},{2,6},{6,10},{... | collective-permute-start | bytes 589832 | tf_op jit(solution)/shard_map/ppermute | solution.py:448

commit v5 on v4

--- a/solution.py
+++ b/solution.py
@@ -250,9 +250,9 @@
         for j in range(kdim // 128):
             at = pl.multiple_of((place_ref[2] ^ j) * 128, 128)
             both_ref[:, j * 128 : (j + 1) * 128] = grad_ref[:, pl.ds(at, 128)]
-        for k in range(2):
-            at = pl.multiple_of((core ^ k) * half, half)
-            down_ref[pl.ds(at, half), :] = ins[len(spans) + k][...]
+        mine, theirs = ins[-2][...], ins[-1][...]
+        down_ref[:half, :] = jnp.where(core == 0, mine, theirs)
+        down_ref[half:, :] = jnp.where(core == 0, theirs, mine)
     else:
         both_ref[:, :kdim] = grad_ref[...]
         down_ref[...] = ins[1][...]

time: 94.3 us -> 94.3 us (level)
  transfers between devices with their start and end apart: 29 -> 29, of which waited for: 13 -> 13; matrix products, arithmetic and copies ran while one was open for 3% -> 3% of each run, Pallas kernels for 30% -> 31%
where the time goes in v5:
time: 94.3 us; the launch traced here: 93.8 us
  Pallas kernels  30.1 us (32%)
  starting transfers between devices  26.3 us (28%)
  waiting for transfers between devices  18 us (19%)
  local copies, waits for them, and re-layouts  17.8 us (19%)
    pallas_call x4, Pallas kernels, base_call(): pl.pallas_call(functools.partial(base_kernel, r, fsdp, spans), out_shape=...  14.6 us
    ppermute x9, starting transfers between devices, per_device_square(): lax.ppermute(v, 'fsdp', [(i, (i + r) % fsdp) for i in range(fsdp)])  14.3 us
    unnamed x33, local copies, waits for them, and re-layouts  13.5 us
    ppermute x20, starting transfers between devices, per_device_square(): over = lambda v, axis: lax.ppermute(v, axis, SWAP)  12 us
    ppermute x20, waiting for transfers between devices, per_device_square(): over = lambda v, axis: lax.ppermute(v, axis, SWAP)  11 us
    ppermute x9, waiting for transfers between devices, per_device_square(): lax.ppermute(v, 'fsdp', [(i, (i + r) % fsdp) for i in range(fsdp)])  7.04 us
    pallas_call x1, Pallas kernels, terms_call(): pl.pallas_call(functools.partial(terms_kernel, fsdp), out_shape=(out, out...  6.41 us
    pallas_call x1, Pallas kernels, residual_call(): pl.pallas_call(functools.partial(residual_kernel, fsdp), out_shape=(jax.S...  4.78 us
  transfers between devices with their start and end apart: 29, of which 13 were waited for; matrix products, arithmetic and copies ran while one was open for 3% of the time, Pallas kernels for 31%

profile of v5, /device:TPU:0, one launch (start us, length us, event | category | flops | bytes accessed | tf_op | source)
XLA Modules:
  0.0 93.8 jit_solution(9081412803657267525)
XLA Ops:
  0.6 1.7 %constant_dynamic-slice_fusion.1 = bf16[1280,128]{1,0:T(8,128)(2,1)} fusion(bf16[1280,1024]{1,0:T(8,128)(2,1)} %rest_0_.1, s32[]{:T(128)S(6)} %select_n.6), kind=kLoop, calls=%fused_computation.4 | loop fusion | bytes 655364 | tf_op jit(solution)/shard_map/dynamic_slice | solution.py:459
  2.4 3.0 %collective-permute-start.1 = (bf16[1280,128]{1,0:T(8,128)(2,1)}, bf16[1280,128]{1,0:T(8,128)(2,1)S(1)}, u32[]{:S(2)}, u32[]{:S(2)}) collective-permute-start(bf16[1280,128]{1,0:T(8,128)(2,1)} %constant_dynamic-slice_fusion.1), channel_id=1, source_target_pairs={{0,4},{4,8},{8,12},{12,0},{1,5},{5,9},{9,13},{13,1},{2,6},{6,10},{... | collective-permute-start | bytes 983048 | tf_op jit(solution)/shard_map/ppermute | solution.py:448
  5.4 2.0 %collective-permute-start = (bf16[1280,128]{1,0:T(8,128)(2,1)}, bf16[1280,128]{1,0:T(8,128)(2,1)}, u32[]{:S(2)}, u32[]{:S(2)}) collective-permute-start(bf16[1280,128]{1,0:T(8,128)(2,1)} %constant_dynamic-slice_fusion.1), channel_id=1, source_target_pairs={{0,12},{4,0},{8,4},{12,8},{1,13},{5,1},{9,5},{13,9},{2,14},{6,2},{... | collective-permute-start | bytes 983048 | tf_op jit(solution)/shard_map/ppermute | solution.py:448
  7.4 0.7 broadcast_subtract_fusion.slot_ref
  8.1 2.9 %copy-done = bf16[10,64,5120]{2,1,0:T(8,128)(2,1)S(1)} copy-done((bf16[10,64,5120]{2,1,0:T(8,128)(2,1)S(1)}, bf16[10,64,5120]{2,1,0:T(8,128)(2,1)}, u32[]{:S(2)}) %copy-start) | copy-done | bytes 6553624
  10.9 1.3 %copy-done.2 = bf16[10,64,1024]{2,1,0:T(8,128)(2,1)S(1)} copy-done((bf16[10,64,1024]{2,1,0:T(8,128)(2,1)S(1)}, bf16[10,64,1024]{2,1,0:T(8,128)(2,1)}, u32[]{:S(2)}) %copy-start.2) | copy-done | bytes 1310744
  12.3 0.9 %copy-done.9 = bf16[128,1024]{1,0:T(8,128)(2,1)S(1)} copy-done((bf16[128,1024]{1,0:T(8,128)(2,1)S(1)}, bf16[128,1024]{1,0:T(8,128)(2,1)}, u32[]{:S(2)}) %copy-start.9) | copy-done | bytes 262168
  13.2 2.5 %norm.1 = (f32[640,128]{1,0:T(8,128)S(1)}, bf16[640,128]{1,0:T(8,128)(2,1)S(1)}, bf16[128,640]{1,0:T(8,128)(2,1)S(1)}) custom-call(s32[10]{0:T(128)S(1)} %broadcast_subtract_fusion.slot_ref, bf16[640,5120]{1,0:T(8,128)(2,1)S(1)} %bitcast.7, bf16[640,1024]{1,0:T(8,128)(2,1)S(1)} %bitcast.16, bf16[128,1024]{1,0:T(8,128)(2,1)S(1)} %copy-done.9), custom_call_target="tpu_custom_call" | custom-call | flops 2500 | bytes 1000 | tf_op jit(solution)/shard_map/norm/pallas_call | solution.py:164
  15.7 0.7 copy-done.6
  16.5 0.7 constant_dynamic-slice_fusion
  17.2 4.7 %collective-permute-done = bf16[1280,128]{1,0:T(8,128)(2,1)} collective-permute-done((bf16[1280,128]{1,0:T(8,128)(2,1)}, bf16[1280,128]{1,0:T(8,128)(2,1)}, u32[]{:S(2)}, u32[]{:S(2)}) %collective-permute-start) | collective-permute-done | bytes 327712 | tf_op jit(solution)/shard_map/ppermute | solution.py:448
  21.9 1.7 %constant_dynamic-update-slice_fusion.1 = bf16[2560,128]{1,0:T(8,128)(2,1)} fusion(bf16[1280,128]{1,0:T(8,128)(2,1)} %collective-permute-done), kind=kLoop, calls=%fused_computation.1 | loop fusion | bytes 655360
  23.6 0.7 constant_dynamic-update-slice_fusion.rest_0_
  24.4 1.5 %collective-permute-start.3 = (bf16[2560,128]{1,0:T(8,128)(2,1)}, bf16[2560,128]{1,0:T(8,128)(2,1)S(1)}, u32[]{:S(2)}, u32[]{:S(2)}) collective-permute-start(bf16[2560,128]{1,0:T(8,128)(2,1)} %constant_dynamic-update-slice_fusion.rest_0_), channel_id=1, source_target_pairs={{0,16},{16,0},{1,17},{17,1},{2,18},{18,2},{3,19},{19,3},{4,20},{20... | collective-permute-start | bytes 1966088 | tf_op jit(solution)/shard_map/ppermute | solution.py:449
  25.9 1.5 %collective-permute-start.2 = (bf16[2560,128]{1,0:T(8,128)(2,1)}, bf16[2560,128]{1,0:T(8,128)(2,1)}, u32[]{:S(2)}, u32[]{:S(2)}) collective-permute-start(bf16[2560,128]{1,0:T(8,128)(2,1)} %constant_dynamic-update-slice_fusion.rest_0_), channel_id=1, source_target_pairs={{0,2},{2,0},{1,3},{3,1},{4,6},{6,4},{5,7},{7,5},{8,10},{10,8},{9,1... | collective-permute-start | bytes 1966088 | tf_op jit(solution)/shard_map/ppermute | solution.py:449
  27.4 1.1 %collective-permute-start.6 = (bf16[640,128]{1,0:T(8,128)(2,1)}, bf16[640,128]{1,0:T(8,128)(2,1)}, u32[]{:S(2)}, u32[]{:S(2)}) collective-permute-start(bf16[640,128]{1,0:T(8,128)(2,1)} %constant_dynamic-slice_fusion), channel_id=1, source_target_pairs={{0,4},{4,8},{8,12},{12,0},{1,5},{5,9},{9,13},{13,1},{2,6},{6,10},{... | collective-permute-start | bytes 491528 | tf_op jit(solution)/shard_map/ppermute | solution.py:448
  28.5 1.8 %collective-permute-start.5 = (bf16[640,128]{1,0:T(8,128)(2,1)}, bf16[640,128]{1,0:T(8,128)(2,1)}, u32[]{:S(2)}, u32[]{:S(2)}) collective-permute-start(bf16[640,128]{1,0:T(8,128)(2,1)} %constant_dynamic-slice_fusion), channel_id=1, source_target_pairs={{0,8},{4,12},{8,0},{12,4},{1,9},{5,13},{9,1},{13,5},{2,10},{6,14},... | collective-permute-start | bytes 491528 | tf_op jit(solution)/shard_map/ppermute | solution.py:448
  30.3 1.3 %collective-permute-start.4 = (bf16[640,128]{1,0:T(8,128)(2,1)}, bf16[640,128]{1,0:T(8,128)(2,1)}, u32[]{:S(2)}, u32[]{:S(2)}) collective-permute-start(bf16[640,128]{1,0:T(8,128)(2,1)} %constant_dynamic-slice_fusion), channel_id=1, source_target_pairs={{0,12},{4,0},{8,4},{12,8},{1,13},{5,1},{9,5},{13,9},{2,14},{6,2},{... | collective-permute-start | bytes 491528 | tf_op jit(solution)/shard_map/ppermute | solution.py:448
  31.6 0.1 pad_add_fusion.place_ref
  31.7 2.9 %copy-done.1 = bf16[10,64,5120]{2,1,0:T(8,128)(2,1)S(1)} copy-done((bf16[10,64,5120]{2,1,0:T(8,128)(2,1)S(1)}, bf16[10,64,5120]{2,1,0:T(8,128)(2,1)}, u32[]{:S(2)}) %copy-start.1) | copy-done | bytes 6553624
  34.6 1.3 %copy-done.3 = bf16[10,64,1024]{2,1,0:T(8,128)(2,1)S(1)} copy-done((bf16[10,64,1024]{2,1,0:T(8,128)(2,1)S(1)}, bf16[10,64,1024]{2,1,0:T(8,128)(2,1)}, u32[]{:S(2)}) %copy-start.3) | copy-done | bytes 1310744
  35.9 1.7 %copy-done.4 = bf16[1280,1024]{1,0:T(8,128)(2,1)S(1)} copy-done((bf16[1280,1024]{1,0:T(8,128)(2,1)S(1)}, bf16[1280,1024]{1,0:T(8,128)(2,1)}, u32[]{:S(2)}) %copy-start.4) | copy-done | bytes 2621464
  37.6 3.0 %base.4 = (bf16[640,1280]{1,0:T(8,128)(2,1)S(1)}, f32[640,128]{1,0:T(8,128)S(1)}) custom-call(s32[4]{0:T(128)S(1)} %pad_add_fusion.place_ref, bf16[640,1024]{1,0:T(8,128)(2,1)S(1)} %bitcast.17, bf16[640,128]{1,0:T(8,128)(2,1)S(1)} %get-tuple-element.65.mid_ref, bf16[640,5120]{1,0:T(8,128)(2,1)S(1)} %bitcast.8, f32[1,5120]{1,0:T(1,128)S(1)} %bitcast.22, ...), custom_call_target="tpu_custom_call" | custom-call | flops 3400 | bytes 1000 | tf_op jit(solution)/shard_map/base/pallas_call | solution.py:278
  40.7 0.0 collective-permute-done.6.rest_2_.rest_8_
  40.7 0.9 collective-permute-done.5.rest_1_.rest_8_
  41.6 0.0 collective-permute-done.4.rest_0_.rest_8_
  41.6 0.0 collective-permute-done.3.rest_2_
  41.6 0.4 collective-permute-done.2.rest_1_
  42.0 0.5 collective-permute-start.10
  42.5 0.0 collective-permute-start.11
  42.5 0.5 collective-permute-start.12
  43.0 1.0 %slice.6 = bf16[1280,128]{1,0:T(8,128)(2,1)S(1)} slice(bf16[2560,128]{1,0:T(8,128)(2,1)} %collective-permute-done.2.rest_1_), slice={[0:1280], [0:128]} | slice | bytes 655360 | tf_op jit(solution)/shard_map/slice | solution.py:472
  44.0 1.6 %collective-permute-start.8 = (bf16[1280,128]{1,0:T(8,128)(2,1)S(1)}, bf16[1280,128]{1,0:T(8,128)(2,1)S(1)}, u32[]{:S(2)}, u32[]{:S(2)}) collective-permute-start(bf16[1280,128]{1,0:T(8,128)(2,1)S(1)} %slice.7), channel_id=1, source_target_pairs={{0,2},{2,0},{1,3},{3,1},{4,6},{6,4},{5,7},{7,5},{8,10},{10,8},{9,1... | collective-permute-start | bytes 983048 | tf_op jit(solution)/shard_map/ppermute | solution.py:449
  45.6 0.8 collective-permute-done.12.rest_3_.rest_9_
  46.4 0.5 collective-permute-start.7
  46.9 3.6 %collective-permute-start.15 = (bf16[1280,128]{1,0:T(8,128)(2,1)S(1)}, bf16[1280,128]{1,0:T(8,128)(2,1)S(1)}, u32[]{:S(2)}, u32[]{:S(2)}) collective-permute-start(bf16[1280,128]{1,0:T(8,128)(2,1)S(1)} %copy-done.13), channel_id=1, source_target_pairs={{0,4},{4,8},{8,12},{12,0},{1,5},{5,9},{9,13},{13,1},{2,6},{6,10},{... | collective-permute-start | bytes 983048 | tf_op jit(solution)/shard_map/ppermute | solution.py:448
  50.5 0.5 collective-permute-start.14
  51.0 1.1 %collective-permute-done.13.rest_4_.rest_9_ = bf16[640,128]{1,0:T(8,128)(2,1)S(1)} collective-permute-done((bf16[640,128]{1,0:T(8,128)(2,1)}, bf16[640,128]{1,0:T(8,128)(2,1)S(1)}, u32[]{:S(2)}, u32[]{:S(2)}) %collective-permute-start.13) | collective-permute-done | bytes 163872 | tf_op jit(solution)/shard_map/ppermute | solution.py:449
  52.1 0.2 collective-permute-done.14.rest_5_.rest_9_
  52.4 6.4 %terms.1 = (f32[4,128,768]{2,1,0:T(8,128)S(1)}, f32[4,128,768]{2,1,0:T(8,128)S(1)}) custom-call(s32[10]{0:T(128)S(1)} %broadcast_subtract_fusion.slot_ref, s32[4]{0:T(128)S(1)} %pad_add_fusion.place_ref, bf16[640,5120]{1,0:T(8,128)(2,1)S(1)} %bitcast.11, bf16[640,1024]{1,0:T(8,128)(2,1)S(1)} %bitcast.18, f32[640,128]{1,0:T(8,128)S(1)} %copy-done.7, ...), custom_call_target="tpu_custom_call" | custom-call | flops 7500 | bytes 1000 | tf_op jit(solution)/shard_map/terms/pallas_call | solution.py:226
  58.8 0.4 collective-permute-start.19
  59.2 0.2 collective-permute-start.16
  59.4 1.5 %collective-permute-start.18 = (bf16[1280,128]{1,0:T(8,128)(2,1)S(1)}, bf16[1280,128]{1,0:T(8,128)(2,1)S(1)}, u32[]{:S(2)}, u32[]{:S(2)}) collective-permute-start(bf16[1280,128]{1,0:T(8,128)(2,1)S(1)} %collective-permute-done.15.rest_0_), channel_id=1, source_target_pairs={{0,16},{16,0},{1,17},{17,1},{2,18},{18,2},{3,19},{19,3},{4,20},{20... | collective-permute-start | bytes 983048 | tf_op jit(solution)/shard_map/ppermute | solution.py:449
  60.9 0.8 collective-permute-start.17
  61.7 0.6 collective-permute-done.19.got_ref
  62.3 0.2 both.1
  62.5 1.3 %collective-permute-start.20 = (bf16[128,768]{1,0:T(8,128)(2,1)S(1)}, bf16[128,768]{1,0:T(8,128)(2,1)S(1)}, u32[]{:S(2)}, u32[]{:S(2)}) collective-permute-start(bf16[128,768]{1,0:T(8,128)(2,1)S(1)} %get-tuple-element.94), channel_id=1, source_target_pairs={{0,4},{4,8},{8,12},{12,0},{1,5},{5,9},{9,13},{13,1},{2,6},{6,10},{... | collective-permute-start | bytes 589832 | tf_op jit(solution)/shard_map/ppermute | solution.py:448
  63.8 4.0 %base.5 = (bf16[640,1280]{1,0:T(8,128)(2,1)S(1)}, f32[640,128]{1,0:T(8,128)S(1)}) custom-call(s32[4]{0:T(128)S(1)} %pad_add_fusion.place_ref, bf16[640,1024]{1,0:T(8,128)(2,1)S(1)} %bitcast.19, bf16[640,128]{1,0:T(8,128)(2,1)S(1)} %get-tuple-element.65.mid_ref, bf16[640,5120]{1,0:T(8,128)(2,1)S(1)} %bitcast.12, f32[1,5120]{1,0:T(1,128)S(1)} %bitcast.24, ...), custom_call_target="tpu_custom_call" | custom-call | flops 3400 | bytes 1000 | tf_op jit(solution)/shard_map/base/pallas_call | solution.py:278
  67.8 1.4 %collective-permute-done.18.rest_2_ = bf16[1280,128]{1,0:T(8,128)(2,1)S(1)} collective-permute-done((bf16[1280,128]{1,0:T(8,128)(2,1)S(1)}, bf16[1280,128]{1,0:T(8,128)(2,1)S(1)}, u32[]{:S(2)}, u32[]{:S(2)}) %collective-permute-start.18) | collective-permute-done | bytes 327712 | tf_op jit(solution)/shard_map/ppermute | solution.py:449
  69.3 1.2 %collective-permute-done.17.rest_1_ = bf16[1280,128]{1,0:T(8,128)(2,1)S(1)} collective-permute-done((bf16[1280,128]{1,0:T(8,128)(2,1)S(1)}, bf16[1280,128]{1,0:T(8,128)(2,1)S(1)}, u32[]{:S(2)}, u32[]{:S(2)}) %collective-permute-start.17) | collective-permute-done | bytes 327712 | tf_op jit(solution)/shard_map/ppermute | solution.py:449
  70.5 1.1 %collective-permute-done.20.got_ref = bf16[128,768]{1,0:T(8,128)(2,1)S(1)} collective-permute-done((bf16[128,768]{1,0:T(8,128)(2,1)S(1)}, bf16[128,768]{1,0:T(8,128)(2,1)S(1)}, u32[]{:S(2)}, u32[]{:S(2)}) %collective-permute-start.20) | collective-permute-done | bytes 196640 | tf_op jit(solution)/shard_map/ppermute | solution.py:448
  71.6 0.5 collective-permute-start.22
  72.2 0.0 collective-permute-start.24
  72.2 0.5 collective-permute-start.23
  72.7 1.5 %collective-permute-start.21 = (bf16[1280,128]{1,0:T(8,128)(2,1)S(1)}, bf16[1280,128]{1,0:T(8,128)(2,1)S(1)}, u32[]{:S(2)}, u32[]{:S(2)}) collective-permute-start(bf16[1280,128]{1,0:T(8,128)(2,1)S(1)} %collective-permute-done.17.rest_1_), channel_id=1, source_target_pairs={{0,16},{16,0},{1,17},{17,1},{2,18},{18,2},{3,19},{19,3},{4,20},{20... | collective-permute-start | bytes 983048 | tf_op jit(solution)/shard_map/ppermute | solution.py:449
  74.2 0.1 collective-permute-start.27
  74.3 4.0 %base.6 = (bf16[640,1280]{1,0:T(8,128)(2,1)S(1)}, f32[640,128]{1,0:T(8,128)S(1)}) custom-call(s32[4]{0:T(128)S(1)} %pad_add_fusion.place_ref, bf16[640,1024]{1,0:T(8,128)(2,1)S(1)} %bitcast.20, bf16[640,128]{1,0:T(8,128)(2,1)S(1)} %get-tuple-element.65.mid_ref, bf16[640,5120]{1,0:T(8,128)(2,1)S(1)} %bitcast.13, f32[1,5120]{1,0:T(1,128)S(1)} %bitcast.25, ...), custom_call_target="tpu_custom_call" | custom-call | flops 3400 | bytes 1000 | tf_op jit(solution)/shard_map/base/pallas_call | solution.py:278
  78.3 4.0 %collective-permute-done.21.rest_3_ = bf16[1280,128]{1,0:T(8,128)(2,1)S(1)} collective-permute-done((bf16[1280,128]{1,0:T(8,128)(2,1)S(1)}, bf16[1280,128]{1,0:T(8,128)(2,1)S(1)}, u32[]{:S(2)}, u32[]{:S(2)}) %collective-permute-start.21) | collective-permute-done | bytes 327712 | tf_op jit(solution)/shard_map/ppermute | solution.py:449
  82.3 0.3 collective-permute-done.27.got_ref
  82.7 0.1 collective-permute-start.28
  82.7 1.2 %collective-permute-done.26.rest_7_ = bf16[1280,128]{1,0:T(8,128)(2,1)S(1)} collective-permute-done((bf16[1280,128]{1,0:T(8,128)(2,1)S(1)}, bf16[1280,128]{1,0:T(8,128)(2,1)S(1)}, u32[]{:S(2)}, u32[]{:S(2)}) %collective-permute-start.26) | collective-permute-done | bytes 327712 | tf_op jit(solution)/shard_map/ppermute | solution.py:449
  83.9 3.6 %base.7 = (bf16[640,1280]{1,0:T(8,128)(2,1)S(1)}, f32[640,128]{1,0:T(8,128)S(1)}) custom-call(s32[4]{0:T(128)S(1)} %pad_add_fusion.place_ref, bf16[640,1024]{1,0:T(8,128)(2,1)S(1)} %bitcast.21, bf16[640,128]{1,0:T(8,128)(2,1)S(1)} %get-tuple-element.65.mid_ref, bf16[640,5120]{1,0:T(8,128)(2,1)S(1)} %bitcast.14, f32[1,5120]{1,0:T(1,128)S(1)} %bitcast.26, ...), custom_call_target="tpu_custom_call" | custom-call | flops 3400 | bytes 1000 | tf_op jit(solution)/shard_map/base/pallas_call | solution.py:278
  87.5 4.8 %residual.1 = (bf16[640,5120]{1,0:T(8,128)(2,1)}, f32[8,128]{1,0:T(8,128)S(1)}) custom-call(s32[10]{0:T(128)S(1)} %broadcast_subtract_fusion.slot_ref, s32[4]{0:T(128)S(1)} %pad_add_fusion.place_ref, bf16[640,5120]{1,0:T(8,128)(2,1)S(1)} %bitcast.15, f32[640,128]{1,0:T(8,128)S(1)} %copy-done.7, bf16[640,1280]{1,0:T(8,128)(2,1)S(1)} %get-tuple-element.66.rest_0_, ...), custom_call_target="tpu_custom_call" | custom-call | flops 4700 | bytes 1000 | tf_op jit(solution)/shard_map/residual/pallas_call | solution.py:336
  92.3 1.5 %finish.1 = (f32[640,128]{1,0:T(8,128)}, f32[128,128]{1,0:T(8,128)}) custom-call(s32[10]{0:T(128)S(1)} %broadcast_subtract_fusion.slot_ref, f32[128,768]{1,0:T(8,128)S(1)} %get-tuple-element.112.held_ref, bf16[128,768]{1,0:T(8,128)(2,1)S(1)} %collective-permute-done.28.got_ref, f32[8,128]{1,0:T(8,128)S(1)} %get-tuple-element.116.done_ref), custom_call_target="tpu_custom_call" | custom-call | flops 1500 | bytes 1000 | tf_op jit(solution)/shard_map/finish/pallas_call | solution.py:407
  (46 shorter events, 0.2 us)
Async XLA Ops:
  2.4 14.8 %collective-permute-start.1 = (bf16[1280,128]{1,0:T(8,128)(2,1)}, bf16[1280,128]{1,0:T(8,128)(2,1)S(1)}, u32[]{:S(2)}, u32[]{:S(2)}) collective-permute-start(bf16[1280,128]{1,0:T(8,128)(2,1)} %constant_dynamic-slice_fusion.1), channel_id=1, source_target_pairs={{0,4},{4,8},{8,12},{12,0},{1,5},{5,9},{9,13},{13,1},{2,6},{6,10},{... | collective-permute-start | bytes 983048 | tf_op jit(solution)/shard_map/ppermute | solution.py:448
  5.4 16.5 %collective-permute-start = (bf16[1280,128]{1,0:T(8,128)(2,1)}, bf16[1280,128]{1,0:T(8,128)(2,1)}, u32[]{:S(2)}, u32[]{:S(2)}) collective-permute-start(bf16[1280,128]{1,0:T(8,128)(2,1)} %constant_dynamic-slice_fusion.1), channel_id=1, source_target_pairs={{0,12},{4,0},{8,4},{12,8},{1,13},{5,1},{9,5},{13,9},{2,14},{6,2},{... | collective-permute-start | bytes 983048 | tf_op jit(solution)/shard_map/ppermute | solution.py:448
  8.1 2.9 %copy-start = (bf16[10,64,5120]{2,1,0:T(8,128)(2,1)S(1)}, bf16[10,64,5120]{2,1,0:T(8,128)(2,1)}, u32[]{:S(2)}) copy-start(bf16[10,64,5120]{2,1,0:T(8,128)(2,1)} %param.7) | copy-start | bytes 19660804
  10.9 1.3 %copy-start.2 = (bf16[10,64,1024]{2,1,0:T(8,128)(2,1)S(1)}, bf16[10,64,1024]{2,1,0:T(8,128)(2,1)}, u32[]{:S(2)}) copy-start(bf16[10,64,1024]{2,1,0:T(8,128)(2,1)} %param.8) | copy-start | bytes 3932164
  12.3 0.9 %copy-start.9 = (bf16[128,1024]{1,0:T(8,128)(2,1)S(1)}, bf16[128,1024]{1,0:T(8,128)(2,1)}, u32[]{:S(2)}) copy-start(bf16[128,1024]{1,0:T(8,128)(2,1)} %up_ref.1) | copy-start | bytes 786436
  13.2 3.3 %copy-start.5 = (bf16[1280,128]{1,0:T(8,128)(2,1)S(1)}, bf16[1280,128]{1,0:T(8,128)(2,1)}, u32[]{:S(2)}) copy-start(bf16[1280,128]{1,0:T(8,128)(2,1)} %own_ref.1) | copy-start | bytes 983044
  13.2 39.1 %slice-start = ((s8[6553600]{0:T(1024)(128)(4,1)}), s8[2359296]{0:T(1024)(128)(4,1)S(1)}, s32[]{:S(2)}) async-start(s8[6553600]{0:T(1024)(128)(4,1)} %bitcast.9), calls=%async_computation | async-start | bytes 4718592
  15.7 0.7 copy-start.6
  16.4 7.2 %copy-start.10 = (bf16[128,640]{1,0:T(8,128)(2,1)}, bf16[128,640]{1,0:T(8,128)(2,1)S(1)}, u32[]{:S(2)}) copy-start(bf16[128,640]{1,0:T(8,128)(2,1)S(1)} %get-tuple-element.78.turned_ref) | copy-start | bytes 491524
  16.5 15.2 %copy-start.8 = (f32[5120]{0:T(1024)S(1)}, f32[5120]{0:T(1024)}, u32[]{:S(2)}) copy-start(f32[5120]{0:T(1024)} %param.12) | copy-start | bytes 61444
  17.2 6.4 %copy-start.12 = (bf16[1280,128]{1,0:T(8,128)(2,1)}, bf16[1280,128]{1,0:T(8,128)(2,1)S(1)}, u32[]{:S(2)}) copy-start(bf16[1280,128]{1,0:T(8,128)(2,1)S(1)} %collective-permute-done.1) | copy-start | bytes 983044
  24.4 17.2 %collective-permute-start.3 = (bf16[2560,128]{1,0:T(8,128)(2,1)}, bf16[2560,128]{1,0:T(8,128)(2,1)S(1)}, u32[]{:S(2)}, u32[]{:S(2)}) collective-permute-start(bf16[2560,128]{1,0:T(8,128)(2,1)} %constant_dynamic-update-slice_fusion.rest_0_), channel_id=1, source_target_pairs={{0,16},{16,0},{1,17},{17,1},{2,18},{18,2},{3,19},{19,3},{4,20},{20... | collective-permute-start | bytes 1966088 | tf_op jit(solution)/shard_map/ppermute | solution.py:449
  25.9 16.1 %collective-permute-start.2 = (bf16[2560,128]{1,0:T(8,128)(2,1)}, bf16[2560,128]{1,0:T(8,128)(2,1)}, u32[]{:S(2)}, u32[]{:S(2)}) collective-permute-start(bf16[2560,128]{1,0:T(8,128)(2,1)} %constant_dynamic-update-slice_fusion.rest_0_), channel_id=1, source_target_pairs={{0,2},{2,0},{1,3},{3,1},{4,6},{6,4},{5,7},{7,5},{8,10},{10,8},{9,1... | collective-permute-start | bytes 1966088 | tf_op jit(solution)/shard_map/ppermute | solution.py:449
  27.4 13.3 %collective-permute-start.6 = (bf16[640,128]{1,0:T(8,128)(2,1)}, bf16[640,128]{1,0:T(8,128)(2,1)}, u32[]{:S(2)}, u32[]{:S(2)}) collective-permute-start(bf16[640,128]{1,0:T(8,128)(2,1)} %constant_dynamic-slice_fusion), channel_id=1, source_target_pairs={{0,4},{4,8},{8,12},{12,0},{1,5},{5,9},{9,13},{13,1},{2,6},{6,10},{... | collective-permute-start | bytes 491528 | tf_op jit(solution)/shard_map/ppermute | solution.py:448
  28.5 13.0 %collective-permute-start.5 = (bf16[640,128]{1,0:T(8,128)(2,1)}, bf16[640,128]{1,0:T(8,128)(2,1)}, u32[]{:S(2)}, u32[]{:S(2)}) collective-permute-start(bf16[640,128]{1,0:T(8,128)(2,1)} %constant_dynamic-slice_fusion), channel_id=1, source_target_pairs={{0,8},{4,12},{8,0},{12,4},{1,9},{5,13},{9,1},{13,5},{2,10},{6,14},... | collective-permute-start | bytes 491528 | tf_op jit(solution)/shard_map/ppermute | solution.py:448
  30.3 11.3 %collective-permute-start.4 = (bf16[640,128]{1,0:T(8,128)(2,1)}, bf16[640,128]{1,0:T(8,128)(2,1)}, u32[]{:S(2)}, u32[]{:S(2)}) collective-permute-start(bf16[640,128]{1,0:T(8,128)(2,1)} %constant_dynamic-slice_fusion), channel_id=1, source_target_pairs={{0,12},{4,0},{8,4},{12,8},{1,13},{5,1},{9,5},{13,9},{2,14},{6,2},{... | collective-permute-start | bytes 491528 | tf_op jit(solution)/shard_map/ppermute | solution.py:448
  31.7 2.9 %copy-start.1 = (bf16[10,64,5120]{2,1,0:T(8,128)(2,1)S(1)}, bf16[10,64,5120]{2,1,0:T(8,128)(2,1)}, u32[]{:S(2)}) copy-start(bf16[10,64,5120]{2,1,0:T(8,128)(2,1)} %param.7) | copy-start | bytes 19660804
  34.6 1.3 %copy-start.3 = (bf16[10,64,1024]{2,1,0:T(8,128)(2,1)S(1)}, bf16[10,64,1024]{2,1,0:T(8,128)(2,1)}, u32[]{:S(2)}) copy-start(bf16[10,64,1024]{2,1,0:T(8,128)(2,1)} %param.8) | copy-start | bytes 3932164
  35.9 1.7 %copy-start.4 = (bf16[1280,1024]{1,0:T(8,128)(2,1)S(1)}, bf16[1280,1024]{1,0:T(8,128)(2,1)}, u32[]{:S(2)}) copy-start(bf16[1280,1024]{1,0:T(8,128)(2,1)} %rest_0_.1) | copy-start | bytes 7864324
  37.6 9.3 %copy-start.13 = (bf16[1280,128]{1,0:T(8,128)(2,1)S(1)}, bf16[1280,128]{1,0:T(8,128)(2,1)}, u32[]{:S(2)}) copy-start(bf16[1280,128]{1,0:T(8,128)(2,1)} %copy-done.12) | copy-start | bytes 983044
  37.6 14.7 %slice-start.1 = ((s8[6553600]{0:T(1024)(128)(4,1)}), s8[4194304]{0:T(1024)(128)(4,1)S(1)}, s32[]{:S(2)}) async-start(s8[6553600]{0:T(1024)(128)(4,1)} %bitcast.9), calls=%async_computation.1 | async-start | bytes 8388608
  37.6 14.7 %copy-start.7 = (f32[640,128]{1,0:T(8,128)S(1)}, f32[640,128]{1,0:T(8,128)}, u32[]{:S(2)}) copy-start(f32[640,128]{1,0:T(8,128)} %copy-done.6) | copy-start | bytes 983044
  37.6 14.7 %copy-start.11 = (bf16[128,640]{1,0:T(8,128)(2,1)S(1)}, bf16[128,640]{1,0:T(8,128)(2,1)}, u32[]{:S(2)}) copy-start(bf16[128,640]{1,0:T(8,128)(2,1)} %copy-done.10) | copy-start | bytes 491524
  42.0 4.9 %collective-permute-start.9 = (bf16[2560,128]{1,0:T(8,128)(2,1)}, bf16[2560,128]{1,0:T(8,128)(2,1)S(1)}, u32[]{:S(2)}, u32[]{:S(2)}) collective-permute-start(bf16[2560,128]{1,0:T(8,128)(2,1)} %constant_dynamic-update-slice_fusion.rest_0_), channel_id=1, source_target_pairs={{0,1},{1,0},{2,3},{3,2},{4,5},{5,4},{6,7},{7,6},{8,9},{9,8},{10,11... | collective-permute-start | bytes 1966088 | tf_op jit(solution)/shard_map/ppermute | solution.py:449
  42.0 8.5 %collective-permute-start.10 = (bf16[2560,128]{1,0:T(8,128)(2,1)}, bf16[2560,128]{1,0:T(8,128)(2,1)S(1)}, u32[]{:S(2)}, u32[]{:S(2)}) collective-permute-start(bf16[2560,128]{1,0:T(8,128)(2,1)} %collective-permute-done.2.rest_1_), channel_id=1, source_target_pairs={{0,1},{1,0},{2,3},{3,2},{4,5},{5,4},{6,7},{7,6},{8,9},{9,8},{10,11... | collective-permute-start | bytes 1966088 | tf_op jit(solution)/shard_map/ppermute | solution.py:449
  42.5 8.0 %collective-permute-start.11 = (bf16[2560,128]{1,0:T(8,128)(2,1)S(1)}, bf16[2560,128]{1,0:T(8,128)(2,1)S(1)}, u32[]{:S(2)}, u32[]{:S(2)}) collective-permute-start(bf16[2560,128]{1,0:T(8,128)(2,1)S(1)} %collective-permute-done.3.rest_2_), channel_id=1, source_target_pairs={{0,1},{1,0},{2,3},{3,2},{4,5},{5,4},{6,7},{7,6},{8,9},{9,8},{10,11... | collective-permute-start | bytes 1966088 | tf_op jit(solution)/shard_map/ppermute | solution.py:449
  42.5 3.9 %collective-permute-start.12 = (bf16[640,128]{1,0:T(8,128)(2,1)}, bf16[640,128]{1,0:T(8,128)(2,1)S(1)}, u32[]{:S(2)}, u32[]{:S(2)}) collective-permute-start(bf16[640,128]{1,0:T(8,128)(2,1)} %collective-permute-done.4.rest_0_.rest_8_), channel_id=1, source_target_pairs={{0,1},{1,0},{2,3},{3,2},{4,5},{5,4},{6,7},{7,6},{8,9},{9,8},{10,11... | collective-permute-start | bytes 491528 | tf_op jit(solution)/shard_map/ppermute | solution.py:449
  44.0 14.8 %collective-permute-start.8 = (bf16[1280,128]{1,0:T(8,128)(2,1)S(1)}, bf16[1280,128]{1,0:T(8,128)(2,1)S(1)}, u32[]{:S(2)}, u32[]{:S(2)}) collective-permute-start(bf16[1280,128]{1,0:T(8,128)(2,1)S(1)} %slice.7), channel_id=1, source_target_pairs={{0,2},{2,0},{1,3},{3,1},{4,6},{6,4},{5,7},{7,5},{8,10},{10,8},{9,1... | collective-permute-start | bytes 983048 | tf_op jit(solution)/shard_map/ppermute | solution.py:449
  46.4 12.4 %collective-permute-start.7 = (bf16[1280,128]{1,0:T(8,128)(2,1)S(1)}, bf16[1280,128]{1,0:T(8,128)(2,1)S(1)}, u32[]{:S(2)}, u32[]{:S(2)}) collective-permute-start(bf16[1280,128]{1,0:T(8,128)(2,1)S(1)} %slice.6), channel_id=1, source_target_pairs={{0,16},{16,0},{1,17},{17,1},{2,18},{18,2},{3,19},{19,3},{4,20},{20... | collective-permute-start | bytes 983048 | tf_op jit(solution)/shard_map/ppermute | solution.py:449
  46.9 11.9 %collective-permute-start.15 = (bf16[1280,128]{1,0:T(8,128)(2,1)S(1)}, bf16[1280,128]{1,0:T(8,128)(2,1)S(1)}, u32[]{:S(2)}, u32[]{:S(2)}) collective-permute-start(bf16[1280,128]{1,0:T(8,128)(2,1)S(1)} %copy-done.13), channel_id=1, source_target_pairs={{0,4},{4,8},{8,12},{12,0},{1,5},{5,9},{9,13},{13,1},{2,6},{6,10},{... | collective-permute-start | bytes 983048 | tf_op jit(solution)/shard_map/ppermute | solution.py:448
  50.5 1.6 %collective-permute-start.13 = (bf16[640,128]{1,0:T(8,128)(2,1)}, bf16[640,128]{1,0:T(8,128)(2,1)S(1)}, u32[]{:S(2)}, u32[]{:S(2)}) collective-permute-start(bf16[640,128]{1,0:T(8,128)(2,1)} %collective-permute-done.5.rest_1_.rest_8_), channel_id=1, source_target_pairs={{0,1},{1,0},{2,3},{3,2},{4,5},{5,4},{6,7},{7,6},{8,9},{9,8},{10,11... | collective-permute-start | bytes 491528 | tf_op jit(solution)/shard_map/ppermute | solution.py:449
  50.5 1.8 %collective-permute-start.14 = (bf16[640,128]{1,0:T(8,128)(2,1)}, bf16[640,128]{1,0:T(8,128)(2,1)S(1)}, u32[]{:S(2)}, u32[]{:S(2)}) collective-permute-start(bf16[640,128]{1,0:T(8,128)(2,1)} %collective-permute-done.6.rest_2_.rest_8_), channel_id=1, source_target_pairs={{0,1},{1,0},{2,3},{3,2},{4,5},{5,4},{6,7},{7,6},{8,9},{9,8},{10,11... | collective-permute-start | bytes 491528 | tf_op jit(solution)/shard_map/ppermute | solution.py:449
  58.8 3.5 %collective-permute-start.19 = (f32[4,128,768]{2,1,0:T(8,128)S(1)}, f32[4,128,768]{2,1,0:T(8,128)S(1)}, u32[]{:S(2)}, u32[]{:S(2)}) collective-permute-start(f32[4,128,768]{2,1,0:T(8,128)S(1)} %get-tuple-element.93), channel_id=1, source_target_pairs={{0,1},{1,0},{2,3},{3,2},{4,5},{5,4},{6,7},{7,6},{8,9},{9,8},{10,11... | collective-permute-start | bytes 4718600 | tf_op jit(solution)/shard_map/ppermute | solution.py:449
  59.2 4.7 %collective-permute-start.16 = (bf16[1280,128]{1,0:T(8,128)(2,1)S(1)}, bf16[1280,128]{1,0:T(8,128)(2,1)S(1)}, u32[]{:S(2)}, u32[]{:S(2)}) collective-permute-start(bf16[1280,128]{1,0:T(8,128)(2,1)S(1)} %collective-permute-done.7.rest_3_), channel_id=1, source_target_pairs={{0,1},{1,0},{2,3},{3,2},{4,5},{5,4},{6,7},{7,6},{8,9},{9,8},{10,11... | collective-permute-start | bytes 983048 | tf_op jit(solution)/shard_map/ppermute | solution.py:449
  59.4 9.9 %collective-permute-start.18 = (bf16[1280,128]{1,0:T(8,128)(2,1)S(1)}, bf16[1280,128]{1,0:T(8,128)(2,1)S(1)}, u32[]{:S(2)}, u32[]{:S(2)}) collective-permute-start(bf16[1280,128]{1,0:T(8,128)(2,1)S(1)} %collective-permute-done.15.rest_0_), channel_id=1, source_target_pairs={{0,16},{16,0},{1,17},{17,1},{2,18},{18,2},{3,19},{19,3},{4,20},{20... | collective-permute-start | bytes 983048 | tf_op jit(solution)/shard_map/ppermute | solution.py:449
  60.9 9.6 %collective-permute-start.17 = (bf16[1280,128]{1,0:T(8,128)(2,1)S(1)}, bf16[1280,128]{1,0:T(8,128)(2,1)S(1)}, u32[]{:S(2)}, u32[]{:S(2)}) collective-permute-start(bf16[1280,128]{1,0:T(8,128)(2,1)S(1)} %collective-permute-done.15.rest_0_), channel_id=1, source_target_pairs={{0,2},{2,0},{1,3},{3,1},{4,6},{6,4},{5,7},{7,5},{8,10},{10,8},{9,1... | collective-permute-start | bytes 983048 | tf_op jit(solution)/shard_map/ppermute | solution.py:449
  62.5 9.1 %collective-permute-start.20 = (bf16[128,768]{1,0:T(8,128)(2,1)S(1)}, bf16[128,768]{1,0:T(8,128)(2,1)S(1)}, u32[]{:S(2)}, u32[]{:S(2)}) collective-permute-start(bf16[128,768]{1,0:T(8,128)(2,1)S(1)} %get-tuple-element.94), channel_id=1, source_target_pairs={{0,4},{4,8},{8,12},{12,0},{1,5},{5,9},{9,13},{13,1},{2,6},{6,10},{... | collective-permute-start | bytes 589832 | tf_op jit(solution)/shard_map/ppermute | solution.py:448
  71.6 2.6 %collective-permute-start.25 = (bf16[1280,128]{1,0:T(8,128)(2,1)S(1)}, bf16[1280,128]{1,0:T(8,128)(2,1)S(1)}, u32[]{:S(2)}, u32[]{:S(2)}) collective-permute-start(bf16[1280,128]{1,0:T(8,128)(2,1)S(1)} %collective-permute-done.8.rest_3_), channel_id=1, source_target_pairs={{0,1},{1,0},{2,3},{3,2},{4,5},{5,4},{6,7},{7,6},{8,9},{9,8},{10,11... | collective-permute-start | bytes 983048 | tf_op jit(solution)/shard_map/ppermute | solution.py:449
  71.6 6.6 %collective-permute-start.22 = (bf16[1280,128]{1,0:T(8,128)(2,1)S(1)}, bf16[1280,128]{1,0:T(8,128)(2,1)S(1)}, u32[]{:S(2)}, u32[]{:S(2)}) collective-permute-start(bf16[1280,128]{1,0:T(8,128)(2,1)S(1)} %collective-permute-done.15.rest_0_), channel_id=1, source_target_pairs={{0,1},{1,0},{2,3},{3,2},{4,5},{5,4},{6,7},{7,6},{8,9},{9,8},{10,11... | collective-permute-start | bytes 983048 | tf_op jit(solution)/shard_map/ppermute | solution.py:449
  72.2 6.2 %collective-permute-start.24 = (bf16[1280,128]{1,0:T(8,128)(2,1)S(1)}, bf16[1280,128]{1,0:T(8,128)(2,1)S(1)}, u32[]{:S(2)}, u32[]{:S(2)}) collective-permute-start(bf16[1280,128]{1,0:T(8,128)(2,1)S(1)} %collective-permute-done.18.rest_2_), channel_id=1, source_target_pairs={{0,1},{1,0},{2,3},{3,2},{4,5},{5,4},{6,7},{7,6},{8,9},{9,8},{10,11... | collective-permute-start | bytes 983048 | tf_op jit(solution)/shard_map/ppermute | solution.py:449
  72.2 6.2 %collective-permute-start.23 = (bf16[1280,128]{1,0:T(8,128)(2,1)S(1)}, bf16[1280,128]{1,0:T(8,128)(2,1)S(1)}, u32[]{:S(2)}, u32[]{:S(2)}) collective-permute-start(bf16[1280,128]{1,0:T(8,128)(2,1)S(1)} %collective-permute-done.17.rest_1_), channel_id=1, source_target_pairs={{0,1},{1,0},{2,3},{3,2},{4,5},{5,4},{6,7},{7,6},{8,9},{9,8},{10,11... | collective-permute-start | bytes 983048 | tf_op jit(solution)/shard_map/ppermute | solution.py:449
  72.7 9.6 %collective-permute-start.21 = (bf16[1280,128]{1,0:T(8,128)(2,1)S(1)}, bf16[1280,128]{1,0:T(8,128)(2,1)S(1)}, u32[]{:S(2)}, u32[]{:S(2)}) collective-permute-start(bf16[1280,128]{1,0:T(8,128)(2,1)S(1)} %collective-permute-done.17.rest_1_), channel_id=1, source_target_pairs={{0,16},{16,0},{1,17},{17,1},{2,18},{18,2},{3,19},{19,3},{4,20},{20... | collective-permute-start | bytes 983048 | tf_op jit(solution)/shard_map/ppermute | solution.py:449
  74.2 8.4 %collective-permute-start.27 = (bf16[128,768]{1,0:T(8,128)(2,1)S(1)}, bf16[128,768]{1,0:T(8,128)(2,1)S(1)}, u32[]{:S(2)}, u32[]{:S(2)}) collective-permute-start(bf16[128,768]{1,0:T(8,128)(2,1)S(1)} %add.24), channel_id=1, source_target_pairs={{0,4},{4,8},{8,12},{12,0},{1,5},{5,9},{9,13},{13,1},{2,6},{6,10},{... | collective-permute-start | bytes 589832 | tf_op jit(solution)/shard_map/ppermute | solution.py:448
  82.3 1.6 %collective-permute-start.26 = (bf16[1280,128]{1,0:T(8,128)(2,1)S(1)}, bf16[1280,128]{1,0:T(8,128)(2,1)S(1)}, u32[]{:S(2)}, u32[]{:S(2)}) collective-permute-start(bf16[1280,128]{1,0:T(8,128)(2,1)S(1)} %collective-permute-done.21.rest_3_), channel_id=1, source_target_pairs={{0,1},{1,0},{2,3},{3,2},{4,5},{5,4},{6,7},{7,6},{8,9},{9,8},{10,11... | collective-permute-start | bytes 983048 | tf_op jit(solution)/shard_map/ppermute | solution.py:449
  82.7 9.6 %collective-permute-start.28 = (bf16[128,768]{1,0:T(8,128)(2,1)S(1)}, bf16[128,768]{1,0:T(8,128)(2,1)S(1)}, u32[]{:S(2)}, u32[]{:S(2)}) collective-permute-start(bf16[128,768]{1,0:T(8,128)(2,1)S(1)} %add.25), channel_id=1, source_target_pairs={{0,4},{4,8},{8,12},{12,0},{1,5},{5,9},{9,13},{13,1},{2,6},{6,10},{... | collective-permute-start | bytes 589832 | tf_op jit(solution)/shard_map/ppermute | solution.py:448
